TPU v7x, 32 devices: a whole 2x2x4 slice. The times are simulated.
32 devices in a mesh: wide: 8 (over z, core), narrow: 4 (over y, x).
Axes of the slice: x: 2, y: 2, z: 4, core: 2. Of those that a mesh axis runs over, the one named last changes fastest.
Arguments:
- tokens: bfloat16 [2, 9216, 512], P(None, ('wide', 'narrow')), may hold values from -6 to 6
- image_lengths: int32 [2, 64], P(None, ('wide', 'narrow')), may hold values from 49 to 144, as said below
- expert_index: int32 [2, 9216, 2], P(None, ('wide', 'narrow')), may hold values from 0 to 15, all different within a row; in each aligned block of 288 rows (0 to 287, 288 to 575, ..., all dimensions but the last counted through in order) at most 38 rows name the same one
- grad_out: bfloat16 [2, 9216, 512], P(None, ('wide', 'narrow')), may hold values from -6 to 6
- ln1_gain: bfloat16 [512], replicated, may hold values from 0.5 to 1.5
- ln1_bias: bfloat16 [512], replicated, may hold values from -3 to 3
- w_qkv: bfloat16 [512, 1536], replicated, may hold values from -0.25 to 0.25
- bias_query: bfloat16 [512], replicated, may hold values from -3 to 3
- bias_value: bfloat16 [512], replicated, may hold values from -3 to 3
- w_out: bfloat16 [512, 512], replicated, may hold values from -0.75 to 0.75
- bias_out: bfloat16 [512], replicated, may hold values from -3 to 3
- ln2_gain: bfloat16 [512], replicated, may hold values from 0.5 to 1.5
- ln2_bias: bfloat16 [512], replicated, may hold values from -3 to 3
- w_router: bfloat16 [512, 16], replicated, may hold values from -0.1875 to 0.1875
- experts_in: bfloat16 [16, 512, 2048], P('wide', None, 'narrow'), may hold values from -0.25 to 0.25
- experts_in_bias: bfloat16 [16, 2048], P('wide', 'narrow'), may hold values from -3 to 3
- experts_out: bfloat16 [16, 2048, 512], P('wide', 'narrow'), may hold values from -4 to 4
- experts_out_bias: bfloat16 [16, 512], P('wide'), may hold values from -12 to 12
Outputs:
- mixed: bfloat16 [2, 9216, 512], P(None, ('wide', 'narrow'))
- grad_tokens: float32 [2, 9216, 512], P(None, ('wide', 'narrow'))
- grad_ln1_gain: float32 [512], replicated
- grad_ln1_bias: float32 [512], replicated
- grad_w_qkv: float32 [512, 1536], replicated
- grad_bias_query: float32 [512], replicated
- grad_bias_value: float32 [512], replicated
- grad_w_out: float32 [512, 512], replicated
- grad_bias_out: float32 [512], replicated
- grad_ln2_gain: float32 [512], replicated
- grad_ln2_bias: float32 [512], replicated
- grad_w_router: float32 [512, 16], replicated
- grad_experts_in: float32 [16, 512, 2048], P('wide', None, 'narrow')
- grad_experts_in_bias: float32 [16, 2048], P('wide', 'narrow')
- grad_experts_out: float32 [16, 2048, 512], P('wide', 'narrow')
- grad_experts_out_bias: float32 [16, 512], P('wide')
Inputs may be any that keep to these rules, and one draw needn't show every extreme that they name: Image i of micro-batch m has its first image_lengths[m, i] patch slots filled; every value is 49 or 144, and both occur. `expert_index`: each patch names two different experts. Among the 288 patches of one device in a micro-batch (aligned blocks of rows), no expert is named more than 38 times, a bound that some block reaches.
All inputs are finite; a program needn't handle non-finite values.
Results may differ from a plain program's by a relative error of at most 0.015.
Values may be sent and summed in bfloat16 or wider, within the bound.
A program may use at most 320 MiB of HBM per device.

v0:
```python
import jax
import jax.numpy as jnp
from jax import lax
from jax.sharding import PartitionSpec as P

HEADS = 8
HEAD_DIM = 64


def layer_norm(values, norm_gain, norm_shift):
    row_mean = jnp.mean(values, axis=-1, keepdims=True)
    centred = values - row_mean
    spread = jnp.mean(centred * centred, axis=-1, keepdims=True)
    return centred * lax.rsqrt(spread + 1e-06) * norm_gain + norm_shift


def contract_rows(left, right):
    return lax.dot_general(
        left, right, (((0,), (0,)), ((), ())), preferred_element_type=jnp.float32
    )


def times_transposed(left, right):
    return lax.dot_general(
        left, right, (((1,), (1,)), ((), ())), preferred_element_type=jnp.float32
    )


def slot_rows(route_ids, expert_count, capacity):
    paired = route_ids.reshape(-1)
    one_hot = (paired[:, None] == jnp.arange(expert_count, dtype=jnp.int32)[None, :]).astype(
        jnp.int32
    )
    before = jnp.cumsum(one_hot, axis=0) - one_hot
    slot = jnp.sum(before * one_hot, axis=1)
    return paired * capacity + slot


def masked_scores(queries, key_rows, lengths):
    images, seq_len = (queries.shape[0], queries.shape[1])
    head_shape = (images, seq_len, HEADS, HEAD_DIM)
    scores = jnp.einsum(
        "gqhd,gkhd->ghqk",
        queries.reshape(head_shape),
        key_rows.reshape(head_shape),
        preferred_element_type=jnp.float32,
    ) * HEAD_DIM ** (-0.5)
    visible = (
        jnp.arange(seq_len, dtype=jnp.int32)[None, None, None, :] < lengths[:, None, None, None]
    )
    return jnp.where(visible, scores, -1e30)


def attend_forward(queries, key_rows, value_rows, lengths):
    images, seq_len = (queries.shape[0], queries.shape[1])
    head_shape = (images, seq_len, HEADS, HEAD_DIM)
    scores = masked_scores(queries, key_rows, lengths)
    top_score = jnp.max(scores, axis=-1, keepdims=True)
    raised = jnp.exp(scores - top_score)
    row_total = jnp.sum(raised, axis=-1, keepdims=True)
    weights = (raised / row_total).astype(jnp.bfloat16)
    attended = jnp.einsum(
        "ghqk,gkhd->gqhd",
        weights,
        value_rows.reshape(head_shape),
        preferred_element_type=jnp.float32,
    )
    return (
        attended.reshape(images * seq_len, HEADS * HEAD_DIM).astype(jnp.bfloat16),
        top_score + jnp.log(row_total),
    )


def attend_backward(queries, key_rows, value_rows, lengths, log_total, grad_attended):
    images, seq_len = (queries.shape[0], queries.shape[1])
    head_shape = (images, seq_len, HEADS, HEAD_DIM)
    scale = HEAD_DIM ** (-0.5)
    probs = jnp.exp(masked_scores(queries, key_rows, lengths) - log_total)
    grad_heads = grad_attended.reshape(head_shape)
    grad_probs = jnp.einsum(
        "gqhd,gkhd->ghqk",
        grad_heads,
        value_rows.reshape(head_shape),
        preferred_element_type=jnp.float32,
    )
    grad_values = jnp.einsum(
        "ghqk,gqhd->gkhd",
        probs.astype(jnp.bfloat16),
        grad_heads,
        preferred_element_type=jnp.float32,
    )
    centre = jnp.sum(probs * grad_probs, axis=-1, keepdims=True)
    grad_scores = (probs * (grad_probs - centre)).astype(jnp.bfloat16)
    grad_queries = (
        jnp.einsum(
            "ghqk,gkhd->gqhd",
            grad_scores,
            key_rows.reshape(head_shape),
            preferred_element_type=jnp.float32,
        )
        * scale
    )
    grad_keys = (
        jnp.einsum(
            "ghqk,gqhd->gkhd",
            grad_scores,
            queries.reshape(head_shape),
            preferred_element_type=jnp.float32,
        )
        * scale
    )
    row_shape = (images * seq_len, HEADS * HEAD_DIM)
    return (
        grad_queries.reshape(row_shape).astype(jnp.bfloat16),
        grad_keys.reshape(row_shape).astype(jnp.bfloat16),
        grad_values.reshape(row_shape).astype(jnp.bfloat16),
    )


def on_device(
    tokens,
    image_lengths,
    expert_index,
    grad_out,
    ln1_gain,
    ln1_bias,
    w_qkv,
    bias_query,
    bias_value,
    w_out,
    bias_out,
    ln2_gain,
    ln2_bias,
    w_router,
    experts_in,
    experts_in_bias,
    experts_out,
    experts_out_bias,
):
    model_width = tokens.shape[2]
    tok_rows = tokens.shape[1]
    image_count = image_lengths.shape[1]
    seq_len = tok_rows // image_count
    local_experts = experts_in.shape[0]
    expert_count = local_experts * lax.axis_size("wide")
    capacity = (tok_rows * 42 + 20 * expert_count - 1) // (20 * expert_count)
    norm1_gain = ln1_gain.astype(jnp.float32)
    norm1_shift = ln1_bias.astype(jnp.float32)
    norm2_gain = ln2_gain.astype(jnp.float32)
    norm2_shift = ln2_bias.astype(jnp.float32)
    query_bias = bias_query.astype(jnp.float32)
    value_bias = bias_value.astype(jnp.float32)
    branch_bias = bias_out.astype(jnp.float32)
    router_wide = w_router.astype(jnp.float32)
    back_bias = experts_out_bias.astype(jnp.float32)
    expert_ids = jnp.arange(expert_count, dtype=jnp.int32)
    layer_in, layer_in_bias, layer_out = (experts_in, experts_in_bias, experts_out)
    layer_bias = layer_in_bias.astype(jnp.float32)
    acc_gain1 = jnp.zeros_like(norm1_gain)
    acc_shift1 = jnp.zeros_like(norm1_shift)
    acc_qkv = jnp.zeros(w_qkv.shape, jnp.float32)
    acc_query_bias = jnp.zeros_like(query_bias)
    acc_value_bias = jnp.zeros_like(value_bias)
    acc_branch = jnp.zeros(w_out.shape, jnp.float32)
    acc_branch_bias = jnp.zeros_like(branch_bias)
    acc_gain2 = jnp.zeros_like(norm2_gain)
    acc_shift2 = jnp.zeros_like(norm2_shift)
    acc_router = jnp.zeros(w_router.shape, jnp.float32)
    acc_in = jnp.zeros(layer_in.shape, jnp.float32)
    acc_in_bias = jnp.zeros(layer_bias.shape, jnp.float32)
    acc_out = jnp.zeros(layer_out.shape, jnp.float32)
    acc_out_bias = jnp.zeros(back_bias.shape, jnp.float32)
    mixed_parts = []
    grad_parts = []
    for micro_step in range(tokens.shape[0]):
        inputs = tokens[micro_step].astype(jnp.float32)
        lengths = image_lengths[micro_step]
        route_ids = expert_index[micro_step]
        cotangent = grad_out[micro_step].astype(jnp.float32)
        image_shape = (image_count, seq_len, model_width)
        normed_f, ln1_pull = jax.vjp(layer_norm, inputs, norm1_gain, norm1_shift)
        normed = normed_f.astype(jnp.bfloat16)
        projected = jnp.dot(normed, w_qkv, preferred_element_type=jnp.float32)
        queries = (projected[:, :model_width] + query_bias).astype(jnp.bfloat16)
        key_rows = projected[:, model_width : 2 * model_width].astype(jnp.bfloat16)
        value_rows = (projected[:, 2 * model_width :] + value_bias).astype(jnp.bfloat16)
        attended, log_total = attend_forward(
            queries.reshape(image_shape),
            key_rows.reshape(image_shape),
            value_rows.reshape(image_shape),
            lengths,
        )
        residual = (
            inputs + jnp.dot(attended, w_out, preferred_element_type=jnp.float32) + branch_bias
        )
        normed_two, ln2_pull = jax.vjp(layer_norm, residual, norm2_gain, norm2_shift)
        expert_input = normed_two.astype(jnp.bfloat16)
        router_logits = jnp.dot(expert_input, w_router, preferred_element_type=jnp.float32)
        expert_probs = jax.nn.softmax(router_logits, axis=-1)
        chosen = route_ids[:, :, None] == expert_ids[None, None, :]
        gates = jnp.sum(jnp.where(chosen, expert_probs[:, None, :], 0.0), axis=-1)
        flat = slot_rows(route_ids, expert_count, capacity)
        pair_rows = jnp.repeat(expert_input, 2, axis=0)
        send_rows = (
            jnp.zeros((expert_count * capacity, model_width), jnp.bfloat16).at[flat].set(pair_rows)
        )
        send_rows = send_rows.reshape(expert_count, capacity, model_width)
        arrived = lax.all_to_all(send_rows, "wide", split_axis=0, concat_axis=1, tiled=True)
        expert_rows = lax.all_gather(arrived, "narrow", axis=1, tiled=True)
        pre_act = (
            jnp.einsum("erd,edf->erf", expert_rows, layer_in, preferred_element_type=jnp.float32)
            + layer_bias[:, None, :]
        )
        hidden_f, gelu_pull = jax.vjp(jax.nn.gelu, pre_act)
        hidden = hidden_f.astype(jnp.bfloat16)
        partial_out = jnp.einsum(
            "erf,efd->erd", hidden, layer_out, preferred_element_type=jnp.float32
        )
        summed = lax.psum_scatter(partial_out, "narrow", scatter_dimension=1, tiled=True)
        result_rows = (summed + back_bias[:, None, :]).astype(jnp.bfloat16)
        returned = lax.all_to_all(result_rows, "wide", split_axis=1, concat_axis=0, tiled=True)
        picked = returned.reshape(expert_count * capacity, model_width)[flat].astype(jnp.float32)
        picked = picked.reshape(tok_rows, 2, model_width)
        mixed_parts.append(
            (residual + jnp.sum(gates[:, :, None] * picked, axis=1)).astype(jnp.bfloat16)
        )
        grad_gates = jnp.sum(cotangent[:, None, :] * picked, axis=-1)
        grad_picked = (
            (gates[:, :, None] * cotangent[:, None, :])
            .astype(jnp.bfloat16)
            .reshape(-1, model_width)
        )
        grad_send = (
            jnp.zeros((expert_count * capacity, model_width), jnp.bfloat16)
            .at[flat]
            .set(grad_picked)
        )
        grad_send = grad_send.reshape(expert_count, capacity, model_width)
        grad_arrived = lax.all_to_all(grad_send, "wide", split_axis=0, concat_axis=1, tiled=True)
        grad_rows = lax.all_gather(grad_arrived, "narrow", axis=1, tiled=True)
        acc_out_bias = acc_out_bias + jnp.sum(grad_rows, axis=1, dtype=jnp.float32)
        acc_out = acc_out + jnp.einsum(
            "erf,erd->efd", hidden, grad_rows, preferred_element_type=jnp.float32
        )
        grad_hidden = jnp.einsum(
            "erd,efd->erf", grad_rows, layer_out, preferred_element_type=jnp.float32
        )
        grad_pre = gelu_pull(grad_hidden)[0].astype(jnp.bfloat16)
        acc_in_bias = acc_in_bias + jnp.sum(grad_pre, axis=1, dtype=jnp.float32)
        acc_in = acc_in + jnp.einsum(
            "erd,erf->edf", expert_rows, grad_pre, preferred_element_type=jnp.float32
        )
        grad_partial = jnp.einsum(
            "erf,edf->erd", grad_pre, layer_in, preferred_element_type=jnp.float32
        )
        grad_summed = lax.psum_scatter(grad_partial, "narrow", scatter_dimension=1, tiled=True)
        grad_back = lax.all_to_all(
            grad_summed.astype(jnp.bfloat16), "wide", split_axis=1, concat_axis=0, tiled=True
        )
        grad_pairs = grad_back.reshape(expert_count * capacity, model_width)[flat].astype(
            jnp.float32
        )
        grad_pairs = jnp.sum(grad_pairs.reshape(tok_rows, 2, model_width), axis=1)
        grad_choice = jnp.sum(jnp.where(chosen, grad_gates[:, :, None], 0.0), axis=1)
        grad_logits = expert_probs * (
            grad_choice - jnp.sum(expert_probs * grad_choice, axis=-1, keepdims=True)
        )
        acc_router = acc_router + lax.dot_general(
            expert_input.astype(jnp.float32),
            grad_logits,
            (((0,), (0,)), ((), ())),
            precision=lax.Precision.HIGHEST,
            preferred_element_type=jnp.float32,
        )
        grad_normed_two = lax.dot_general(
            grad_logits,
            router_wide,
            (((1,), (1,)), ((), ())),
            precision=lax.Precision.HIGHEST,
            preferred_element_type=jnp.float32,
        )
        grad_residual, grad_gain2, grad_shift2 = ln2_pull(grad_normed_two + grad_pairs)
        acc_gain2 = acc_gain2 + grad_gain2
        acc_shift2 = acc_shift2 + grad_shift2
        grad_residual = grad_residual + cotangent
        grad_branch = grad_residual.astype(jnp.bfloat16)
        acc_branch_bias = acc_branch_bias + jnp.sum(grad_branch, axis=0, dtype=jnp.float32)
        acc_branch = acc_branch + contract_rows(attended, grad_branch)
        grad_attended = times_transposed(grad_branch, w_out).astype(jnp.bfloat16)
        grad_queries, grad_keys, grad_values = attend_backward(
            queries.reshape(image_shape),
            key_rows.reshape(image_shape),
            value_rows.reshape(image_shape),
            lengths,
            log_total,
            grad_attended.reshape(image_shape),
        )
        acc_query_bias = acc_query_bias + jnp.sum(grad_queries, axis=0, dtype=jnp.float32)
        acc_value_bias = acc_value_bias + jnp.sum(grad_values, axis=0, dtype=jnp.float32)
        grad_projected = jnp.concatenate([grad_queries, grad_keys, grad_values], axis=1)
        acc_qkv = acc_qkv + contract_rows(normed, grad_projected)
        grad_normed = times_transposed(grad_projected, w_qkv)
        grad_inputs, grad_gain1, grad_shift1 = ln1_pull(grad_normed)
        acc_gain1 = acc_gain1 + grad_gain1
        acc_shift1 = acc_shift1 + grad_shift1
        grad_parts.append(grad_residual + grad_inputs)
    dense_sums = lax.psum(
        (
            acc_gain1,
            acc_shift1,
            acc_qkv,
            acc_query_bias,
            acc_value_bias,
            acc_branch,
            acc_branch_bias,
            acc_gain2,
            acc_shift2,
            acc_router,
        ),
        ("wide", "narrow"),
    )
    final_in, final_in_bias, final_out, final_out_bias = (
        acc_in,
        acc_in_bias,
        acc_out,
        acc_out_bias,
    )
    return (
        jnp.stack(mixed_parts, axis=0),
        jnp.stack(grad_parts, axis=0),
        dense_sums[0],
        dense_sums[1],
        dense_sums[2],
        dense_sums[3],
        dense_sums[4],
        dense_sums[5],
        dense_sums[6],
        dense_sums[7],
        dense_sums[8],
        dense_sums[9],
        final_in,
        final_in_bias,
        final_out,
        final_out_bias,
    )


def solution(mesh):
    in_specs = (
        P(None, ("wide", "narrow"), None),
        P(None, ("wide", "narrow")),
        P(None, ("wide", "narrow"), None),
        P(None, ("wide", "narrow"), None),
        P(),
        P(),
        P(),
        P(),
        P(),
        P(),
        P(),
        P(),
        P(),
        P(),
        P("wide", None, "narrow"),
        P("wide", "narrow"),
        P("wide", "narrow", None),
        P("wide", None),
    )
    out_specs = (
        P(None, ("wide", "narrow"), None),
        P(None, ("wide", "narrow"), None),
        P(),
        P(),
        P(),
        P(),
        P(),
        P(),
        P(),
        P(),
        P(),
        P(),
        P("wide", None, "narrow"),
        P("wide", "narrow"),
        P("wide", "narrow", None),
        P("wide", None),
    )
    return jax.shard_map(
        on_device, mesh=mesh, in_specs=in_specs, out_specs=out_specs, check_vma=False
    )
```

profile of v0, /device:TPU:0, one launch (start us, length us, event | category | flops | bytes accessed | tf_op | source)
XLA Modules:
  0.0 828.7 jit_solution(2633847154594045253)
XLA Ops:
  22.3 3.1 mul.484
  66.1 9.7 %scatter_custom_fusion.2 = bf16[608,512]{1,0:T(8,128)(2,1)} fusion(s32[576]{0:T(1024)S(1)} %fusion.83, f32[576,512]{1,0:T(8,128)} %mul.484, f32[576]{0:T(1024)S(1)} %mul.482, bf16[]{:T(256)} %constant.50.clone.1), kind=kCustom, calls=%fused_computation.130 | custom fusion | flops 589824 | bytes 1806338 | tf_op jit(solution)/shard_map/scatter | solution.py:236
  77.9 24.5 %all_to_all.132 = bf16[16,38,512]{2,1,0:T(8,128)(2,1)S(1)} all-to-all(bf16[16,38,512]{2,1,0:T(8,128)(2,1)} %reshape.451), channel_id=1, replica_groups=mesh['wide'=8,'narrow'=4] {'wide'}, dimensions={0} | all-to-all | bytes 1245184 | tf_op jit(solution)/shard_map/all_to_all | solution.py:239
  109.2 6.4 scatter_custom_fusion
  116.6 21.7 %all_to_all.133 = bf16[16,38,512]{2,1,0:T(8,128)(2,1)S(1)} all-to-all(bf16[16,38,512]{2,1,0:T(8,128)(2,1)} %reshape.444), channel_id=1, replica_groups=mesh['wide'=8,'narrow'=4] {'wide'}, dimensions={0} | all-to-all | bytes 1245184 | tf_op jit(solution)/shard_map/all_to_all | solution.py:208
  146.3 3.3 reduce-window.16
  151.9 3.1 mul.518
  158.4 8.8 %scatter_custom_fusion.3 = bf16[608,512]{1,0:T(8,128)(2,1)S(1)} fusion(s32[576]{0:T(1024)S(1)} %fusion.84, f32[576,512]{1,0:T(8,128)} %mul.518, f32[576]{0:T(1024)S(1)} %mul.516, bf16[]{:T(256)} %constant.50.clone.1), kind=kCustom, calls=%fused_computation.131 | custom fusion | flops 589824 | bytes 1806338 | tf_op jit(solution)/shard_map/scatter | solution.py:236
  168.2 21.7 %all_to_all.134 = bf16[16,38,512]{2,1,0:T(8,128)(2,1)S(1)} all-to-all(bf16[16,38,512]{2,1,0:T(8,128)(2,1)} %reshape.453), channel_id=1, replica_groups=mesh['wide'=8,'narrow'=4] {'wide'}, dimensions={0} | all-to-all | bytes 1245184 | tf_op jit(solution)/shard_map/all_to_all | solution.py:239
  196.1 6.6 scatter_custom_fusion.1
  204.0 20.6 %all_to_all.135 = bf16[16,38,512]{2,1,0:T(8,128)(2,1)S(1)} all-to-all(bf16[16,38,512]{2,1,0:T(8,128)(2,1)S(1)} %reshape.449), channel_id=1, replica_groups=mesh['wide'=8,'narrow'=4] {'wide'}, dimensions={0} | all-to-all | bytes 1245184 | tf_op jit(solution)/shard_map/all_to_all | solution.py:208
  226.5 5.6 fusion.113
  232.1 9.1 %convert_reduce_fusion.3 = (f32[2,512]{1,0:T(2,128)}, bf16[2,1216,512]{2,1,0:T(8,128)(2,1)S(1)}, f32[2,1216,512]{2,1,0:T(8,128)}) fusion(f32[2,1216,512]{2,1,0:T(8,128)} %fusion.113, f32[2,512]{1,0:T(2,128)S(1)} %convert_element_type.336, bf16[2,1216,512]{2,1,0:T(8,128)(2,1)} %all-gather.5.cloned.1.call-done, bf16[2,512,512]{2,1,0:T(8,128)(2,1)} %param.32), kind=kOutput, calls=%fused_computation.29 | convolution fusion | flops 1303706624 | bytes 15998976 | tf_op jit(solution)/shard_map/erd,edf->erf/dot_general | solution.py:211
  242.7 3.7 fusion.114
  246.5 5.7 fusion.115
  252.2 19.2 %all-gather.7.cloned.1.call-done = bf16[2,1216,512]{2,1,0:T(8,128)(2,1)} async-done(((bf16[2,304,512]{2,1,0:T(8,128)(2,1)}), bf16[2,1216,512]{2,1,0:T(8,128)(2,1)}) %all-gather.7.cloned.1.call-update) | async-done | bytes 2490384 | tf_op jit(solution)/shard_map/all_gather | solution.py:209
  271.4 9.2 %convert_reduce_fusion.2 = (f32[2,512]{1,0:T(2,128)}, bf16[2,1216,512]{2,1,0:T(8,128)(2,1)S(1)}, f32[2,1216,512]{2,1,0:T(8,128)}) fusion(f32[2,1216,512]{2,1,0:T(8,128)} %fusion.115, f32[2,512]{1,0:T(2,128)S(1)} %convert_element_type.336, bf16[2,1216,512]{2,1,0:T(8,128)(2,1)} %all-gather.7.cloned.1.call-done, bf16[2,512,512]{2,1,0:T(8,128)(2,1)} %param.32), kind=kOutput, calls=%fused_computation.28 | convolution fusion | flops 1303706624 | bytes 15998976 | tf_op jit(solution)/shard_map/erd,edf->erf/dot_general | solution.py:211
  282.1 3.8 fusion.116
  286.0 7.0 fusion.100
  293.4 7.0 fusion.98
  300.5 33.1 %reduce-scatter.9.cloned.1.call-done = f32[2,304,512]{2,1,0:T(8,128)} async-done(((f32[2,1216,512]{2,1,0:T(8,128)}), f32[2,304,512]{2,1,0:T(8,128)}) %reduce-scatter.9.cloned.1.call-update) | async-done | bytes 1245200 | tf_op jit(solution)/shard_map/reduce_scatter | solution.py:256
  336.5 4.6 all-to-all-start.5
  345.1 50.7 %reduce-scatter.11.cloned.1.call-done = f32[2,304,512]{2,1,0:T(8,128)} async-done(((f32[2,1216,512]{2,1,0:T(8,128)}), f32[2,304,512]{2,1,0:T(8,128)}) %reduce-scatter.11.cloned.1.call-update) | async-done | bytes 1245200 | tf_op jit(solution)/shard_map/reduce_scatter | solution.py:256
  398.6 4.6 all-to-all-start.7
  403.3 7.3 fusion.99
  410.6 47.6 %reduce-scatter.5.cloned.1.call-done = f32[2,304,512]{2,1,0:T(8,128)} async-done(((f32[2,1216,512]{2,1,0:T(8,128)}), f32[2,304,512]{2,1,0:T(8,128)}) %reduce-scatter.5.cloned.1.call-update) | async-done | bytes 1245200 | tf_op jit(solution)/shard_map/reduce_scatter | solution.py:219
  458.1 62.3 %reduce-scatter.7.cloned.1.call-done = f32[2,304,512]{2,1,0:T(8,128)} async-done(((f32[2,1216,512]{2,1,0:T(8,128)}), f32[2,304,512]{2,1,0:T(8,128)}) %reduce-scatter.7.cloned.1.call-update) | async-done | bytes 1245200 | tf_op jit(solution)/shard_map/reduce_scatter | solution.py:219
  520.5 2.8 add_convert_fusion.1
  524.7 4.6 all-to-all-start.1
  529.4 5.5 fusion.119
  536.4 5.8 convolution_add_fusion.3
  543.7 3.2 all-to-all-done.1
  546.9 4.2 all-to-all-start.3
  554.6 5.2 convolution_add_fusion.4
  562.1 3.4 gather_fusion.2
  571.5 3.3 gather_fusion.3
  577.5 3.5 reduce_sum.577
  581.0 3.5 reduce_sum.586
  587.8 3.3 gather_fusion
  593.8 4.4 multiply_reduce_fusion.3
  602.8 3.3 gather_fusion.1
  608.9 4.7 multiply_reduce_fusion.2
  629.1 3.1 convert_reduce_fusion.4
  639.0 3.2 convert_reduce_fusion.5
  670.9 2.9 convolution_add_fusion.2
  679.4 41.3 %all-reduce.2 = (f32[512]{0:T(512)}, f32[512]{0:T(512)}, f32[512]{0:T(512)}, f32[512]{0:T(512)}, f32[512]{0:T(512)}, /*index=5*/f32[512]{0:T(512)}, f32[512]{0:T(512)}, f32[512,16]{0,1:T(8,128)}) all-reduce(f32[512]{0:T(512)S(1)} %add.365, f32[512]{0:T(512)S(1)} %add.366, ...), channel_id=1, replica_groups=mesh['wide'=8,'narrow'=4] {'wide','narrow'}, use_global_device_ids=true, to_apply=%region_54.55 | all-reduce | flops 11776 | bytes 94208 | tf_op jit(solution)/shard_map/psum | solution.py:307
  727.0 90.1 %all-reduce.6.cloned.1.call-done = (f32[512,1536]{1,0:T(8,128)}, f32[512,512]{1,0:T(8,128)}) async-done(((f32[512,1536]{1,0:T(8,128)}, f32[512,512]{1,0:T(8,128)}), (f32[512,1536]{1,0:T(8,128)}, f32[512,512]{1,0:T(8,128)})) %all-reduce.6.cloned.1.call-update) | async-done | bytes 4194320 | tf_op jit(solution)/shard_map/psum | solution.py:307
  817.1 3.8 copy.338
  (466 shorter events, 197.9 us)
Async XLA Ops:
  7.2 18.2 %copy-start = (bf16[512,1536]{1,0:T(8,128)(2,1)S(1)}, bf16[512,1536]{1,0:T(8,128)(2,1)}, u32[]{:S(2)}) copy-start(bf16[512,1536]{1,0:T(8,128)(2,1)} %param.24) | copy-start | bytes 4718596
  7.2 12.7 %copy-start.15 = (bf16[2,288,512]{2,1,0:T(8,128)(2,1)S(1)}, bf16[2,288,512]{2,1,0:T(8,128)(2,1)}, u32[]{:S(2)}) copy-start(bf16[2,288,512]{2,1,0:T(8,128)(2,1)} %param.21) | copy-start | bytes 1769476
  7.2 219.3 %all-gather.9.cloned.1.call-start = ((), (), s32[]{:S(2)}) async-start(), calls=%async_computation.16 | async-start | bytes 3112960 | tf_op jit(solution)/shard_map/all_gather | solution.py:240
  8.8 20.1 %copy-start.73 = (f32[512]{0:T(512)}, f32[512]{0:T(512)S(1)}, u32[]{:S(2)}) copy-start(f32[512]{0:T(512)S(1)} %convert_element_type.320) | copy-start | bytes 6148
  9.5 19.4 %copy-start.97 = (f32[512]{0:T(512)}, f32[512]{0:T(512)S(1)}, u32[]{:S(2)}) copy-start(f32[512]{0:T(512)S(1)} %convert_element_type.321) | copy-start | bytes 6148
  10.2 53.2 %copy-start.81 = (f32[512]{0:T(512)}, f32[512]{0:T(512)S(1)}, u32[]{:S(2)}) copy-start(f32[512]{0:T(512)S(1)} %convert_element_type.332) | copy-start | bytes 6148
  14.1 11.2 %copy-start.75 = (f32[288]{0:T(512)}, f32[288]{0:T(512)S(1)}, u32[]{:S(2)}) copy-start(f32[288]{0:T(512)S(1)} %get-tuple-element.122) | copy-start | bytes 3460
  14.1 14.8 %copy-start.77 = (f32[288]{0:T(512)}, f32[288]{0:T(512)S(1)}, u32[]{:S(2)}) copy-start(f32[288]{0:T(512)S(1)} %get-tuple-element.123) | copy-start | bytes 3460
  15.5 9.9 %copy-start.99 = (f32[288]{0:T(512)}, f32[288]{0:T(512)S(1)}, u32[]{:S(2)}) copy-start(f32[288]{0:T(512)S(1)} %get-tuple-element.37) | copy-start | bytes 3460
  16.1 12.8 %copy-start.87 = (f32[288]{0:T(512)}, f32[288]{0:T(512)S(1)}, u32[]{:S(2)}) copy-start(f32[288]{0:T(512)S(1)} %fusion.85) | copy-start | bytes 3460
  16.1 9.3 %copy-start.89 = (f32[288]{0:T(512)}, f32[288]{0:T(512)S(1)}, u32[]{:S(2)}) copy-start(f32[288]{0:T(512)S(1)} %fusion.87) | copy-start | bytes 3460
  17.4 47.7 %copy-start.94 = (s32[288,2]{0,1:T(2,128)}, s32[288,2]{0,1:T(2,128)S(1)}, u32[]{:S(2)}) copy-start(s32[288,2]{0,1:T(2,128)S(1)} %get-tuple-element.74) | copy-start | bytes 6916
  51.6 11.7 %copy-start.69 = (f32[288]{0:T(512)}, f32[288]{0:T(512)S(1)}, u32[]{:S(2)}) copy-start(f32[288]{0:T(512)S(1)} %broadcast_multiply_fusion.4) | copy-start | bytes 3460
  51.9 11.5 %copy-start.83 = (f32[288]{0:T(512)}, f32[288]{0:T(512)S(1)}, u32[]{:S(2)}) copy-start(f32[288]{0:T(512)S(1)} %fusion.86) | copy-start | bytes 3460
  63.1 14.8 %copy-start.71 = (f32[288]{0:T(512)}, f32[288]{0:T(512)S(1)}, u32[]{:S(2)}) copy-start(f32[288]{0:T(512)S(1)} %broadcast_multiply_fusion.2) | copy-start | bytes 3460
  63.9 14.0 %copy-start.85 = (f32[288]{0:T(512)}, f32[288]{0:T(512)S(1)}, u32[]{:S(2)}) copy-start(f32[288]{0:T(512)S(1)} %fusion.88) | copy-start | bytes 3460
  64.8 40.6 %copy-start.26 = (bf16[288,512]{1,0:T(8,128)(2,1)}, bf16[288,512]{1,0:T(8,128)(2,1)S(1)}, u32[]{:S(2)}) copy-start(bf16[288,512]{1,0:T(8,128)(2,1)S(1)} %get-tuple-element.84) | copy-start | bytes 884740
  65.0 38.2 %copy-start.91 = (f32[288]{0:T(512)}, f32[288]{0:T(512)S(1)}, u32[]{:S(2)}) copy-start(f32[288]{0:T(512)S(1)} %get-tuple-element.105) | copy-start | bytes 3460
  65.1 38.2 %copy-start.107 = (f32[288]{0:T(512)}, f32[288]{0:T(512)S(1)}, u32[]{:S(2)}) copy-start(f32[288]{0:T(512)S(1)} %fusion.79) | copy-start | bytes 3460
  66.0 43.1 %copy-start.110 = (s32[576]{0:T(1024)}, s32[576]{0:T(1024)S(1)}, u32[]{:S(2)}) copy-start(s32[576]{0:T(1024)S(1)} %fusion.83) | copy-start | bytes 6916
  105.4 126.8 %all-gather.5.cloned.1.call-start = ((), (), s32[]{:S(2)}) async-start(), calls=%async_computation.12 | async-start | bytes 3112960 | tf_op jit(solution)/shard_map/all_gather | solution.py:209
  116.6 33.9 %copy-start.17 = (f32[288,512]{1,0:T(8,128)S(1)}, f32[288,512]{1,0:T(8,128)}, u32[]{:S(2)}) copy-start(f32[288,512]{1,0:T(8,128)} %get-tuple-element.73) | copy-start | bytes 1769476
  141.3 105.2 %all-gather.11.cloned.1.call-start = ((), (), s32[]{:S(2)}) async-start(), calls=%async_computation.18 | async-start | bytes 3112960 | tf_op jit(solution)/shard_map/all_gather | solution.py:240
  156.1 34.7 %copy-start.93 = (f32[288]{0:T(512)}, f32[288]{0:T(512)S(1)}, u32[]{:S(2)}) copy-start(f32[288]{0:T(512)S(1)} %get-tuple-element.102) | copy-start | bytes 3460
  156.2 34.7 %copy-start.109 = (f32[288]{0:T(512)}, f32[288]{0:T(512)S(1)}, u32[]{:S(2)}) copy-start(f32[288]{0:T(512)S(1)} %fusion.81) | copy-start | bytes 3460
  158.4 37.8 %copy-start.112 = (s32[576]{0:T(1024)}, s32[576]{0:T(1024)S(1)}, u32[]{:S(2)}) copy-start(s32[576]{0:T(1024)S(1)} %fusion.84) | copy-start | bytes 6916
  168.2 24.8 %copy-start.25 = (bf16[288,512]{1,0:T(8,128)(2,1)S(1)}, bf16[288,512]{1,0:T(8,128)(2,1)}, u32[]{:S(2)}) copy-start(bf16[288,512]{1,0:T(8,128)(2,1)} %get-tuple-element.85) | copy-start | bytes 884740
  193.0 78.5 %all-gather.7.cloned.1.call-start = ((), (), s32[]{:S(2)}) async-start(), calls=%async_computation.14 | async-start | bytes 3112960 | tf_op jit(solution)/shard_map/all_gather | solution.py:209
  225.6 108.0 %reduce-scatter.9.cloned.1.call-start = ((), (), s32[]{:S(2)}) async-start(), calls=%async_computation.17 | async-start | bytes 6225920 | tf_op jit(solution)/shard_map/reduce_scatter | solution.py:256
  232.1 10.6 %copy-start.28 = (bf16[2,512,512]{2,1,0:T(8,128)(2,1)S(1)}, bf16[2,512,512]{2,1,0:T(8,128)(2,1)}, u32[]{:S(2)}) copy-start(bf16[2,512,512]{2,1,0:T(8,128)(2,1)} %param.32) | copy-start | bytes 3145732
  246.5 149.3 %reduce-scatter.11.cloned.1.call-start = ((), (), s32[]{:S(2)}) async-start(), calls=%async_computation.19 | async-start | bytes 6225920 | tf_op jit(solution)/shard_map/reduce_scatter | solution.py:256
  271.4 10.7 %copy-start.29 = (bf16[2,512,512]{2,1,0:T(8,128)(2,1)S(1)}, bf16[2,512,512]{2,1,0:T(8,128)(2,1)}, u32[]{:S(2)}) copy-start(bf16[2,512,512]{2,1,0:T(8,128)(2,1)} %param.32) | copy-start | bytes 3145732
  285.9 172.2 %reduce-scatter.5.cloned.1.call-start = ((), (), s32[]{:S(2)}) async-start(), calls=%async_computation.13 | async-start | bytes 6225920 | tf_op jit(solution)/shard_map/reduce_scatter | solution.py:219
  293.0 227.5 %reduce-scatter.7.cloned.1.call-start = ((), (), s32[]{:S(2)}) async-start(), calls=%async_computation.15 | async-start | bytes 6225920 | tf_op jit(solution)/shard_map/reduce_scatter | solution.py:219
  300.5 41.9 %copy-start.64 = (f32[2,8,144]{2,1,0:T(8,128)S(1)}, f32[2,8,144]{2,1,0:T(8,128)}, u32[]{:S(2)}) copy-start(f32[2,8,144]{2,1,0:T(8,128)} %copy-done.63) | copy-start | bytes 27652
  300.5 43.2 %copy-start.66 = (f32[2,8,144]{2,1,0:T(8,128)S(1)}, f32[2,8,144]{2,1,0:T(8,128)}, u32[]{:S(2)}) copy-start(f32[2,8,144]{2,1,0:T(8,128)} %copy-done.65) | copy-start | bytes 27652
  336.5 62.2 %all-to-all-start.5 = ((bf16[2,304,512]{2,0,1:T(2,128)(2,1)}), bf16[2,304,512]{2,0,1:T(2,128)(2,1)S(1)}, u32[]{:S(2)}, u32[]{:S(2)}) async-start(bf16[2,304,512]{2,0,1:T(2,128)(2,1)} %copy.269), calls=%async_computation.8 | async-start | bytes 1245184 | tf_op jit(solution)/shard_map/all_to_all | solution.py:257
  343.7 59.6 %copy-start.111 = (s32[576]{0:T(1024)S(1)}, s32[576]{0:T(1024)}, u32[]{:S(2)}) copy-start(s32[576]{0:T(1024)} %copy-done.110) | copy-start | bytes 6916
  343.7 59.6 %copy-start.117 = (bf16[2,512]{1,0:T(2,128)(2,1)S(1)}, bf16[2,512]{1,0:T(2,128)(2,1)}, u32[]{:S(2)}) copy-start(bf16[2,512]{1,0:T(2,128)(2,1)} %param.35) | copy-start | bytes 6148
  398.6 126.1 %all-to-all-start.7 = ((bf16[2,304,512]{2,0,1:T(2,128)(2,1)}), bf16[2,304,512]{2,0,1:T(2,128)(2,1)}, u32[]{:S(2)}, u32[]{:S(2)}) async-start(bf16[2,304,512]{2,0,1:T(2,128)(2,1)} %copy.286), calls=%async_computation.11 | async-start | bytes 1245184 | tf_op jit(solution)/shard_map/all_to_all | solution.py:257
  524.7 22.2 %all-to-all-start.1 = ((bf16[2,304,512]{2,0,1:T(2,128)(2,1)}), bf16[2,304,512]{2,0,1:T(2,128)(2,1)}, u32[]{:S(2)}, u32[]{:S(2)}) async-start(bf16[2,304,512]{2,0,1:T(2,128)(2,1)} %copy.249), calls=%async_computation.2 | async-start | bytes 1245184 | tf_op jit(solution)/shard_map/all_to_all | solution.py:221
  542.2 11.8 %copy-start.115 = (f32[2,512]{1,0:T(2,128)S(1)}, f32[2,512]{1,0:T(2,128)}, u32[]{:S(2)}) copy-start(f32[2,512]{1,0:T(2,128)} %get-tuple-element.52) | copy-start | bytes 12292
  542.2 11.8 %copy-start.116 = (f32[2,512]{1,0:T(2,128)S(1)}, f32[2,512]{1,0:T(2,128)}, u32[]{:S(2)}) copy-start(f32[2,512]{1,0:T(2,128)} %get-tuple-element.50) | copy-start | bytes 12292
  546.9 52.6 %all-to-all-start.3 = ((bf16[2,304,512]{2,0,1:T(2,128)(2,1)}), bf16[2,304,512]{2,0,1:T(2,128)(2,1)}, u32[]{:S(2)}, u32[]{:S(2)}) async-start(bf16[2,304,512]{2,0,1:T(2,128)(2,1)} %copy.263), calls=%async_computation.5 | async-start | bytes 1245184 | tf_op jit(solution)/shard_map/all_to_all | solution.py:221
  551.1 265.9 %all-reduce.6.cloned.1.call-start = ((), (), s32[]{:S(2)}) async-start(), calls=%async_computation.20 | async-start | bytes 8388608 | tf_op jit(solution)/shard_map/psum | solution.py:307
  659.9 9.4 %copy-start.36 = (f32[288,512]{1,0:T(8,128)}, f32[288,512]{1,0:T(8,128)S(1)}, u32[]{:S(2)}) copy-start(f32[288,512]{1,0:T(8,128)S(1)} %fusion.117) | copy-start | bytes 1769476
  673.9 50.0 %copy-start.12 = (f32[288,512]{1,0:T(8,128)S(1)}, f32[288,512]{1,0:T(8,128)}, u32[]{:S(2)}) copy-start(f32[288,512]{1,0:T(8,128)} %copy-done.11) | copy-start | bytes 1769476
  673.9 50.0 %copy-start.14 = (f32[288,512]{1,0:T(8,128)S(1)}, f32[288,512]{1,0:T(8,128)}, u32[]{:S(2)}) copy-start(f32[288,512]{1,0:T(8,128)} %copy-done.13) | copy-start | bytes 1769476
  (84 other events, 315.2 us)
Sparse Core Ops, SparseCore 0:
  105.5 37.4 all-gather.8
  145.4 38.5 all-gather.4
  193.1 37.4 all-gather.10
  232.8 38.5 all-gather.6
  274.3 59.2 reduce-scatter.8
  336.5 59.2 reduce-scatter.10
  398.8 59.2 reduce-scatter.4
  461.2 59.2 reduce-scatter.6
  674.0 143.0 all-reduce.5
where the time goes:
time: 835 us; the launch traced here: 829 us
  waiting for transfers between devices  306 us (37%)
  local copies, waits for them, and re-layouts  160 us (19%)
  blocking collectives  130 us (16%)
  matrix products  115 us (14%)
  other arithmetic  82.7 us (10%)
  starting transfers between devices  19 us (2%)
  between operations  15.7 us (2%)
    reduce_scatter x2, waiting for transfers between devices, on_device(): lax.psum_scatter(partial_out, 'narrow', scatter_dimension=1, tiled=True)  110 us
    psum x1, waiting for transfers between devices, on_device(): lax.psum((acc_gain1, acc_shift1, acc_qkv, acc_query_bias, acc_value_bias,...  90.1 us
    reduce_scatter x2, waiting for transfers between devices, on_device(): lax.psum_scatter(grad_partial, 'narrow', scatter_dimension=1, tiled=True)  83.8 us
    all_to_all x2, blocking collectives, on_device(): lax.all_to_all(grad_send, 'wide', split_axis=0, concat_axis=1, tiled=True)  46.2 us
    all_to_all x2, blocking collectives, on_device(): lax.all_to_all(send_rows, 'wide', split_axis=0, concat_axis=1, tiled=True)  42.3 us
    psum x1, blocking collectives, on_device(): lax.psum((acc_gain1, acc_shift1, acc_qkv, acc_query_bias, acc_value_bias,...  41.3 us
    unnamed x244, local copies, waits for them, and re-layouts  23.6 us
    all_gather x2, waiting for transfers between devices, on_device(): expert_rows = lax.all_gather(arrived, 'narrow', axis=1, tiled=True)  19.2 us
  transfers between devices with their start and end apart: 13, of which 7 were waited for; matrix products, arithmetic and copies ran while one was open for 23% of the time, Pallas kernels for 0%

commit v1 on v0

v1 whole, which is shorter than its diff:
```python
import functools
from types import SimpleNamespace

import jax
import jax.numpy as jnp
from jax import lax
from jax.experimental import pallas as pl
from jax.experimental.pallas import tpu as pltpu
from jax.sharding import PartitionSpec as P

HEADS = 8
HEAD_DIM = 64
MESH = pl.DeviceIdType.MESH
BF = jnp.bfloat16
F32 = jnp.float32
VMEM_LIMIT = 60 * 2**20


def dot(a, b):
    return lax.dot_general(a, b, (((1,), (0,)), ((), ())), preferred_element_type=F32)


def dot_nt(a, b):
    return lax.dot_general(a, b, (((1,), (1,)), ((), ())), preferred_element_type=F32)


def dot_tn(a, b):
    return lax.dot_general(a, b, (((0,), (0,)), ((), ())), preferred_element_type=F32)


class Geometry:
    def __init__(self, n_wide, n_narrow, local_experts):
        self.planes = n_wide // 2
        self.places = n_narrow
        self.local_experts = local_experts
        self.plane_experts = 2 * local_experts
        self.group = n_narrow // self.plane_experts
        self.partners = self.planes * self.plane_experts

    def here(self):
        wide, place = lax.axis_index("wide"), lax.axis_index("narrow")
        return wide // 2, wide % 2, place

    def mine(self):
        z, _, n = self.here()
        return z * self.plane_experts + n // self.group

    def partner(self, p):
        _, k, n = self.here()
        place = (p % self.plane_experts) * self.group + n % self.group
        return ((p // self.plane_experts) * 2 + k, place)


def remote(src, dst, send_sem, recv_sem, device):
    return pltpu.make_async_remote_copy(
        src_ref=src,
        dst_ref=dst,
        send_sem=send_sem,
        recv_sem=recv_sem,
        device_id=device,
        device_id_type=MESH,
    )


def norm_parts(values):
    centred = values - jnp.mean(values, axis=-1, keepdims=True)
    scale = lax.rsqrt(jnp.mean(centred * centred, axis=-1, keepdims=True) + 1e-06)
    return centred * scale, scale


def norm_back(grad, unit, scale, gain):
    pulled = grad * gain
    inner = jnp.mean(pulled, axis=-1, keepdims=True)
    along = jnp.mean(pulled * unit, axis=-1, keepdims=True)
    return scale * (pulled - inner - unit * along)


def head_pair(rows, low):
    zero = jnp.zeros_like(rows)
    return jnp.concatenate([jnp.where(low, rows, zero), jnp.where(low, zero, rows)], axis=0)


def pair_probs(stacked, keys, length):
    scores = dot_nt(stacked, keys) * HEAD_DIM ** (-0.5)
    visible = lax.broadcasted_iota(jnp.int32, scores.shape, 1) < length
    scores = jnp.where(visible, scores, -1e30)
    raised = jnp.exp(scores - jnp.max(scores, axis=-1, keepdims=True))
    return raised / jnp.sum(raised, axis=-1, keepdims=True)


def attend_image(queries, keys, values, length):
    seq = queries.shape[0]
    low = lax.broadcasted_iota(jnp.int32, (seq, 128), 1) < HEAD_DIM
    parts = []
    for g in range(queries.shape[1] // 128):
        cols = slice(g * 128, (g + 1) * 128)
        probs = pair_probs(head_pair(queries[:, cols], low), keys[:, cols], length).astype(BF)
        out = dot(probs, values[:, cols])
        parts.append(jnp.where(low, out[:seq], out[seq:]).astype(BF))
    return jnp.concatenate(parts, axis=1)


def attend_image_back(queries, keys, values, length, grad):
    seq = queries.shape[0]
    low = lax.broadcasted_iota(jnp.int32, (seq, 128), 1) < HEAD_DIM
    scale = HEAD_DIM ** (-0.5)
    parts = ([], [], [])
    for g in range(queries.shape[1] // 128):
        cols = slice(g * 128, (g + 1) * 128)
        stacked = head_pair(queries[:, cols], low)
        stacked_grad = head_pair(grad[:, cols], low)
        probs = pair_probs(stacked, keys[:, cols], length)
        grad_probs = dot_nt(stacked_grad, values[:, cols])
        parts[2].append(dot_tn(probs.astype(BF), stacked_grad).astype(BF))
        centre = jnp.sum(probs * grad_probs, axis=-1, keepdims=True)
        grad_scores = (probs * (grad_probs - centre)).astype(BF)
        grad_q = dot(grad_scores, keys[:, cols])
        parts[0].append((jnp.where(low, grad_q[:seq], grad_q[seq:]) * scale).astype(BF))
        parts[1].append((dot_tn(grad_scores, stacked) * scale).astype(BF))
    return [jnp.concatenate(part, axis=1) for part in parts]


def split_two(values):
    high = values.astype(BF)
    return high, (values - high.astype(F32)).astype(BF)


def each(count, step, unroll=False):
    if unroll:
        for i in range(count):
            step(i)
    else:

        def body(i, _):
            step(i)
            return 0

        lax.fori_loop(0, count, body, 0)


class Swap:
    def __init__(self, geo, block, src, dst, sems):
        self.geo, self.block, self.src, self.dst = geo, block, src, dst
        self.send_sem, self.recv_sem, self.local_sem = sems

    def rows(self, ref, p):
        return ref.at[pl.ds(pl.multiple_of(p * self.block, 16), self.block)]

    def local(self):
        mine = self.geo.mine()
        return pltpu.make_async_copy(self.rows(self.src, mine), self.rows(self.dst, mine), self.local_sem)

    def send(self, p):
        mine = self.geo.mine()

        @pl.when(p == mine)
        def _():
            self.local().start()

        @pl.when(p != mine)
        def _():
            remote(
                self.rows(self.src, p),
                self.rows(self.dst, mine),
                self.send_sem.at[p],
                self.recv_sem.at[mine],
                self.geo.partner(p),
            ).start()

    def copy(self, p):
        return remote(
            self.rows(self.src, p),
            self.rows(self.dst, p),
            self.send_sem.at[p],
            self.recv_sem.at[p],
            self.geo.partner(p),
        )

    def wait_got(self, p):
        mine = self.geo.mine()

        @pl.when(p == mine)
        def _():
            self.local().wait()

        @pl.when(p != mine)
        def _():
            self.copy(p).wait_recv()

    def wait_sent(self):
        mine = self.geo.mine()
        each(self.geo.partners - 1, lambda i: self.copy(lax.rem(mine + 1 + i, self.geo.partners)).wait_send())


def swap_sems(geo):
    dma = pltpu.SemaphoreType.DMA
    return [dma((geo.partners,)), dma((geo.partners,)), dma]


class Weights:
    def __init__(self, geo, own, full, tiles, all_tiles, sems):
        self.geo, self.own, self.full, self.tiles, self.all_tiles = geo, own, full, tiles, all_tiles
        (
            self.send_sem,
            self.recv_sem,
            self.tile_send,
            self.tile_recv,
            self.relay_send,
            self.relay_recv,
            self.local_sem,
            self.tile_local,
        ) = sems

    @staticmethod
    def sems(geo):
        dma = pltpu.SemaphoreType.DMA
        sends, places = (2, geo.local_experts, geo.group), (geo.places,)
        return [dma(sends), dma(places), dma(sends), dma(places), dma(places), dma(places), dma, dma]

    def slot(self, core, s):
        part = self.own[core].shape[2 - core]
        spot = pl.ds(pl.multiple_of(s * part, 128), part)
        return self.full[0].at[:, spot] if core == 0 else self.full[1].at[spot]

    def targets(self):
        geo = self.geo
        z, k, n = geo.here()
        for i in range(geo.local_experts):
            for g in range(geo.group):
                place = (geo.local_experts * k + i) * geo.group + g
                for core in range(2):
                    yield i, g, core, jnp.logical_and(k == core, place == n), (z * 2 + core, place)

    def start(self):
        n = self.geo.here()[2]
        for i, g, core, here, device in self.targets():

            @pl.when(here)
            def _():
                pltpu.make_async_copy(self.own[core].at[i], self.slot(core, n), self.local_sem).start()
                pltpu.make_async_copy(self.tiles.at[i], self.all_tiles.at[n], self.tile_local).start()

            @pl.when(jnp.logical_not(here))
            def _():
                remote(
                    self.own[core].at[i],
                    self.slot(core, n),
                    self.send_sem.at[core, i, g],
                    self.recv_sem.at[n],
                    device,
                ).start()
                remote(
                    self.tiles.at[i],
                    self.all_tiles.at[n],
                    self.tile_send.at[core, i, g],
                    self.tile_recv.at[n],
                    device,
                ).start()

    def relay_copy(self, core, s):
        z, k, n = self.geo.here()
        spot = self.slot(core, s)
        return remote(spot, spot, self.relay_send.at[s], self.relay_recv.at[s], (z * 2 + 1 - k, n))

    def relay(self):
        geo = self.geo
        z, k, n = geo.here()
        owner_core = (n // geo.group) // geo.local_experts
        sibling = (z * 2 + 1 - k, n)
        for s in range(geo.places):
            here = jnp.logical_and(k == owner_core, n == s)

            @pl.when(here)
            def _():
                pltpu.make_async_copy(self.tiles.at[0], self.all_tiles.at[s], self.tile_local).wait()

            @pl.when(jnp.logical_not(here))
            def _():
                spot = self.all_tiles.at[s]
                remote(spot, spot, self.tile_send.at[0, 0, 0], self.tile_recv.at[s], sibling).wait_recv()

            for core in range(2):
                spot = self.slot(core, s)

                @pl.when(jnp.logical_and(k == core, here))
                def _():
                    pltpu.make_async_copy(self.own[core].at[0], spot, self.local_sem).wait()

                @pl.when(jnp.logical_and(k == core, jnp.logical_not(here)))
                def _():
                    remote(spot, spot, self.send_sem.at[0, 0, 0], self.recv_sem.at[s], sibling).wait_recv()

                @pl.when(k == core)
                def _():
                    self.relay_copy(core, s).start()

    def finish(self):
        k = self.geo.here()[1]
        for s in range(self.geo.places):
            for core in range(2):

                @pl.when(k == core)
                def _():
                    self.relay_copy(1 - core, s).wait_recv()

    def wait_sent(self):
        k = self.geo.here()[1]
        for s in range(self.geo.places):
            for core in range(2):

                @pl.when(k == core)
                def _():
                    self.relay_copy(core, s).wait_send()

        for i, g, core, here, device in self.targets():

            @pl.when(jnp.logical_not(here))
            def _():
                remote(
                    self.own[core].at[i],
                    self.slot(core, 0),
                    self.send_sem.at[core, i, g],
                    self.recv_sem.at[0],
                    device,
                ).wait_send()
                remote(
                    self.tiles.at[i],
                    self.all_tiles.at[0],
                    self.tile_send.at[core, i, g],
                    self.tile_recv.at[0],
                    device,
                ).wait_send()


class ExpertGrads:
    def __init__(self, geo, grads, got, tiles, got_tiles, inbox, inbox_tiles, sems):
        self.geo, self.grads, self.got, self.tiles = geo, grads, got, tiles
        self.got_tiles, self.inbox, self.inbox_tiles = got_tiles, inbox, inbox_tiles
        (
            self.pair_send,
            self.pair_recv,
            self.send_sem,
            self.recv_sem,
            self.tile_send,
            self.tile_recv,
            self.local_sem,
            self.tile_local,
        ) = sems
        self.half = grads.shape[2] // 2
        self.part = grads.shape[2] // geo.places

    @staticmethod
    def sems(geo):
        dma = pltpu.SemaphoreType.DMA
        owners = (geo.local_experts, geo.group)
        return [
            dma((3,)),
            dma((3,)),
            dma((2, geo.places)),
            dma((2,) + owners),
            dma((geo.places,)),
            dma(owners),
            dma((2,)),
            dma,
        ]

    def columns(self, layer, first, count):
        return self.grads.at[layer, :, pl.ds(pl.multiple_of(first, 128), count)]

    def pair(self, layer):
        z, k, n = self.geo.here()
        away = self.columns(layer, (1 - k) * self.half, self.half)
        sibling = (z * 2 + 1 - k, n)
        return remote(away, self.got.at[layer], self.pair_send.at[layer], self.pair_recv.at[layer], sibling)

    def pair_tiles(self):
        z, k, n = self.geo.here()
        return remote(self.tiles, self.got_tiles, self.pair_send.at[2], self.pair_recv.at[2], (z * 2 + 1 - k, n))

    def towards(self):
        n = self.geo.here()[2]
        expert = n // self.geo.group
        return expert // self.geo.local_experts, expert % self.geo.local_experts, n % self.geo.group

    def slices(self):
        geo = self.geo
        z, k, n = geo.here()
        owner_core = self.towards()[0]
        for j in range(geo.places // 2):
            s = k * (geo.places // 2) + j
            yield s, jnp.logical_and(owner_core == k, n == s), (z * 2 + owner_core, s)

    def forward(self):
        k = self.geo.here()[1]
        _, i, g = self.towards()
        for layer in range(2):
            self.pair(layer).wait()
            for j in range(self.geo.places // 2):
                here = pl.ds(j * self.part, self.part)
                there = pl.ds(pl.multiple_of(k * self.half + j * self.part, 128), self.part)
                total = self.grads[layer, :, there].astype(F32) + self.got[layer, :, here].astype(F32)
                self.grads[layer, :, there] = total.astype(BF)
            for s, here, owner in self.slices():
                src = self.columns(layer, s * self.part, self.part)
                dst = self.inbox.at[layer, i, g]

                @pl.when(here)
                def _():
                    pltpu.make_async_copy(src, dst, self.local_sem.at[layer]).start()

                @pl.when(jnp.logical_not(here))
                def _():
                    remote(
                        src, dst, self.send_sem.at[layer, s], self.recv_sem.at[layer, i, g], owner
                    ).start()

        self.pair_tiles().wait()
        self.tiles[...] = self.tiles[...] + self.got_tiles[...]
        for s, here, owner in self.slices():
            src, dst = self.tiles.at[s], self.inbox_tiles.at[i, g]

            @pl.when(here)
            def _():
                pltpu.make_async_copy(src, dst, self.tile_local).start()

            @pl.when(jnp.logical_not(here))
            def _():
                remote(src, dst, self.tile_send.at[s], self.tile_recv.at[i, g], owner).start()

    def wait_got(self):
        geo = self.geo
        z, k, n = geo.here()
        sibling = (z * 2 + 1 - k, n)
        keeper = n // (geo.places // 2)
        for i in range(geo.local_experts):
            for g in range(geo.group):
                source = (k * geo.local_experts + i) * geo.group + g
                here = jnp.logical_and(source == n, keeper == k)
                for layer in range(2):
                    spot = self.inbox.at[layer, i, g]

                    @pl.when(here)
                    def _():
                        pltpu.make_async_copy(spot, spot, self.local_sem.at[layer]).wait()

                    @pl.when(jnp.logical_not(here))
                    def _():
                        remote(
                            spot, spot, self.send_sem.at[0, 0], self.recv_sem.at[layer, i, g], sibling
                        ).wait_recv()

                spot = self.inbox_tiles.at[i, g]

                @pl.when(here)
                def _():
                    pltpu.make_async_copy(spot, spot, self.tile_local).wait()

                @pl.when(jnp.logical_not(here))
                def _():
                    remote(spot, spot, self.tile_send.at[0], self.tile_recv.at[i, g], sibling).wait_recv()

    def wait_sent(self):
        for s, here, owner in self.slices():

            @pl.when(jnp.logical_not(here))
            def _():
                for layer in range(2):
                    src = self.columns(layer, s * self.part, self.part)
                    remote(
                        src, src, self.send_sem.at[layer, s], self.recv_sem.at[0, 0, 0], owner
                    ).wait_send()
                src = self.tiles.at[s]
                remote(src, src, self.tile_send.at[s], self.tile_recv.at[0, 0], owner).wait_send()


class DenseSum:
    def __init__(self, geo, mine, got_pair, got_plane, piece, got_z, whole, small, s_pair, s_plane, s_z, sems):
        self.geo, self.mine, self.got_pair, self.got_plane = geo, mine, got_pair, got_plane
        self.piece, self.got_z, self.whole = piece, got_z, whole
        self.small, self.s_pair, self.s_plane, self.s_z = small, s_pair, s_plane, s_z
        self.sems = sems
        self.half = mine.shape[0] // 2
        self.rows = self.half // geo.places
        self.columns = mine.shape[1] // geo.planes

    @staticmethod
    def semaphores(geo):
        dma = pltpu.SemaphoreType.DMA
        places, planes, both = (geo.places,), (geo.planes,), (geo.places, geo.planes)
        shapes = dict(
            pair=(1,), plane=places, z=planes, zg=planes, pg=both, cg=both, sp=(1,), sn=places, sz=planes
        )
        return list(shapes), [dma(s) for s in shapes.values() for _ in range(2)]

    def sem(self, name):
        names, _ = self.semaphores(self.geo)
        i = names.index(name) * 2
        return self.sems[i], self.sems[i + 1]

    def where(self):
        z, k, n = self.geo.here()
        return z, k, n, (z * 2 + 1 - k, n)

    def half_rows(self, k):
        return self.mine.at[pl.ds(pl.multiple_of(k * self.half, 16), self.half)]

    def pair(self):
        z, k, n, sibling = self.where()
        send, recv = self.sem("pair")
        return remote(self.half_rows(1 - k), self.got_pair, send.at[0], recv.at[0], sibling)

    def place_rows(self, k, q):
        return pl.ds(pl.multiple_of(k * self.half + q * self.rows, 16), self.rows)

    def plane_copy(self, q):
        z, k, n, _ = self.where()
        send, recv = self.sem("plane")
        src = self.mine.at[self.place_rows(k, q)]
        return remote(src, self.got_plane.at[n], send.at[q], recv.at[n], (z * 2 + k, q))

    def plane_start(self):
        z, k, n, _ = self.where()
        geo = self.geo
        self.pair().wait()
        keep = self.half_rows(k)
        step = self.half // 4
        for i in range(4):
            there = pl.ds(pl.multiple_of(k * self.half + i * step, 16), step)
            total = self.mine[there].astype(F32) + self.got_pair[i * step : (i + 1) * step].astype(F32)
            self.mine[there] = total.astype(BF)
        for i in range(1, geo.places):
            self.plane_copy(lax.rem(n + i, geo.places)).start()
        self.got_plane[n] = self.mine[self.place_rows(k, n)]

    def z_copy(self, q):
        z, k, n, _ = self.where()
        send, recv = self.sem("z")
        return remote(self.piece.at[q], self.got_z.at[z], send.at[q], recv.at[z], (q * 2 + k, n))

    def z_start(self):
        z, k, n, sibling = self.where()
        geo = self.geo
        send, recv = self.sem("plane")
        for i in range(1, geo.places):
            q = lax.rem(n + i, geo.places)
            spot = self.got_plane.at[q]
            remote(spot, spot, send.at[q], recv.at[q], sibling).wait_recv()
        for p in range(geo.planes):
            cols = slice(p * self.columns, (p + 1) * self.columns)
            total = self.got_plane[0, :, cols].astype(F32)
            for i in range(1, geo.places):
                total = total + self.got_plane[i, :, cols].astype(F32)
            self.piece[p] = total.astype(BF)
        for i in range(1, geo.planes):
            self.z_copy(lax.rem(z + i, geo.planes)).start()
        self.got_z[z] = self.piece[z]

    def spot(self, k, q, p):
        cols = pl.ds(pl.multiple_of(p * self.columns, 128), self.columns)
        return self.whole.at[self.place_rows(k, q), cols]

    def gather_copy(self, name, k, q, p, index, device):
        send, recv = self.sem(name)
        spot = self.spot(k, q, p)
        return remote(spot, spot, send.at[index], recv.at[index], device)

    def zg_copy(self, q):
        z, k, n, _ = self.where()
        send, recv = self.sem("zg")
        spot = self.spot(k, n, z)
        return remote(spot, spot, send.at[q], recv.at[z], (q * 2 + k, n))

    def pg_copy(self, q, p):
        z, k, n, _ = self.where()
        send, recv = self.sem("pg")
        spot = self.spot(k, n, p)
        return remote(spot, spot, send.at[q, p], recv.at[n, p], (z * 2 + k, q))

    def cg_copy(self, q, p):
        z, k, n, sibling = self.where()
        send, recv = self.sem("cg")
        spot = self.spot(k, q, p)
        return remote(spot, spot, send.at[q, p], recv.at[q, p], sibling)

    def gather_start(self):
        z, k, n, sibling = self.where()
        geo = self.geo
        send, recv = self.sem("z")
        for i in range(1, geo.planes):
            q = lax.rem(z + i, geo.planes)
            spot = self.got_z.at[q]
            remote(spot, spot, send.at[q], recv.at[q], sibling).wait_recv()
        total = self.got_z[0].astype(F32)
        for i in range(1, geo.planes):
            total = total + self.got_z[i].astype(F32)
        cols = pl.ds(pl.multiple_of(z * self.columns, 128), self.columns)
        self.whole[self.place_rows(k, n), cols] = total.astype(BF)
        for i in range(1, geo.planes):
            self.zg_copy(lax.rem(z + i, geo.planes)).start()
        send, recv = self.sem("zg")
        for i in range(geo.planes):
            p = lax.rem(z + i, geo.planes)
            if i > 0:
                spot = self.spot(k, n, p)
                remote(spot, spot, send.at[p], recv.at[p], sibling).wait_recv()
            for j in range(1, geo.places):
                self.pg_copy(lax.rem(n + j, geo.places), p).start()
            self.cg_copy(n, p).start()

    def gather_finish(self):
        z, k, n, sibling = self.where()
        geo = self.geo
        send, recv = self.sem("pg")
        for j in range(1, geo.places):
            q = lax.rem(n + j, geo.places)
            for i in range(geo.planes):
                p = lax.rem(z + i, geo.planes)
                spot = self.spot(k, q, p)
                remote(spot, spot, send.at[q, p], recv.at[q, p], sibling).wait_recv()
                self.cg_copy(q, p).start()
        send, recv = self.sem("cg")
        for q in range(geo.places):
            for p in range(geo.planes):
                spot = self.spot(1 - k, q, p)
                remote(spot, spot, send.at[q, p], recv.at[q, p], sibling).wait_recv()

    def small_pair(self):
        send, recv = self.sem("sp")
        return remote(self.small, self.s_pair, send.at[0], recv.at[0], self.where()[3])

    def sn_copy(self, q):
        z, k, n, _ = self.where()
        send, recv = self.sem("sn")
        return remote(self.s_plane.at[n], self.s_plane.at[n], send.at[q], recv.at[n], (z * 2 + k, q))

    def sz_copy(self, q):
        z, k, n, _ = self.where()
        send, recv = self.sem("sz")
        return remote(self.s_z.at[z], self.s_z.at[z], send.at[q], recv.at[z], (q * 2 + k, n))

    def small_plane(self):
        z, k, n, _ = self.where()
        self.small_pair().wait()
        self.s_plane[n] = self.small[...] + self.s_pair[...]
        for i in range(1, self.geo.places):
            self.sn_copy(lax.rem(n + i, self.geo.places)).start()

    def small_z(self):
        z, k, n, sibling = self.where()
        geo = self.geo
        send, recv = self.sem("sn")
        for i in range(1, geo.places):
            q = lax.rem(n + i, geo.places)
            spot = self.s_plane.at[q]
            remote(spot, spot, send.at[q], recv.at[q], sibling).wait_recv()
        total = self.s_plane[0]
        for i in range(1, geo.places):
            total = total + self.s_plane[i]
        self.s_z[z] = total
        for i in range(1, geo.planes):
            self.sz_copy(lax.rem(z + i, geo.planes)).start()

    def small_finish(self, out):
        z, k, n, sibling = self.where()
        geo = self.geo
        send, recv = self.sem("sz")
        for i in range(1, geo.planes):
            q = lax.rem(z + i, geo.planes)
            spot = self.s_z.at[q]
            remote(spot, spot, send.at[q], recv.at[q], sibling).wait_recv()
        total = self.s_z[0]
        for i in range(1, geo.planes):
            total = total + self.s_z[i]
        out[...] = total

    def wait_sent(self):
        z, k, n, _ = self.where()
        geo = self.geo
        for i in range(1, geo.places):
            q = lax.rem(n + i, geo.places)
            self.plane_copy(q).wait_send()
            self.sn_copy(q).wait_send()
            for p in range(geo.planes):
                self.pg_copy(q, p).wait_send()
        for i in range(1, geo.planes):
            q = lax.rem(z + i, geo.planes)
            self.z_copy(q).wait_send()
            self.zg_copy(q).wait_send()
            self.sz_copy(q).wait_send()
        for q in range(geo.places):
            for p in range(geo.planes):
                self.cg_copy(q, p).wait_send()


def greet_start(devices):
    barrier = pltpu.get_barrier_semaphore()
    for device in devices:
        pl.semaphore_signal(barrier, inc=1, device_id=device, device_id_type=MESH)


def all_devices(geo):
    z, k, n = geo.here()
    found = [(z * 2 + k, lax.rem(n + i, geo.places)) for i in range(1, geo.places)]
    found += [(z * 2 + 1 - k, lax.rem(n + i, geo.places)) for i in range(geo.places)]
    for i in range(1, geo.planes):
        other = lax.rem(z + i, geo.planes)
        found += [geo.partner(other * geo.plane_experts + j) for j in range(geo.plane_experts)]
    return found


def lane_row(row, count):
    shape = (count, row.shape[1])
    diagonal = lax.broadcasted_iota(jnp.int32, shape, 0) == lax.broadcasted_iota(jnp.int32, shape, 1)
    return jnp.sum(jnp.where(diagonal, row, 0.0), axis=1, keepdims=True)


def row_of(column, lanes):
    shape = (column.shape[0], lanes)
    diagonal = lax.broadcasted_iota(jnp.int32, shape, 0) == lax.broadcasted_iota(jnp.int32, shape, 1)
    return jnp.sum(jnp.where(diagonal, column, 0.0), axis=0, keepdims=True)


def put_pair(tail, high, low):
    row = lax.broadcasted_iota(jnp.int32, tail.shape, 0)
    return jnp.where(row == 14, high, jnp.where(row == 15, low, tail))


def block_kernel(geo, sizes, names, *refs):
    r = SimpleNamespace(**dict(zip(names, refs, strict=True)))
    rows, per_micro, seq, capacity, block, width, hidden = sizes
    experts = geo.partners
    slots = experts * block
    images = rows // seq
    z, k, n = geo.here()
    quad = geo.plane_experts
    chunk = quad * block
    part = r.w1.shape[2]
    tile = 256

    r.mine = r.hidden.at[0:width, 0 : 4 * width]
    r.grad_qkv = r.grad_pre.at[0:rows, 0 : 3 * width]
    r.grad_branch = r.grad_pre.at[rows : 2 * rows, 0:width]
    r.grad_att = r.grad_pre.at[rows : 2 * rows, width : 2 * width]
    r.logits_high = r.grad_pre.at[0:rows, 4 * width - 256 : 4 * width - 128]
    r.logits_low = r.grad_pre.at[0:rows, 4 * width - 128 : 4 * width]
    lanes = -(-rows // 128) * 128
    r.table0 = r.grad_pre.at[:, 0:lanes]
    r.slot_grad = r.grad_pre.at[:, 3 * width : 3 * width + 256]

    def span(i, count, align=16):
        return pl.ds(pl.multiple_of(i * count, align), count)

    def sems(name):
        return [ref for key, ref in zip(names, refs, strict=True) if key.startswith(name)]

    greet_start(all_devices(geo))
    for i in range(geo.local_experts):
        r.tile[i] = jnp.zeros((8, width), F32)
        r.tile[i, 0:1, 0:part] = r.b1[i : i + 1, :].astype(F32)
        r.tile[i, 1:2, :] = r.b2[i : i + 1, :].astype(F32)
    weights = Weights(
        geo, (r.w1, r.w2), (r.first, r.second), r.tile, r.tiles, sems("weights_sem")
    )
    cot_swap = Swap(geo, block, r.send_a, r.cot_got, sems("cot_sem"))
    x_swap = Swap(geo, block, r.send_b, r.x_got, sems("x_sem"))
    grad_swap = Swap(geo, block, r.send_a, r.grad_got, sems("grad_sem"))
    ret_swap = Swap(geo, block, r.send_b, r.ret_got, sems("ret_sem"))

    choices = r.choices[...]
    ids = lax.broadcasted_iota(jnp.int32, (experts, rows), 0)
    named = [ids == choices[i : i + 1, :] for i in range(2)]
    either = jnp.logical_or(named[0], named[1])
    first_row = lax.broadcasted_iota(jnp.int32, (rows, rows), 0)
    second_row = lax.broadcasted_iota(jnp.int32, (rows, rows), 1)
    same = (first_row >= per_micro) == (second_row >= per_micro)
    earlier = jnp.logical_and(first_row < second_row, same)
    before = dot(either.astype(F32).astype(BF), earlier.astype(F32).astype(BF))
    late = lax.broadcasted_iota(jnp.int32, (experts, rows), 1) >= per_micro
    slot = before + jnp.where(late, float(capacity), 0.0)
    r.held[...] = jnp.full(r.held.shape, -1.0, F32)
    r.held[0, :, 0:rows] = jnp.where(either, slot, -1.0)
    r.held[1, :, 0:rows] = jnp.where(named[0], slot, -1.0)
    spots = lax.broadcasted_iota(jnp.int32, (block, lanes), 0).astype(F32)

    def fill(e):
        here = span(e, block)
        either, chosen = [
            jnp.where(spots == r.held[i, pl.ds(e, 1), :], 1.0, 0.0).astype(BF) for i in range(2)
        ]
        r.table[here, :] = either[:, 0:rows]
        r.table0[here, :] = chosen

    each(experts, fill)
    r.table[pl.ds(slots, 128), :] = jnp.zeros((128, rows), BF)

    pl.semaphore_wait(pltpu.get_barrier_semaphore(), len(all_devices(geo)))
    weights.start()

    def send_cot(i):
        plane = lax.rem(z + 1 + i, geo.planes)
        blocks = dot(r.table[span(plane, chunk), :], r.cot[...])
        r.send_a[span(plane, chunk), :] = blocks.astype(BF)
        for j in range(quad):
            cot_swap.send(plane * quad + j)

    each(geo.planes, send_cot)

    def norm_in(i):
        unit, _ = norm_parts(r.tokens[span(i, seq), :].astype(F32))
        normed = unit * r.gain1[...].astype(F32) + r.shift1[...].astype(F32)
        r.normed[span(i, seq), :] = normed.astype(BF)

    each(images, norm_in)
    for c in range(3 * width // tile):
        cols = slice(c * tile, (c + 1) * tile)
        out = dot(r.normed[...], r.w_qkv[:, cols])
        if c * tile < width:
            out = out + r.bias_q[:, cols].astype(F32)
        elif c * tile >= 2 * width:
            out = out + r.bias_v[:, c * tile - 2 * width : (c + 1) * tile - 2 * width].astype(F32)
        r.qkv[:, cols] = out.astype(BF)

    def attend(i):
        here = span(i, seq)
        length = r.lengths[i // (per_micro // seq), i % (per_micro // seq)]
        r.attended[here, :] = attend_image(
            r.qkv[here, 0:width],
            r.qkv[here, width : 2 * width],
            r.qkv[here, 2 * width : 3 * width],
            length,
        )

    each(images, attend)

    def branch(i):
        here = span(i, seq)
        residual = (
            r.tokens[here, :].astype(F32)
            + dot(r.attended[here, :], r.w_out[...])
            + r.bias_out[...].astype(F32)
        )
        r.residual[here, :] = residual
        unit, _ = norm_parts(residual)
        expert_in = (unit * r.gain2[...].astype(F32) + r.shift2[...].astype(F32)).astype(BF)
        r.expert_in[here, :] = expert_in
        logits = dot(expert_in, r.w_router[...])
        raised = jnp.exp(logits - jnp.max(logits, axis=-1, keepdims=True))
        probs = raised / jnp.sum(raised, axis=-1, keepdims=True)
        r.probs[here, 0:experts] = probs

    r.probs[...] = jnp.zeros(r.probs.shape, F32)
    each(images, branch)
    probs_t = jnp.transpose(r.probs[...])[0:experts, :]
    high, low = split_two(probs_t)
    r.probs_t[0:experts, :] = high
    r.probs_t[experts : 2 * experts, :] = low

    def send_x(i):
        plane = lax.rem(z + 1 + i, geo.planes)
        blocks = dot(r.table[span(plane, chunk), :], r.expert_in[...])
        for j in range(quad):
            e = plane * quad + j
            at = e * block
            values = blocks[j * block : (j + 1) * block]
            gates = dot_nt(r.probs_t[...], r.table[pl.ds(pl.multiple_of(at, 16), 128), :])
            line = lax.broadcasted_iota(jnp.int32, gates.shape, 0)
            high = jnp.sum(jnp.where(line == e, gates, 0.0), axis=0, keepdims=True)
            low = jnp.sum(jnp.where(line == experts + e, gates, 0.0), axis=0, keepdims=True)
            r.send_b[span(e, block), :] = values.astype(BF)
            tail = put_pair(values[block - 16 :, 0:128], high, low)
            r.send_b[pl.ds(pl.multiple_of(at + block - 16, 16), 16), 0:128] = tail.astype(BF)
            x_swap.send(e)

    each(geo.planes, send_x)

    r.table_t[...] = jnp.transpose(r.table[0:slots, :])
    r.table0_t[...] = jnp.transpose(r.table0[...])[0:rows, :]
    weights.relay()
    weights.finish()
    for s in range(geo.places):
        r.bias1[:, s * part : (s + 1) * part] = jnp.broadcast_to(r.tiles[s, 0:1, 0:part], (8, part))
    cot_swap.wait_sent()
    x_swap.wait_sent()

    root = 0.7978845608028654
    r.sum_pre[...] = jnp.zeros(r.sum_pre.shape, F32)
    r.sum_ret[...] = jnp.zeros(r.sum_ret.shape, F32)

    def expert_chunk(i):
        plane = lax.rem(z + i, geo.planes)
        here = span(plane, chunk)
        for j in range(quad):
            cot_swap.wait_got(plane * quad + j)
        for j in range(quad):
            x_swap.wait_got(plane * quad + j)
        for j in range(quad):
            at = (plane * quad + j) * block
            tail = r.x_got[pl.ds(pl.multiple_of(at + block - 16, 16), 16), 0:128].astype(F32)
            gate = lane_row(tail[14:15] + tail[15:16], block)
            there = span(plane * quad + j, block)
            r.grad_ret[there, :] = (gate * r.cot_got[there, :].astype(F32)).astype(BF)
        total_ret = jnp.sum(r.grad_ret[here, :].astype(F32), axis=0, keepdims=True)
        r.sum_ret[0:1, :] = r.sum_ret[0:1, :] + total_ret
        for c in range(hidden // tile):
            cols = slice(c * tile, (c + 1) * tile)
            pre = dot(r.x_got[here, :], r.first[:, cols]) + r.bias1[0:1, cols]
            square = pre * pre
            bend = jnp.tanh(root * pre * (1.0 + 0.044715 * square))
            half = 0.5 * (1.0 + bend)
            r.hidden[here, cols] = (pre * half).astype(BF)
            slope = half + 0.5 * pre * (1.0 - bend * bend) * (root + 3 * 0.044715 * root * square)
            back = dot_nt(r.grad_ret[here, :], r.second[cols, :])
            grad_pre = (back * slope).astype(BF)
            r.grad_pre[here, cols] = grad_pre
            total = jnp.sum(grad_pre.astype(F32), axis=0, keepdims=True)
            r.sum_pre[0:1, cols] = r.sum_pre[0:1, cols] + total
        returned = dot(r.hidden[here, :], r.second[...]) + r.tiles[0, 1:2, :]
        r.send_b[here, :] = returned.astype(BF)
        grad_in = dot_nt(r.grad_pre[here, :], r.first[...])
        for j in range(quad):
            e = plane * quad + j
            there = span(e, block)
            product = r.cot_got[there, :].astype(F32) * r.send_b[there, :].astype(F32)
            high, low = split_two(row_of(jnp.sum(product, axis=-1, keepdims=True), 128))
            values = grad_in[j * block : (j + 1) * block]
            r.send_a[there, :] = values.astype(BF)
            tail = put_pair(values[block - 16 :, 0:128], high.astype(F32), low.astype(F32))
            at = pl.ds(pl.multiple_of(e * block + block - 16, 16), 16)
            r.send_a[at, 0:128] = tail.astype(BF)
            grad_swap.send(e)

    each(geo.planes, expert_chunk)
    each(experts, lambda i: ret_swap.send(lax.rem(geo.mine() + 1 + i, experts)))

    grads = ExpertGrads(
        geo,
        r.d_experts,
        r.d_got,
        r.d_tiles,
        r.d_got_tiles,
        r.inbox,
        r.inbox_tiles,
        sems("expert_sem"),
    )
    quarter = hidden // 4

    def weight_grads(side):
        for layer, left, right in ((0, r.x_got, r.grad_pre), (1, r.grad_ret, r.hidden)):
            for c in range(2):
                cols = pl.ds(pl.multiple_of(side * (hidden // 2) + c * quarter, 128), quarter)
                r.d_experts[layer, :, cols] = dot_tn(left[...], right[:, cols]).astype(BF)

    weight_grads(1 - k)
    grads.pair(0).start()
    grads.pair(1).start()
    r.d_tiles[...] = jnp.zeros(r.d_tiles.shape, F32)
    for s in range(geo.places):
        r.d_tiles[s, 0:1, 0:part] = r.sum_pre[0:1, s * part : (s + 1) * part]
        r.d_tiles[s, 1:2, :] = r.sum_ret[0:1, :]
    grads.pair_tiles().start()
    weight_grads(k)
    grads.forward()

    dense = DenseSum(
        geo,
        r.mine,
        r.got_pair,
        r.got_plane,
        r.piece,
        r.got_z,
        r.whole,
        r.small,
        r.s_pair,
        r.s_plane,
        r.s_z,
        sems("dense_sem"),
    )

    def slot_grads(e):
        grad_swap.wait_got(e)
        at = pl.ds(pl.multiple_of(e * block + block - 16, 16), 16)
        tail = r.grad_got[at, 0:128].astype(F32)
        column = lane_row(tail[14:15] + tail[15:16], block)
        lane = lax.broadcasted_iota(jnp.int32, (block, 128), 1)
        high, low = split_two(jnp.where(lane == e, column, 0.0))
        r.slot_grad[span(e, block), 0:128] = high
        r.slot_grad[span(e, block), 128:256] = low

    each(experts, slot_grads)
    for c in range(width // tile):
        cols = slice(c * tile, (c + 1) * tile)
        r.grad_two[:, cols] = dot(r.table_t[...], r.grad_got[:, cols])
    both = dot(r.table_t[...], r.slot_grad[...])
    r.grad_choice[...] = both[:, 0:128] + both[:, 128:256]
    r.small[...] = jnp.zeros(r.small.shape, F32)

    def add_small(row, value):
        r.small[row : row + 1, :] = r.small[row : row + 1, :] + jnp.sum(value, axis=0, keepdims=True)

    def norm_two_back(i):
        here = span(i, seq)
        probs = r.probs[here, :]
        choice = r.grad_choice[here, :]
        logits = probs * (choice - jnp.sum(probs * choice, axis=-1, keepdims=True))
        high, low = split_two(logits)
        r.logits_high[here, :] = high
        r.logits_low[here, :] = low
        weight = r.w_router[...]
        grad = r.grad_two[here, :]
        grad = grad + dot_nt(high[:, 0:experts], weight) + dot_nt(low[:, 0:experts], weight)
        unit, scale = norm_parts(r.residual[here, :])
        add_small(5, grad * unit)
        add_small(6, grad)
        grad = r.cot[here, :].astype(F32) + norm_back(grad, unit, scale, r.gain2[...].astype(F32))
        r.grad_two[here, :] = grad
        low_grad = grad.astype(BF)
        r.grad_branch[here, :] = low_grad
        add_small(4, low_grad.astype(F32))

    each(images, norm_two_back)
    for c in range(width // tile):
        cols = slice(c * tile, (c + 1) * tile)
        r.grad_att[:, cols] = dot_nt(r.grad_branch[...], r.w_out[cols, :]).astype(BF)
        out = dot_tn(r.attended[...], r.grad_branch[:, cols])
        r.mine[:, 3 * width + c * tile : 3 * width + (c + 1) * tile] = out.astype(BF)
    router = dot_tn(r.logits_high[...], r.expert_in[...]) + dot_tn(
        r.logits_low[...], r.expert_in[...]
    )
    r.small[8 : 8 + experts, :] = router[0:experts, :]

    def attend_back(i):
        here = span(i, seq)
        length = r.lengths[i // (per_micro // seq), i % (per_micro // seq)]
        parts = attend_image_back(
            r.qkv[here, 0:width],
            r.qkv[here, width : 2 * width],
            r.qkv[here, 2 * width : 3 * width],
            length,
            r.grad_att[here, :],
        )
        for c, value in enumerate(parts):
            r.grad_qkv[here, c * width : (c + 1) * width] = value
        add_small(2, parts[0].astype(F32))
        add_small(3, parts[2].astype(F32))

    each(images, attend_back)
    for c in range(3 * width // tile):
        cols = slice(c * tile, (c + 1) * tile)
        r.mine[:, cols] = dot_tn(r.normed[...], r.grad_qkv[:, cols]).astype(BF)
    dense.pair().start()

    def norm_one_back(i):
        here = span(i, seq)
        grad = dot_nt(r.grad_qkv[here, :], r.w_qkv[...])
        unit, scale = norm_parts(r.tokens[here, :].astype(F32))
        add_small(0, grad * unit)
        add_small(1, grad)
        r.grad_two[here, :] = r.grad_two[here, :] + norm_back(
            grad, unit, scale, r.gain1[...].astype(F32)
        )

    each(images, norm_one_back)
    dense.small_pair().start()
    tokens_copy = pltpu.make_async_copy(r.grad_two, r.grad_tokens, r.out_sem.at[1])
    tokens_copy.start()
    dense.plane_start()
    dense.small_plane()

    each(experts, ret_swap.wait_got)

    def mix(i):
        here = span(i, seq)
        total = dot(r.table_t[here, :], r.ret_got[...])
        chosen = dot(r.table0_t[here, :], r.ret_got[...])
        probs = r.probs[here, :]
        lane = lax.broadcasted_iota(jnp.int32, probs.shape, 1)
        gates = [
            jnp.sum(jnp.where(lane == r.ids[here, j : j + 1], probs, 0.0), axis=-1, keepdims=True)
            for j in range(2)
        ]
        mixed = r.residual[here, :] + gates[0] * chosen + gates[1] * (total - chosen)
        r.expert_in[here, :] = mixed.astype(BF)

    each(images, mix)
    mixed_copy = pltpu.make_async_copy(r.expert_in, r.mixed, r.out_sem.at[0])
    mixed_copy.start()
    dense.small_z()
    dense.z_start()
    grads.wait_got()
    layers_copy = pltpu.make_async_copy(r.inbox, r.d_layers, r.out_sem.at[2])
    bias_copy = pltpu.make_async_copy(r.inbox_tiles, r.d_bias, r.out_sem.at[3])
    layers_copy.start()
    bias_copy.start()
    dense.gather_start()
    dense.small_finish(r.small_out)
    dense.gather_finish()
    big_copy = pltpu.make_async_copy(r.whole, r.big_out, r.out_sem.at[4])
    big_copy.start()
    grad_swap.wait_sent()
    ret_swap.wait_sent()
    weights.wait_sent()
    grads.wait_sent()
    dense.wait_sent()
    for copy in (mixed_copy, tokens_copy, layers_copy, bias_copy, big_copy):
        copy.wait()


def on_device(
    geo,
    tokens,
    image_lengths,
    expert_index,
    grad_out,
    ln1_gain,
    ln1_bias,
    w_qkv,
    bias_query,
    bias_value,
    w_out,
    bias_out,
    ln2_gain,
    ln2_bias,
    w_router,
    experts_in,
    experts_in_bias,
    experts_out,
    experts_out_bias,
):
    micros, per_micro, width = tokens.shape
    rows = micros * per_micro
    seq = per_micro // image_lengths.shape[1]
    experts = geo.partners
    capacity = (per_micro * 42 + 20 * experts - 1) // (20 * experts)
    block = -(-(micros * capacity + 2) // 16) * 16
    slots = experts * block
    part = experts_in.shape[2]
    hidden = part * geo.places
    places, planes, local, group = geo.places, geo.planes, geo.local_experts, geo.group
    flat_ids = expert_index.reshape(rows, 2)
    row = lambda v: v[None, :]
    inputs = dict(
        tokens=tokens.reshape(rows, width),
        cot=grad_out.reshape(rows, width),
        choices=flat_ids.T,
        ids=flat_ids,
        lengths=image_lengths,
        gain1=row(ln1_gain),
        shift1=row(ln1_bias),
        w_qkv=w_qkv,
        bias_q=row(bias_query),
        bias_v=row(bias_value),
        w_out=w_out,
        bias_out=row(bias_out),
        gain2=row(ln2_gain),
        shift2=row(ln2_bias),
        w_router=w_router,
        w1=experts_in,
        b1=experts_in_bias,
        w2=experts_out,
        b2=experts_out_bias,
    )
    vmem, smem = pl.BlockSpec(memory_space=pltpu.VMEM), pl.BlockSpec(memory_space=pltpu.SMEM)
    anywhere = pl.BlockSpec(memory_space=pl.ANY)
    in_specs = {name: vmem for name in inputs}
    in_specs.update(lengths=smem, w1=anywhere, w2=anywhere)
    small_rows = 8 + experts
    outputs = dict(
        mixed=((rows, width), BF, anywhere),
        grad_tokens=((rows, width), F32, anywhere),
        big_out=((width, 4 * width), BF, anywhere),
        small_out=((small_rows, width), F32, vmem),
        d_layers=((2, local, group, width, part), BF, anywhere),
        d_bias=((local, group, 8, width), F32, anywhere),
    )
    half = width // 2
    scratch = dict(
        tile=((local, 8, width), F32),
        tiles=((places, 8, width), F32),
        first=((width, hidden), BF),
        second=((hidden, width), BF),
        bias1=((8, hidden), F32),
        held=((2, experts, -(-rows // 128) * 128), F32),
        table=((slots + 128, rows), BF),
        table_t=((rows, slots), BF),
        table0_t=((rows, slots), BF),
        send_a=((slots, width), BF),
        send_b=((slots, width), BF),
        cot_got=((slots, width), BF),
        x_got=((slots, width), BF),
        grad_got=((slots, width), BF),
        ret_got=((slots, width), BF),
        normed=((rows, width), BF),
        qkv=((rows, 3 * width), BF),
        attended=((rows, width), BF),
        residual=((rows, width), F32),
        expert_in=((rows, width), BF),
        probs=((rows, 128), F32),
        probs_t=((2 * experts, rows), BF),
        grad_ret=((slots, width), BF),
        hidden=((slots, hidden), BF),
        grad_pre=((slots, hidden), BF),
        sum_pre=((8, hidden), F32),
        sum_ret=((8, width), F32),
        d_experts=((2, width, hidden), BF),
        d_got=((2, width, hidden // 2), BF),
        d_tiles=((places, 8, width), F32),
        d_got_tiles=((places, 8, width), F32),
        inbox=((2, local, group, width, part), BF),
        inbox_tiles=((local, group, 8, width), F32),
        grad_two=((rows, width), F32),
        grad_choice=((rows, 128), F32),
        got_pair=((half, 4 * width), BF),
        got_plane=((places, half // places, 4 * width), BF),
        piece=((planes, half // places, 4 * width // planes), BF),
        got_z=((planes, half // places, 4 * width // planes), BF),
        whole=((width, 4 * width), BF),
        small=((small_rows, width), F32),
        s_pair=((small_rows, width), F32),
        s_plane=((places, small_rows, width), F32),
        s_z=((planes, small_rows, width), F32),
    )
    sem_sets = dict(
        weights_sem=Weights.sems(geo),
        cot_sem=swap_sems(geo),
        x_sem=swap_sems(geo),
        grad_sem=swap_sems(geo),
        ret_sem=swap_sems(geo),
        expert_sem=ExpertGrads.sems(geo),
        dense_sem=DenseSum.semaphores(geo)[1],
    )
    sem_names = [name + str(i) for name, found in sem_sets.items() for i in range(len(found))]
    sem_shapes = [s for found in sem_sets.values() for s in found]
    names = [*inputs, *outputs, *scratch, *sem_names, "out_sem"]
    sizes = (rows, per_micro, seq, capacity, block, width, hidden)
    results = pl.pallas_call(
        functools.partial(block_kernel, geo, sizes, names),
        out_shape=[jax.ShapeDtypeStruct(shape, dtype) for shape, dtype, _ in outputs.values()],
        in_specs=list(in_specs.values()),
        out_specs=[spec for _, _, spec in outputs.values()],
        scratch_shapes=[pltpu.VMEM(shape, dtype) for shape, dtype in scratch.values()]
        + sem_shapes
        + [pltpu.SemaphoreType.DMA((5,))],
        compiler_params=pltpu.CompilerParams(
            collective_id=0, has_side_effects=True, vmem_limit_bytes=VMEM_LIMIT
        ),
    )(*inputs.values())
    out = dict(zip(outputs, results, strict=True))
    big, small = out["big_out"], out["small_out"]
    layers = jnp.sum(out["d_layers"].astype(F32), axis=2)
    d_bias = jnp.sum(out["d_bias"], axis=1)
    return (
        out["mixed"].reshape(tokens.shape),
        out["grad_tokens"].reshape(tokens.shape),
        small[0],
        small[1],
        big[:, : 3 * width].astype(F32),
        small[2],
        small[3],
        big[:, 3 * width :].astype(F32),
        small[4],
        small[5],
        small[6],
        small[8:].T,
        layers[0],
        d_bias[:, 0, :part],
        jnp.swapaxes(layers[1], 1, 2),
        d_bias[:, 1, :],
    )


def solution(mesh):
    split = ("wide", "narrow")
    in_specs = (
        P(None, split, None),
        P(None, split),
        P(None, split, None),
        P(None, split, None),
        *([P()] * 10),
        P("wide", None, "narrow"),
        P("wide", "narrow"),
        P("wide", "narrow", None),
        P("wide", None),
    )
    out_specs = (
        P(None, split, None),
        P(None, split, None),
        *([P()] * 10),
        P("wide", None, "narrow"),
        P("wide", "narrow"),
        P("wide", "narrow", None),
        P("wide", None),
    )

    def step(*args):
        geo = Geometry(mesh.shape["wide"], mesh.shape["narrow"], args[14].shape[0])
        return on_device(geo, *args)

    return jax.shard_map(step, mesh=mesh, in_specs=in_specs, out_specs=out_specs, check_vma=False)
```

time: 835 us -> 220 us (0.26)
  waiting for transfers between devices: 306 us -> 0 us
  Pallas kernels: 0 us -> 189 us
  local copies, waits for them, and re-layouts: 160 us -> 21.1 us
  blocking collectives: 130 us -> 0 us
  matrix products: 115 us -> 0 us
  other arithmetic: 82.7 us -> 7.95 us
  starting transfers between devices: 19 us -> 0 us
  between operations: 15.7 us -> 0.69 us
    reduce_scatter x4 -> x0, waiting for transfers between devices: 194 us -> none  [the longest x2 110 us: on_device(): lax.psum_scatter(partial_out, 'narrow', scatter_dimension=1, tiled=True)]
    pallas_call x0 -> x1, Pallas kernels: none -> 189 us  [on_device(): pl.pallas_call(functools.partial(block_kernel, geo, sizes, names), out_sh...]
    dot_general x42 -> x0, matrix products: 115 us -> none  [the longest x2 18.4 us: on_device(): jnp.einsum('erd,edf->erf', expert_rows, layer_in, preferred_element_type=...]
    psum x1 -> x0, waiting for transfers between devices: 90.1 us -> none  [on_device(): lax.psum((acc_gain1, acc_shift1, acc_qkv, acc_query_bias, acc_value_bias,...]
    all_to_all x4 -> x0, blocking collectives: 88.5 us -> none  [the longest x2 46.2 us: on_device(): lax.all_to_all(grad_send, 'wide', split_axis=0, concat_axis=1, tiled=True)]
    psum x1 -> x0, blocking collectives: 41.3 us -> none  [on_device(): lax.psum((acc_gain1, acc_shift1, acc_qkv, acc_query_bias, acc_value_bias,...]
    convert_element_type x24 -> x0, local copies, waits for them, and re-layouts: 36.9 us -> none  [the longest x4 6.83 us: attend_forward(): attended.reshape(images * seq_len, HEADS * HEAD_DIM).astype(jnp.bfloat16)]
    reduce_sum x25 -> x0, other arithmetic: 29.7 us -> none  [the longest x2 9.05 us: on_device(): grad_gates = jnp.sum(cotangent[:, None, :] * picked, axis=-1)]
  transfers between devices with their start and end apart: 13 -> 0, of which waited for: 7 -> 0; matrix products, arithmetic and copies ran while one was open for 23% -> 0% of each run, Pallas kernels for 0% -> 0%
where the time goes in v1:
time: 220 us; the launch traced here: 218 us
  Pallas kernels  189 us (86%)
  local copies, waits for them, and re-layouts  21.1 us (10%)
  other arithmetic  7.95 us (4%)
    pallas_call x1, Pallas kernels, on_device(): pl.pallas_call(functools.partial(block_kernel, geo, sizes, names), out_sh...  189 us
    broadcast_in_dim x7, local copies, waits for them, and re-layouts, on_device(): row = lambda v: v[None, :]  8.81 us
    unnamed x14, local copies, waits for them, and re-layouts  6.57 us

profile of v1, /device:TPU:0, one launch (start us, length us, event | category | flops | bytes accessed | tf_op | source)
XLA Modules:
  0.0 218.5 jit_solution(4565428709986232989)
XLA Ops:
  0.6 0.8 copy.34
  1.5 0.0 copy-start
  1.5 0.7 copy.35.refs_2_
  2.2 1.5 copy.36.refs_14_
  3.7 1.3 broadcast_in_dim.21.refs_5_
  5.0 1.3 broadcast_in_dim.22.refs_6_
  6.2 1.3 broadcast_in_dim.23.refs_8_
  7.5 1.3 broadcast_in_dim.24.refs_9_
  8.8 1.3 broadcast_in_dim.25.refs_11_
  10.0 1.3 broadcast_in_dim.26.refs_12_
  11.3 1.3 broadcast_in_dim.27.refs_13_
  12.5 0.0 copy-done
  12.5 188.7 %shard_map.297 = (bf16[576,512]{1,0:T(8,128)(2,1)}, f32[576,512]{1,0:T(8,128)}, bf16[512,2048]{1,0:T(8,128)(2,1)}, f32[24,512]{1,0:T(8,128)}, bf16[2,2,1,512,512...) custom-call(bf16[576,512]{1,0:T(8,128)(2,1)} %bitcast.31, bf16[576,512]{1,0:T(8,128)(2,1)} %bitcast.32, ...), custom_call_target="tpu_custom_call" | custom-call | tf_op jit(solution)/shard_map/pallas_call | solution.py:1235
  201.3 0.8 fusion.1
  202.1 0.6 copy_bitcast_fusion
  202.7 1.6 fusion
  204.3 2.2 convert_element_type.11
  206.4 2.0 slice_bitcast_fusion
  208.4 1.8 copy.37
  210.2 0.0 copy-start.3
  210.2 0.0 copy-start.2
  210.2 3.5 %slice_convert_fusion = f32[512,1536]{1,0:T(8,128)} fusion(bf16[512,2048]{1,0:T(8,128)(2,1)} %get-tuple-element.25), kind=kLoop, calls=%fused_computation.2 | loop fusion | flops 786432 | bytes 4718592 | tf_op jit(solution)/shard_map/convert_element_type | solution.py:1256
  213.8 0.0 copy-start.1
  213.8 2.2 %slice_convert_fusion.1 = f32[512,512]{1,0:T(8,128)} fusion(bf16[512,2048]{1,0:T(8,128)(2,1)} %get-tuple-element.25), kind=kLoop, calls=%fused_computation.3 | loop fusion | flops 262144 | bytes 1572864 | tf_op jit(solution)/shard_map/convert_element_type | solution.py:1259
  216.0 0.0 copy-done.3
  216.0 0.6 slice_bitcast_fusion.2
  216.6 0.0 copy-done.2
  216.6 0.8 copy.44
  217.5 0.0 copy-done.1
  217.5 1.0 copy.45
Async XLA Ops:
  1.5 11.0 %copy-start = (s32[2,288,2]{2,1,0:T(8,128)}, s32[2,288,2]{2,1,0:T(8,128)S(1)}, u32[]{:S(2)}) copy-start(s32[2,288,2]{2,1,0:T(8,128)S(1)} %copy.34) | copy-start | bytes 13828
  210.2 5.8 %copy-start.3 = (f32[24,512]{1,0:T(8,128)S(1)}, f32[24,512]{1,0:T(8,128)}, u32[]{:S(2)}) copy-start(f32[24,512]{1,0:T(8,128)} %get-tuple-element.24) | copy-start | bytes 147460
  210.2 6.4 %copy-start.2 = (bf16[576,512]{1,0:T(8,128)(2,1)S(1)}, bf16[576,512]{1,0:T(8,128)(2,1)}, u32[]{:S(2)}) copy-start(bf16[576,512]{1,0:T(8,128)(2,1)} %get-tuple-element.22) | copy-start | bytes 1769476
  213.8 3.7 %copy-start.1 = (f32[576,512]{1,0:T(8,128)S(1)}, f32[576,512]{1,0:T(8,128)}, u32[]{:S(2)}) copy-start(f32[576,512]{1,0:T(8,128)} %get-tuple-element.23) | copy-start | bytes 3538948

commit v2 on v1

--- a/solution.py
+++ b/solution.py
@@ -13,7 +13,7 @@
 MESH = pl.DeviceIdType.MESH
 BF = jnp.bfloat16
 F32 = jnp.float32
-VMEM_LIMIT = 60 * 2**20
+VMEM_LIMIT = 62 * 2**20
 
 
 def dot(a, b):
@@ -139,16 +139,20 @@
 
 
 class Swap:
-    def __init__(self, geo, block, src, dst, sems):
+    def __init__(self, geo, block, src, dst, sems, first=0, count=None, base=0):
         self.geo, self.block, self.src, self.dst = geo, block, src, dst
+        self.first, self.count, self.base = first, count or block, base
         self.send_sem, self.recv_sem, self.local_sem = sems
 
-    def rows(self, ref, p):
-        return ref.at[pl.ds(pl.multiple_of(p * self.block, 16), self.block)]
+    def given(self, p):
+        return self.src.at[pl.ds(pl.multiple_of(p * self.block + self.first, 16), self.count)]
+
+    def kept(self, p):
+        return self.dst.at[pl.ds(pl.multiple_of(self.base + p * self.count, 16), self.count)]
 
     def local(self):
         mine = self.geo.mine()
-        return pltpu.make_async_copy(self.rows(self.src, mine), self.rows(self.dst, mine), self.local_sem)
+        return pltpu.make_async_copy(self.given(mine), self.kept(mine), self.local_sem)
 
     def send(self, p):
         mine = self.geo.mine()
@@ -160,8 +164,8 @@
         @pl.when(p != mine)
         def _():
             remote(
-                self.rows(self.src, p),
-                self.rows(self.dst, mine),
+                self.given(p),
+                self.kept(mine),
                 self.send_sem.at[p],
                 self.recv_sem.at[mine],
                 self.geo.partner(p),
@@ -169,8 +173,8 @@
 
     def copy(self, p):
         return remote(
-            self.rows(self.src, p),
-            self.rows(self.dst, p),
+            self.given(p),
+            self.kept(p),
             self.send_sem.at[p],
             self.recv_sem.at[p],
             self.geo.partner(p),
@@ -474,26 +478,59 @@
 
 
 class DenseSum:
-    def __init__(self, geo, mine, got_pair, got_plane, piece, got_z, whole, small, s_pair, s_plane, s_z, sems):
+    def __init__(
+        self,
+        geo,
+        mine,
+        got_pair,
+        got_plane,
+        piece,
+        got_z,
+        wide_z,
+        wide_sum,
+        wide_plane,
+        whole,
+        small,
+        s_pair,
+        s_plane,
+        s_z,
+        sems,
+        wide_chunk,
+    ):
         self.geo, self.mine, self.got_pair, self.got_plane = geo, mine, got_pair, got_plane
         self.piece, self.got_z, self.whole = piece, got_z, whole
+        self.wide_z, self.wide_sum, self.wide_plane = wide_z, wide_sum, wide_plane
+        self.wide_chunk = wide_chunk
         self.small, self.s_pair, self.s_plane, self.s_z = small, s_pair, s_plane, s_z
         self.sems = sems
         self.half = mine.shape[0] // 2
         self.rows = self.half // geo.places
-        self.columns = mine.shape[1] // geo.planes
+        self.columns = self.chunk_columns(geo)
+        self.part = self.columns // geo.planes
 
     @staticmethod
-    def semaphores(geo):
+    def chunk_columns(geo):
+        return 128 * geo.planes
+
+    @staticmethod
+    def semaphores(geo, chunks):
         dma = pltpu.SemaphoreType.DMA
-        places, planes, both = (geo.places,), (geo.planes,), (geo.places, geo.planes)
+        places, planes, both = (chunks, geo.places), (chunks, geo.planes), (chunks, geo.places)
         shapes = dict(
-            pair=(1,), plane=places, z=planes, zg=planes, pg=both, cg=both, sp=(1,), sn=places, sz=planes
+            pair=(chunks,),
+            plane=places,
+            z=planes,
+            zg=planes,
+            pg=both,
+            cg=both,
+            sp=(1,),
+            sn=(geo.places,),
+            sz=(geo.planes,),
         )
         return list(shapes), [dma(s) for s in shapes.values() for _ in range(2)]
 
     def sem(self, name):
-        names, _ = self.semaphores(self.geo)
+        names, _ = self.semaphores(self.geo, 1)
         i = names.index(name) * 2
         return self.sems[i], self.sems[i + 1]
 
@@ -501,128 +538,245 @@
         z, k, n = self.geo.here()
         return z, k, n, (z * 2 + 1 - k, n)
 
-    def half_rows(self, k):
-        return self.mine.at[pl.ds(pl.multiple_of(k * self.half, 16), self.half)]
-
-    def pair(self):
+    def others(self, here, count):
+        return [lax.rem(here + i, count) for i in range(1, count)]
+
+    def cols(self, c):
+        return pl.ds(c * self.columns, self.columns)
+
+    def place_rows(self, k, q):
+        return pl.ds(pl.multiple_of(k * self.half + q * self.rows, 16), self.rows)
+
+    def pair(self, c):
         z, k, n, sibling = self.where()
         send, recv = self.sem("pair")
-        return remote(self.half_rows(1 - k), self.got_pair, send.at[0], recv.at[0], sibling)
-
-    def place_rows(self, k, q):
-        return pl.ds(pl.multiple_of(k * self.half + q * self.rows, 16), self.rows)
-
-    def plane_copy(self, q):
+        away = pl.ds(pl.multiple_of((1 - k) * self.half, 16), self.half)
+        return remote(
+            self.mine.at[away, self.cols(c)], self.got_pair.at[c], send.at[c], recv.at[c], sibling
+        )
+
+    def plane_copy(self, c, q):
         z, k, n, _ = self.where()
         send, recv = self.sem("plane")
-        src = self.mine.at[self.place_rows(k, q)]
-        return remote(src, self.got_plane.at[n], send.at[q], recv.at[n], (z * 2 + k, q))
-
-    def plane_start(self):
+        src = self.mine.at[self.place_rows(k, q), self.cols(c)]
+        return remote(src, self.got_plane.at[c, n], send.at[c, q], recv.at[c, n], (z * 2 + k, q))
+
+    def plane_start(self, c):
         z, k, n, _ = self.where()
-        geo = self.geo
-        self.pair().wait()
-        keep = self.half_rows(k)
-        step = self.half // 4
-        for i in range(4):
-            there = pl.ds(pl.multiple_of(k * self.half + i * step, 16), step)
-            total = self.mine[there].astype(F32) + self.got_pair[i * step : (i + 1) * step].astype(F32)
-            self.mine[there] = total.astype(BF)
-        for i in range(1, geo.places):
-            self.plane_copy(lax.rem(n + i, geo.places)).start()
-        self.got_plane[n] = self.mine[self.place_rows(k, n)]
-
-    def z_copy(self, q):
+        self.pair(c).wait()
+        keep = pl.ds(pl.multiple_of(k * self.half, 16), self.half)
+        total = self.mine[keep, self.cols(c)].astype(F32) + self.got_pair[c].astype(F32)
+        self.mine[keep, self.cols(c)] = total.astype(BF)
+        for q in self.others(n, self.geo.places):
+            self.plane_copy(c, q).start()
+        self.got_plane[c, n] = self.mine[self.place_rows(k, n), self.cols(c)]
+
+    def z_copy(self, c, q):
         z, k, n, _ = self.where()
         send, recv = self.sem("z")
-        return remote(self.piece.at[q], self.got_z.at[z], send.at[q], recv.at[z], (q * 2 + k, n))
-
-    def z_start(self):
+        return remote(
+            self.piece.at[c, q], self.got_z.at[c, z], send.at[c, q], recv.at[c, z], (q * 2 + k, n)
+        )
+
+    def z_start(self, c):
         z, k, n, sibling = self.where()
-        geo = self.geo
         send, recv = self.sem("plane")
-        for i in range(1, geo.places):
-            q = lax.rem(n + i, geo.places)
-            spot = self.got_plane.at[q]
-            remote(spot, spot, send.at[q], recv.at[q], sibling).wait_recv()
-        for p in range(geo.planes):
-            cols = slice(p * self.columns, (p + 1) * self.columns)
-            total = self.got_plane[0, :, cols].astype(F32)
-            for i in range(1, geo.places):
-                total = total + self.got_plane[i, :, cols].astype(F32)
-            self.piece[p] = total.astype(BF)
-        for i in range(1, geo.planes):
-            self.z_copy(lax.rem(z + i, geo.planes)).start()
-        self.got_z[z] = self.piece[z]
-
-    def spot(self, k, q, p):
-        cols = pl.ds(pl.multiple_of(p * self.columns, 128), self.columns)
-        return self.whole.at[self.place_rows(k, q), cols]
-
-    def gather_copy(self, name, k, q, p, index, device):
-        send, recv = self.sem(name)
-        spot = self.spot(k, q, p)
-        return remote(spot, spot, send.at[index], recv.at[index], device)
-
-    def zg_copy(self, q):
+        for q in self.others(n, self.geo.places):
+            spot = self.got_plane.at[c, q]
+            remote(spot, spot, send.at[c, q], recv.at[c, q], sibling).wait_recv()
+        total = self.got_plane[c, 0].astype(F32)
+        for i in range(1, self.geo.places):
+            total = total + self.got_plane[c, i].astype(F32)
+        for p in range(self.geo.planes):
+            self.piece[c, p] = total[:, p * self.part : (p + 1) * self.part].astype(BF)
+        for q in self.others(z, self.geo.planes):
+            self.z_copy(c, q).start()
+        self.got_z[c, z] = self.piece[c, z]
+
+    def spot(self, c, p):
+        k, n = self.geo.here()[1:]
+        first = pl.multiple_of(c * self.columns + p * self.part, 128)
+        return self.whole.at[self.place_rows(k, n), pl.ds(first, self.part)]
+
+    def zg_copy(self, c, q):
         z, k, n, _ = self.where()
         send, recv = self.sem("zg")
-        spot = self.spot(k, n, z)
-        return remote(spot, spot, send.at[q], recv.at[z], (q * 2 + k, n))
-
-    def pg_copy(self, q, p):
+        spot = self.spot(c, z)
+        return remote(spot, spot, send.at[c, q], recv.at[c, z], (q * 2 + k, n))
+
+    def gather_z(self, c):
+        z, k, n, sibling = self.where()
+        send, recv = self.sem("z")
+        for q in self.others(z, self.geo.planes):
+            spot = self.got_z.at[c, q]
+            remote(spot, spot, send.at[c, q], recv.at[c, q], sibling).wait_recv()
+        total = self.got_z[c, 0].astype(F32)
+        for i in range(1, self.geo.planes):
+            total = total + self.got_z[c, i].astype(F32)
+        first = pl.multiple_of(c * self.columns + z * self.part, 128)
+        self.whole[self.place_rows(k, n), pl.ds(first, self.part)] = total.astype(BF)
+        for q in self.others(z, self.geo.planes):
+            self.zg_copy(c, q).start()
+
+    def row_spot(self, c, k, q):
+        return self.whole.at[self.place_rows(k, q), self.cols(c)]
+
+    def pg_copy(self, c, q):
         z, k, n, _ = self.where()
         send, recv = self.sem("pg")
-        spot = self.spot(k, n, p)
-        return remote(spot, spot, send.at[q, p], recv.at[n, p], (z * 2 + k, q))
-
-    def cg_copy(self, q, p):
+        spot = self.row_spot(c, k, n)
+        return remote(spot, spot, send.at[c, q], recv.at[c, n], (z * 2 + k, q))
+
+    def cg_copy(self, c, q):
         z, k, n, sibling = self.where()
         send, recv = self.sem("cg")
-        spot = self.spot(k, q, p)
-        return remote(spot, spot, send.at[q, p], recv.at[q, p], sibling)
-
-    def gather_start(self):
+        spot = self.row_spot(c, k, q)
+        return remote(spot, spot, send.at[c, q], recv.at[c, q], sibling)
+
+    def gather_plane(self, c):
         z, k, n, sibling = self.where()
-        geo = self.geo
+        send, recv = self.sem("zg")
+        for q in self.others(z, self.geo.planes):
+            spot = self.spot(c, q)
+            remote(spot, spot, send.at[c, q], recv.at[c, q], sibling).wait_recv()
+        for q in self.others(n, self.geo.places):
+            self.pg_copy(c, q).start()
+        self.cg_copy(c, n).start()
+
+    def gather_pair(self, c):
+        z, k, n, sibling = self.where()
+        send, recv = self.sem("pg")
+        for q in self.others(n, self.geo.places):
+            spot = self.row_spot(c, k, q)
+            remote(spot, spot, send.at[c, q], recv.at[c, q], sibling).wait_recv()
+            self.cg_copy(c, q).start()
+
+    def gather_end(self, c):
+        z, k, n, sibling = self.where()
+        send, recv = self.sem("cg")
+        for q in range(self.geo.places):
+            spot = self.row_spot(c, 1 - k, q)
+            remote(spot, spot, send.at[c, q], recv.at[c, q], sibling).wait_recv()
+
+
+    def half_part(self, p, c):
+        k = self.geo.here()[1]
+        first = pl.multiple_of(c * self.columns + p * self.part, 128)
+        return pl.ds(pl.multiple_of(k * self.half, 16), self.half), pl.ds(first, self.part)
+
+    def wide_z_copy(self, c, q):
+        z, k, n, _ = self.where()
         send, recv = self.sem("z")
-        for i in range(1, geo.planes):
-            q = lax.rem(z + i, geo.planes)
-            spot = self.got_z.at[q]
-            remote(spot, spot, send.at[q], recv.at[q], sibling).wait_recv()
-        total = self.got_z[0].astype(F32)
-        for i in range(1, geo.planes):
-            total = total + self.got_z[i].astype(F32)
-        cols = pl.ds(pl.multiple_of(z * self.columns, 128), self.columns)
-        self.whole[self.place_rows(k, n), cols] = total.astype(BF)
-        for i in range(1, geo.planes):
-            self.zg_copy(lax.rem(z + i, geo.planes)).start()
+        src = self.mine.at[self.half_part(q, c)]
+        return remote(src, self.wide_z.at[z], send.at[c, q], recv.at[c, z], (q * 2 + k, n))
+
+    def wide_z_start(self, c):
+        z, k, n, _ = self.where()
+        self.pair(c).wait()
+        keep = pl.ds(pl.multiple_of(k * self.half, 16), self.half)
+        total = self.mine[keep, self.cols(c)].astype(F32) + self.got_pair[c].astype(F32)
+        self.mine[keep, self.cols(c)] = total.astype(BF)
+        for q in self.others(z, self.geo.planes):
+            self.wide_z_copy(c, q).start()
+
+    def wide_plane_copy(self, c, q):
+        z, k, n, _ = self.where()
+        send, recv = self.sem("plane")
+        src = self.wide_sum.at[pl.ds(pl.multiple_of(q * self.rows, 16), self.rows)]
+        return remote(src, self.wide_plane.at[n], send.at[c, q], recv.at[c, n], (z * 2 + k, q))
+
+    def wide_plane_start(self, c):
+        z, k, n, sibling = self.where()
+        send, recv = self.sem("z")
+        total = self.mine[self.half_part(z, c)].astype(F32)
+        for q in self.others(z, self.geo.planes):
+            spot = self.wide_z.at[q]
+            remote(spot, spot, send.at[c, q], recv.at[c, q], sibling).wait_recv()
+            total = total + self.wide_z[q].astype(F32)
+        self.wide_sum[...] = total.astype(BF)
+        for q in self.others(n, self.geo.places):
+            self.wide_plane_copy(c, q).start()
+
+    def wide_gather_plane(self, c):
+        z, k, n, sibling = self.where()
+        send, recv = self.sem("plane")
+        here = pl.ds(pl.multiple_of(n * self.rows, 16), self.rows)
+        total = self.wide_sum[here].astype(F32)
+        for q in self.others(n, self.geo.places):
+            spot = self.wide_plane.at[q]
+            remote(spot, spot, send.at[c, q], recv.at[c, q], sibling).wait_recv()
+            total = total + self.wide_plane[q].astype(F32)
+        first = pl.multiple_of(c * self.columns + z * self.part, 128)
+        self.whole[self.place_rows(k, n), pl.ds(first, self.part)] = total.astype(BF)
+        for q in self.others(n, self.geo.places):
+            self.wide_pg_copy(c, q).start()
+
+    def wide_spot(self, c, q):
+        z, k, n, _ = self.where()
+        first = pl.multiple_of(c * self.columns + z * self.part, 128)
+        return self.whole.at[self.place_rows(k, q), pl.ds(first, self.part)]
+
+    def wide_pg_copy(self, c, q):
+        z, k, n, _ = self.where()
+        send, recv = self.sem("pg")
+        spot = self.wide_spot(c, n)
+        return remote(spot, spot, send.at[c, q], recv.at[c, n], (z * 2 + k, q))
+
+    def wide_zg_copy(self, c, q):
+        z, k, n, _ = self.where()
         send, recv = self.sem("zg")
-        for i in range(geo.planes):
-            p = lax.rem(z + i, geo.planes)
-            if i > 0:
-                spot = self.spot(k, n, p)
-                remote(spot, spot, send.at[p], recv.at[p], sibling).wait_recv()
-            for j in range(1, geo.places):
-                self.pg_copy(lax.rem(n + j, geo.places), p).start()
-            self.cg_copy(n, p).start()
-
-    def gather_finish(self):
+        spot = self.whole.at[self.half_part(z, c)]
+        return remote(spot, spot, send.at[c, q], recv.at[c, z], (q * 2 + k, n))
+
+    def wide_gather_z(self, c):
         z, k, n, sibling = self.where()
-        geo = self.geo
         send, recv = self.sem("pg")
-        for j in range(1, geo.places):
-            q = lax.rem(n + j, geo.places)
-            for i in range(geo.planes):
-                p = lax.rem(z + i, geo.planes)
-                spot = self.spot(k, q, p)
-                remote(spot, spot, send.at[q, p], recv.at[q, p], sibling).wait_recv()
-                self.cg_copy(q, p).start()
+        for q in self.others(n, self.geo.places):
+            spot = self.wide_spot(c, q)
+            remote(spot, spot, send.at[c, q], recv.at[c, q], sibling).wait_recv()
+        for q in self.others(z, self.geo.planes):
+            self.wide_zg_copy(c, q).start()
+
+    def wide_pair_copy(self, c):
+        z, k, n, sibling = self.where()
         send, recv = self.sem("cg")
-        for q in range(geo.places):
-            for p in range(geo.planes):
-                spot = self.spot(1 - k, q, p)
-                remote(spot, spot, send.at[q, p], recv.at[q, p], sibling).wait_recv()
+        half = pl.ds(pl.multiple_of(k * self.half, 16), self.half)
+        spot = self.whole.at[half, self.cols(c)]
+        return remote(spot, spot, send.at[c, 0], recv.at[c, 0], sibling)
+
+    def wide_gather_pair(self, c):
+        z, k, n, sibling = self.where()
+        send, recv = self.sem("zg")
+        for q in self.others(z, self.geo.planes):
+            spot = self.whole.at[self.half_part(q, c)]
+            remote(spot, spot, send.at[c, q], recv.at[c, q], sibling).wait_recv()
+        self.wide_pair_copy(c).start()
+
+    def wide_gather_end(self, c):
+        z, k, n, sibling = self.where()
+        send, recv = self.sem("cg")
+        half = pl.ds(pl.multiple_of((1 - k) * self.half, 16), self.half)
+        spot = self.whole.at[half, self.cols(c)]
+        remote(spot, spot, send.at[c, 0], recv.at[c, 0], sibling).wait_recv()
+
+    def stages(self, c):
+        if c == self.wide_chunk:
+            return (
+                self.wide_z_start,
+                self.wide_plane_start,
+                self.wide_gather_plane,
+                self.wide_gather_z,
+                self.wide_gather_pair,
+                self.wide_gather_end,
+            )
+        return (
+            self.plane_start,
+            self.z_start,
+            self.gather_z,
+            self.gather_plane,
+            self.gather_pair,
+            self.gather_end,
+        )
 
     def small_pair(self):
         send, recv = self.sem("sp")
@@ -673,23 +827,30 @@
             total = total + self.s_z[i]
         out[...] = total
 
-    def wait_sent(self):
+    def wait_sent(self, chunks):
         z, k, n, _ = self.where()
-        geo = self.geo
-        for i in range(1, geo.places):
-            q = lax.rem(n + i, geo.places)
-            self.plane_copy(q).wait_send()
+        for q in self.others(n, self.geo.places):
             self.sn_copy(q).wait_send()
-            for p in range(geo.planes):
-                self.pg_copy(q, p).wait_send()
-        for i in range(1, geo.planes):
-            q = lax.rem(z + i, geo.planes)
-            self.z_copy(q).wait_send()
-            self.zg_copy(q).wait_send()
+        for q in self.others(z, self.geo.planes):
             self.sz_copy(q).wait_send()
-        for q in range(geo.places):
-            for p in range(geo.planes):
-                self.cg_copy(q, p).wait_send()
+        for c in range(chunks):
+            if c == self.wide_chunk:
+                for q in self.others(n, self.geo.places):
+                    self.wide_plane_copy(c, q).wait_send()
+                    self.wide_pg_copy(c, q).wait_send()
+                for q in self.others(z, self.geo.planes):
+                    self.wide_z_copy(c, q).wait_send()
+                    self.wide_zg_copy(c, q).wait_send()
+                self.wide_pair_copy(c).wait_send()
+                continue
+            for q in self.others(n, self.geo.places):
+                self.plane_copy(c, q).wait_send()
+                self.pg_copy(c, q).wait_send()
+            for q in self.others(z, self.geo.planes):
+                self.z_copy(c, q).wait_send()
+                self.zg_copy(c, q).wait_send()
+            for q in range(self.geo.places):
+                self.cg_copy(c, q).wait_send()
 
 
 def greet_start(devices):
@@ -708,6 +869,10 @@
     return found
 
 
+def vector(ref, cols=slice(None)):
+    return ref[...].astype(F32)[None, :][:, cols]
+
+
 def lane_row(row, count):
     shape = (count, row.shape[1])
     diagonal = lax.broadcasted_iota(jnp.int32, shape, 0) == lax.broadcasted_iota(jnp.int32, shape, 1)
@@ -720,9 +885,9 @@
     return jnp.sum(jnp.where(diagonal, column, 0.0), axis=0, keepdims=True)
 
 
-def put_pair(tail, high, low):
-    row = lax.broadcasted_iota(jnp.int32, tail.shape, 0)
-    return jnp.where(row == 14, high, jnp.where(row == 15, low, tail))
+def put_pair(rows, line, high, low):
+    row = lax.broadcasted_iota(jnp.int32, rows.shape, 0)
+    return jnp.where(row == line, high, jnp.where(row == line + 1, low, rows))
 
 
 def block_kernel(geo, sizes, names, *refs):
@@ -744,7 +909,12 @@
     r.logits_high = r.grad_pre.at[0:rows, 4 * width - 256 : 4 * width - 128]
     r.logits_low = r.grad_pre.at[0:rows, 4 * width - 128 : 4 * width]
     lanes = -(-rows // 128) * 128
-    r.table0 = r.grad_pre.at[:, 0:lanes]
+    r.late_table = r.grad_pre.at[:, 0:lanes]
+    r.late_table0 = r.grad_pre.at[:, lanes : 2 * lanes]
+    head = -(-(capacity + 2) // 16) * 16
+    rest = block - head
+    heads = experts * head
+    gate_group, gate_line = capacity // 16 * 16, capacity % 16
     r.slot_grad = r.grad_pre.at[:, 3 * width : 3 * width + 256]
 
     def span(i, count, align=16):
@@ -754,21 +924,38 @@
         return [ref for key, ref in zip(names, refs, strict=True) if key.startswith(name)]
 
     greet_start(all_devices(geo))
-    for i in range(geo.local_experts):
-        r.tile[i] = jnp.zeros((8, width), F32)
-        r.tile[i, 0:1, 0:part] = r.b1[i : i + 1, :].astype(F32)
-        r.tile[i, 1:2, :] = r.b2[i : i + 1, :].astype(F32)
+    arrive = [
+        pltpu.make_async_copy(src, dst, r.in_sem.at[i])
+        for i, (src, dst) in enumerate(
+            (
+                (r.given_cot, r.cot),
+                (r.given_tokens, r.tokens),
+                (r.given_w_qkv, r.w_qkv),
+                (r.given_w_out, r.w_out),
+            )
+        )
+    ]
+    for copy in arrive:
+        copy.start()
     weights = Weights(
         geo, (r.w1, r.w2), (r.first, r.second), r.tile, r.tiles, sems("weights_sem")
     )
     cot_swap = Swap(geo, block, r.send_a, r.cot_got, sems("cot_sem"))
     x_swap = Swap(geo, block, r.send_b, r.x_got, sems("x_sem"))
-    grad_swap = Swap(geo, block, r.send_a, r.grad_got, sems("grad_sem"))
-    ret_swap = Swap(geo, block, r.send_b, r.ret_got, sems("ret_sem"))
-
-    choices = r.choices[...]
-    ids = lax.broadcasted_iota(jnp.int32, (experts, rows), 0)
-    named = [ids == choices[i : i + 1, :] for i in range(2)]
+    grad_swap, late_grad_swap = (
+        Swap(geo, block, r.send_a, r.grad_got, sems("head_grad_sem"), 0, head, 0),
+        Swap(geo, block, r.send_a, r.grad_got, sems("rest_grad_sem"), head, rest, heads),
+    )
+    ret_swap, late_ret_swap = (
+        Swap(geo, block, r.send_b, r.ret_got, sems("head_ret_sem"), 0, head, 0),
+        Swap(geo, block, r.send_b, r.ret_got, sems("rest_ret_sem"), head, rest, heads),
+    )
+
+    r.ids[...] = jnp.zeros(r.ids.shape, F32)
+    for m in range(rows // per_micro):
+        r.ids[0:2, m * per_micro : (m + 1) * per_micro] = r.choices[m].astype(F32)
+    lines = lax.broadcasted_iota(jnp.int32, (experts, rows), 0).astype(F32)
+    named = [lines == r.ids[i : i + 1, 0:rows] for i in range(2)]
     either = jnp.logical_or(named[0], named[1])
     first_row = lax.broadcasted_iota(jnp.int32, (rows, rows), 0)
     second_row = lax.broadcasted_iota(jnp.int32, (rows, rows), 1)
@@ -776,48 +963,60 @@
     earlier = jnp.logical_and(first_row < second_row, same)
     before = dot(either.astype(F32).astype(BF), earlier.astype(F32).astype(BF))
     late = lax.broadcasted_iota(jnp.int32, (experts, rows), 1) >= per_micro
-    slot = before + jnp.where(late, float(capacity), 0.0)
+    slot = before + jnp.where(late, float(capacity + 2), 0.0)
     r.held[...] = jnp.full(r.held.shape, -1.0, F32)
     r.held[0, :, 0:rows] = jnp.where(either, slot, -1.0)
     r.held[1, :, 0:rows] = jnp.where(named[0], slot, -1.0)
     spots = lax.broadcasted_iota(jnp.int32, (block, lanes), 0).astype(F32)
 
     def fill(e):
-        here = span(e, block)
-        either, chosen = [
-            jnp.where(spots == r.held[i, pl.ds(e, 1), :], 1.0, 0.0).astype(BF) for i in range(2)
-        ]
-        r.table[here, :] = either[:, 0:rows]
-        r.table0[here, :] = chosen
-
-    each(experts, fill)
-    r.table[pl.ds(slots, 128), :] = jnp.zeros((128, rows), BF)
-
-    pl.semaphore_wait(pltpu.get_barrier_semaphore(), len(all_devices(geo)))
-    weights.start()
+        either = jnp.where(spots == r.held[0, pl.ds(e, 1), :], 1.0, 0.0).astype(BF)
+        r.table[span(e, block), :] = either[:, 0:rows]
+
+    def late_fill(e):
+        for i, table in enumerate((r.late_table, r.late_table0)):
+            found = jnp.where(spots == r.held[i, pl.ds(e, 1), :], 1.0, 0.0).astype(BF)
+            table[span(e, head), :] = found[0:head]
+            table[pl.ds(pl.multiple_of(heads + e * rest, 16), rest), :] = found[head:]
 
     def send_cot(i):
         plane = lax.rem(z + 1 + i, geo.planes)
+        for j in range(quad):
+            fill(plane * quad + j)
+
+        @pl.when(i == 0)
+        def _():
+            arrive[0].wait()
+            pl.semaphore_wait(pltpu.get_barrier_semaphore(), len(all_devices(geo)))
+
         blocks = dot(r.table[span(plane, chunk), :], r.cot[...])
         r.send_a[span(plane, chunk), :] = blocks.astype(BF)
         for j in range(quad):
             cot_swap.send(plane * quad + j)
 
     each(geo.planes, send_cot)
+    r.table[pl.ds(slots, 128), :] = jnp.zeros((128, rows), BF)
+    for i in range(geo.local_experts):
+        r.tile[i] = jnp.zeros((8, width), F32)
+        r.tile[i, 0:1, 0:part] = r.b1[i : i + 1, :].astype(F32)
+        r.tile[i, 1:2, :] = r.b2[i : i + 1, :].astype(F32)
+    weights.start()
 
     def norm_in(i):
         unit, _ = norm_parts(r.tokens[span(i, seq), :].astype(F32))
-        normed = unit * r.gain1[...].astype(F32) + r.shift1[...].astype(F32)
+        normed = unit * vector(r.gain1) + vector(r.shift1)
         r.normed[span(i, seq), :] = normed.astype(BF)
 
+    arrive[1].wait()
     each(images, norm_in)
+    arrive[2].wait()
     for c in range(3 * width // tile):
         cols = slice(c * tile, (c + 1) * tile)
         out = dot(r.normed[...], r.w_qkv[:, cols])
         if c * tile < width:
-            out = out + r.bias_q[:, cols].astype(F32)
+            out = out + vector(r.bias_q, cols)
         elif c * tile >= 2 * width:
-            out = out + r.bias_v[:, c * tile - 2 * width : (c + 1) * tile - 2 * width].astype(F32)
+            out = out + vector(r.bias_v, slice(c * tile - 2 * width, (c + 1) * tile - 2 * width))
         r.qkv[:, cols] = out.astype(BF)
 
     def attend(i):
@@ -837,18 +1036,19 @@
         residual = (
             r.tokens[here, :].astype(F32)
             + dot(r.attended[here, :], r.w_out[...])
-            + r.bias_out[...].astype(F32)
+            + vector(r.bias_out)
         )
         r.residual[here, :] = residual
         unit, _ = norm_parts(residual)
-        expert_in = (unit * r.gain2[...].astype(F32) + r.shift2[...].astype(F32)).astype(BF)
+        expert_in = (unit * vector(r.gain2) + vector(r.shift2)).astype(BF)
         r.expert_in[here, :] = expert_in
-        logits = dot(expert_in, r.w_router[...])
+        logits = dot_nt(expert_in, r.w_router[...])
         raised = jnp.exp(logits - jnp.max(logits, axis=-1, keepdims=True))
         probs = raised / jnp.sum(raised, axis=-1, keepdims=True)
         r.probs[here, 0:experts] = probs
 
     r.probs[...] = jnp.zeros(r.probs.shape, F32)
+    arrive[3].wait()
     each(images, branch)
     probs_t = jnp.transpose(r.probs[...])[0:experts, :]
     high, low = split_two(probs_t)
@@ -867,14 +1067,16 @@
             high = jnp.sum(jnp.where(line == e, gates, 0.0), axis=0, keepdims=True)
             low = jnp.sum(jnp.where(line == experts + e, gates, 0.0), axis=0, keepdims=True)
             r.send_b[span(e, block), :] = values.astype(BF)
-            tail = put_pair(values[block - 16 :, 0:128], high, low)
-            r.send_b[pl.ds(pl.multiple_of(at + block - 16, 16), 16), 0:128] = tail.astype(BF)
+            group = put_pair(values[gate_group : gate_group + 16, 0:128], gate_line, high, low)
+            r.send_b[pl.ds(pl.multiple_of(at + gate_group, 16), 16), 0:128] = group.astype(BF)
             x_swap.send(e)
 
     each(geo.planes, send_x)
 
-    r.table_t[...] = jnp.transpose(r.table[0:slots, :])
-    r.table0_t[...] = jnp.transpose(r.table0[...])[0:rows, :]
+    r.ids_t[...] = jnp.transpose(r.ids[...])
+    each(experts, late_fill)
+    r.table_t[...] = jnp.transpose(r.late_table[...])[0:rows, :]
+    r.table0_t[...] = jnp.transpose(r.late_table0[...])[0:rows, :]
     weights.relay()
     weights.finish()
     for s in range(geo.places):
@@ -895,8 +1097,8 @@
             x_swap.wait_got(plane * quad + j)
         for j in range(quad):
             at = (plane * quad + j) * block
-            tail = r.x_got[pl.ds(pl.multiple_of(at + block - 16, 16), 16), 0:128].astype(F32)
-            gate = lane_row(tail[14:15] + tail[15:16], block)
+            group = r.x_got[pl.ds(pl.multiple_of(at + gate_group, 16), 16), 0:128].astype(F32)
+            gate = lane_row(group[gate_line : gate_line + 1] + group[gate_line + 1 : gate_line + 2], block)
             there = span(plane * quad + j, block)
             r.grad_ret[there, :] = (gate * r.cot_got[there, :].astype(F32)).astype(BF)
         total_ret = jnp.sum(r.grad_ret[here, :].astype(F32), axis=0, keepdims=True)
@@ -924,13 +1126,15 @@
             high, low = split_two(row_of(jnp.sum(product, axis=-1, keepdims=True), 128))
             values = grad_in[j * block : (j + 1) * block]
             r.send_a[there, :] = values.astype(BF)
-            tail = put_pair(values[block - 16 :, 0:128], high.astype(F32), low.astype(F32))
-            at = pl.ds(pl.multiple_of(e * block + block - 16, 16), 16)
-            r.send_a[at, 0:128] = tail.astype(BF)
+            group = values[gate_group : gate_group + 16, 0:128]
+            group = put_pair(group, gate_line, high.astype(F32), low.astype(F32))
+            at = pl.ds(pl.multiple_of(e * block + gate_group, 16), 16)
+            r.send_a[at, 0:128] = group.astype(BF)
             grad_swap.send(e)
 
     each(geo.planes, expert_chunk)
-    each(experts, lambda i: ret_swap.send(lax.rem(geo.mine() + 1 + i, experts)))
+    for swap in (late_grad_swap, ret_swap, late_ret_swap):
+        each(experts, lambda i: swap.send(lax.rem(geo.mine() + 1 + i, experts)))
 
     grads = ExpertGrads(
         geo,
@@ -968,30 +1172,39 @@
         r.got_plane,
         r.piece,
         r.got_z,
+        r.wide_z,
+        r.wide_sum,
+        r.wide_plane,
         r.whole,
         r.small,
         r.s_pair,
         r.s_plane,
         r.s_z,
         sems("dense_sem"),
+        4 * width // (128 * geo.planes) - (2 if 128 * geo.planes == width else 1),
     )
 
     def slot_grads(e):
         grad_swap.wait_got(e)
-        at = pl.ds(pl.multiple_of(e * block + block - 16, 16), 16)
-        tail = r.grad_got[at, 0:128].astype(F32)
-        column = lane_row(tail[14:15] + tail[15:16], block)
+        at = pl.ds(pl.multiple_of(e * head + gate_group, 16), 16)
+        group = r.grad_got[at, 0:128].astype(F32)
+        column = lane_row(group[gate_line : gate_line + 1] + group[gate_line + 1 : gate_line + 2], block)
         lane = lax.broadcasted_iota(jnp.int32, (block, 128), 1)
-        high, low = split_two(jnp.where(lane == e, column, 0.0))
-        r.slot_grad[span(e, block), 0:128] = high
-        r.slot_grad[span(e, block), 128:256] = low
-
-    each(experts, slot_grads)
-    for c in range(width // tile):
-        cols = slice(c * tile, (c + 1) * tile)
-        r.grad_two[:, cols] = dot(r.table_t[...], r.grad_got[:, cols])
-    both = dot(r.table_t[...], r.slot_grad[...])
-    r.grad_choice[...] = both[:, 0:128] + both[:, 128:256]
+        late = pl.ds(pl.multiple_of(heads + e * rest, 16), rest)
+        for i, value in enumerate(split_two(jnp.where(lane == e, column, 0.0))):
+            cols = slice(i * 128, (i + 1) * 128)
+            r.slot_grad[span(e, head), cols] = value[0:head]
+            r.slot_grad[late, cols] = value[head:]
+
+    def combine(m):
+        here = slice(m * per_micro, (m + 1) * per_micro)
+        there = slice(0, heads if m == 0 else slots)
+        for c in range(width // tile):
+            cols = slice(c * tile, (c + 1) * tile)
+            r.grad_two[here, cols] = dot(r.table_t[here, there], r.grad_got[there, cols])
+        both = dot(r.table_t[here, there], r.slot_grad[there, :])
+        r.grad_choice[here, :] = both[:, 0:128] + both[:, 128:256]
+
     r.small[...] = jnp.zeros(r.small.shape, F32)
 
     def add_small(row, value):
@@ -1007,26 +1220,35 @@
         r.logits_low[here, :] = low
         weight = r.w_router[...]
         grad = r.grad_two[here, :]
-        grad = grad + dot_nt(high[:, 0:experts], weight) + dot_nt(low[:, 0:experts], weight)
+        grad = grad + dot(high[:, 0:experts], weight) + dot(low[:, 0:experts], weight)
         unit, scale = norm_parts(r.residual[here, :])
         add_small(5, grad * unit)
         add_small(6, grad)
-        grad = r.cot[here, :].astype(F32) + norm_back(grad, unit, scale, r.gain2[...].astype(F32))
+        grad = r.cot[here, :].astype(F32) + norm_back(grad, unit, scale, vector(r.gain2))
         r.grad_two[here, :] = grad
         low_grad = grad.astype(BF)
         r.grad_branch[here, :] = low_grad
         add_small(4, low_grad.astype(F32))
 
-    each(images, norm_two_back)
-    for c in range(width // tile):
-        cols = slice(c * tile, (c + 1) * tile)
-        r.grad_att[:, cols] = dot_nt(r.grad_branch[...], r.w_out[cols, :]).astype(BF)
-        out = dot_tn(r.attended[...], r.grad_branch[:, cols])
-        r.mine[:, 3 * width + c * tile : 3 * width + (c + 1) * tile] = out.astype(BF)
-    router = dot_tn(r.logits_high[...], r.expert_in[...]) + dot_tn(
-        r.logits_low[...], r.expert_in[...]
-    )
-    r.small[8 : 8 + experts, :] = router[0:experts, :]
+    columns = dense.columns
+    chunks = 4 * width // columns
+    stages = dense.stages(chunks - 1)
+
+    def dense_grad(first):
+        cols = pl.ds(first, tile)
+        if first < 3 * width:
+            out = dot_tn(r.normed[...], r.grad_qkv[:, cols])
+        else:
+            out = dot_tn(r.attended[...], r.grad_branch[:, pl.ds(first - 3 * width, tile)])
+        r.mine[:, cols] = out.astype(BF)
+
+    early = columns == width
+
+    def attend_grad(m):
+        here = slice(m * per_micro, (m + 1) * per_micro)
+        for c in range(width // tile):
+            cols = slice(c * tile, (c + 1) * tile)
+            r.grad_att[here, cols] = dot_nt(r.grad_branch[here, :], r.w_out[cols, :]).astype(BF)
 
     def attend_back(i):
         here = span(i, seq)
@@ -1043,12 +1265,6 @@
         add_small(2, parts[0].astype(F32))
         add_small(3, parts[2].astype(F32))
 
-    each(images, attend_back)
-    for c in range(3 * width // tile):
-        cols = slice(c * tile, (c + 1) * tile)
-        r.mine[:, cols] = dot_tn(r.normed[...], r.grad_qkv[:, cols]).astype(BF)
-    dense.pair().start()
-
     def norm_one_back(i):
         here = span(i, seq)
         grad = dot_nt(r.grad_qkv[here, :], r.w_qkv[...])
@@ -1056,52 +1272,139 @@
         add_small(0, grad * unit)
         add_small(1, grad)
         r.grad_two[here, :] = r.grad_two[here, :] + norm_back(
-            grad, unit, scale, r.gain1[...].astype(F32)
+            grad, unit, scale, vector(r.gain1)
         )
-
-    each(images, norm_one_back)
-    dense.small_pair().start()
-    tokens_copy = pltpu.make_async_copy(r.grad_two, r.grad_tokens, r.out_sem.at[1])
-    tokens_copy.start()
-    dense.plane_start()
-    dense.small_plane()
-
-    each(experts, ret_swap.wait_got)
 
     def mix(i):
         here = span(i, seq)
         total = dot(r.table_t[here, :], r.ret_got[...])
         chosen = dot(r.table0_t[here, :], r.ret_got[...])
         probs = r.probs[here, :]
-        lane = lax.broadcasted_iota(jnp.int32, probs.shape, 1)
+        lane = lax.broadcasted_iota(jnp.int32, probs.shape, 1).astype(F32)
         gates = [
-            jnp.sum(jnp.where(lane == r.ids[here, j : j + 1], probs, 0.0), axis=-1, keepdims=True)
+            jnp.sum(jnp.where(lane == r.ids_t[here, j : j + 1], probs, 0.0), axis=-1, keepdims=True)
             for j in range(2)
         ]
         mixed = r.residual[here, :] + gates[0] * chosen + gates[1] * (total - chosen)
         r.expert_in[here, :] = mixed.astype(BF)
 
-    each(images, mix)
+    def some(step, m):
+        count = images * per_micro // rows
+        each(count, lambda i: step(m * count + i))
+
+    micros = rows // per_micro
+    each(experts, slot_grads)
+    for m in range(micros):
+        if m == 1:
+            each(experts, late_grad_swap.wait_got)
+        combine(m)
+        some(norm_two_back, m)
+        if m == micros - 1 and early:
+            for first in range(3 * width, 4 * width, tile):
+                dense_grad(first)
+            dense.pair(chunks - 1).start()
+        attend_grad(m)
+        if m == micros - 1 and early:
+            stages[0](chunks - 1)
+        some(attend_back, m)
+        if m < micros - 1:
+            some(norm_one_back, m)
+    router = dot_tn(r.logits_high[...], r.expert_in[...]) + dot_tn(r.logits_low[...], r.expert_in[...])
+    r.small[8 : 8 + experts, :] = router[0:experts, :]
+    late = chunks - 1 if early else chunks
+    done = 1 if early else 0
+    tokens_copy = pltpu.make_async_copy(r.grad_two, r.grad_tokens, r.out_sem.at[1])
     mixed_copy = pltpu.make_async_copy(r.expert_in, r.mixed, r.out_sem.at[0])
-    mixed_copy.start()
-    dense.small_z()
-    dense.z_start()
-    grads.wait_got()
     layers_copy = pltpu.make_async_copy(r.inbox, r.d_layers, r.out_sem.at[2])
     bias_copy = pltpu.make_async_copy(r.inbox_tiles, r.d_bias, r.out_sem.at[3])
-    layers_copy.start()
-    bias_copy.start()
-    dense.gather_start()
-    dense.small_finish(r.small_out)
-    dense.gather_finish()
+
+    def tokens_done():
+        tokens_copy.start()
+        dense.small_pair().start()
+
+    def owner_done():
+        grads.wait_got()
+        layers_copy.start()
+        bias_copy.start()
+
+    beside = [functools.partial(norm_one_back, i) for i in range((micros - 1) * images // micros, images)]
+    beside += [tokens_done, dense.small_plane, dense.small_z]
+    beside += [lambda: each(experts, ret_swap.wait_got), lambda: each(experts, late_ret_swap.wait_got)]
+    beside += [functools.partial(mix, i) for i in range(images)]
+    beside += [mixed_copy.start, lambda: dense.small_finish(r.small_out), owner_done]
+    for c in range(late):
+        for first in range(c * columns, (c + 1) * columns, tile):
+            dense_grad(first)
+        dense.pair(c).start()
+    for stage in range(len(stages)):
+        for c in range(late):
+            dense.stages(c)[stage](c)
+        if early and done + stage < len(stages):
+            stages[done + stage](chunks - 1)
+        for step in beside[:4]:
+            step()
+        beside = beside[4:]
+    for step in beside:
+        step()
     big_copy = pltpu.make_async_copy(r.whole, r.big_out, r.out_sem.at[4])
     big_copy.start()
-    grad_swap.wait_sent()
-    ret_swap.wait_sent()
+    for swap in (grad_swap, late_grad_swap, ret_swap, late_ret_swap):
+        swap.wait_sent()
     weights.wait_sent()
     grads.wait_sent()
-    dense.wait_sent()
+    dense.wait_sent(chunks)
     for copy in (mixed_copy, tokens_copy, layers_copy, bias_copy, big_copy):
+        copy.wait()
+
+
+def finish_kernel(names, *refs):
+    r = SimpleNamespace(**dict(zip(names, refs, strict=True)))
+    width, part = r.w_out.shape[0], r.w1.shape[2]
+    local, group = r.g_d_layers.shape[1:3]
+    come_big = pltpu.make_async_copy(r.g_big_out, r.v_big, r.sem.at[0])
+    come_layers = pltpu.make_async_copy(r.g_d_layers, r.v_layers, r.sem.at[1])
+    come_tokens = pltpu.make_async_copy(r.g_grad_tokens, r.v_tokens, r.sem.at[2])
+    come_mixed = pltpu.make_async_copy(r.g_mixed, r.v_mixed, r.sem.at[3])
+    copies = []
+    for copy in (come_big, come_layers, come_tokens, come_mixed):
+        copy.start()
+    vectors = dict(gain1=0, shift1=1, bias_q=2, bias_v=3, bias_out=4, gain2=5, shift2=6)
+    for name, line in vectors.items():
+        getattr(r, name)[...] = r.g_small_out[line]
+    r.router[...] = r.g_small_out[8:, :]
+    tiles = r.g_d_bias[:, 0]
+    for g in range(1, group):
+        tiles = tiles + r.g_d_bias[:, g]
+    r.b1[...] = tiles[:, 0, 0:part]
+    r.b2[...] = tiles[:, 1, :]
+
+    def leave(src, dst, sem):
+        copy = pltpu.make_async_copy(src, dst, sem)
+        copy.start()
+        copies.append(copy)
+
+    come_big.wait()
+    for i, (out, first) in enumerate(((r.w_qkv, 0), (r.w_out, 3 * width))):
+        cols = slice(first, first + out.shape[1])
+        r.o_big[:, cols] = r.v_big[:, cols].astype(F32)
+        leave(r.o_big.at[:, cols], out, r.sem.at[4 + i])
+    come_tokens.wait()
+    leave(r.v_tokens, r.grad_tokens, r.sem.at[2])
+    come_mixed.wait()
+    leave(r.v_mixed, r.mixed, r.sem.at[3])
+    come_layers.wait()
+    for i in range(local):
+        for layer in range(2):
+            total = r.v_layers[layer, i, 0].astype(F32)
+            for g in range(1, group):
+                total = total + r.v_layers[layer, i, g].astype(F32)
+            if layer == 0:
+                r.o_first[i] = total
+                leave(r.o_first.at[i], r.w1.at[i], r.sem.at[6 + 2 * i])
+            else:
+                r.o_second[i] = jnp.transpose(total)
+                leave(r.o_second.at[i], r.w2.at[i], r.sem.at[7 + 2 * i])
+    for copy in copies:
         copy.wait()
 
 
@@ -1136,24 +1439,21 @@
     part = experts_in.shape[2]
     hidden = part * geo.places
     places, planes, local, group = geo.places, geo.planes, geo.local_experts, geo.group
-    flat_ids = expert_index.reshape(rows, 2)
-    row = lambda v: v[None, :]
     inputs = dict(
-        tokens=tokens.reshape(rows, width),
-        cot=grad_out.reshape(rows, width),
-        choices=flat_ids.T,
-        ids=flat_ids,
+        given_tokens=tokens.reshape(rows, width),
+        given_cot=grad_out.reshape(rows, width),
+        choices=jnp.swapaxes(expert_index, 1, 2),
         lengths=image_lengths,
-        gain1=row(ln1_gain),
-        shift1=row(ln1_bias),
-        w_qkv=w_qkv,
-        bias_q=row(bias_query),
-        bias_v=row(bias_value),
-        w_out=w_out,
-        bias_out=row(bias_out),
-        gain2=row(ln2_gain),
-        shift2=row(ln2_bias),
-        w_router=w_router,
+        gain1=ln1_gain,
+        shift1=ln1_bias,
+        given_w_qkv=w_qkv,
+        bias_q=bias_query,
+        bias_v=bias_value,
+        given_w_out=w_out,
+        bias_out=bias_out,
+        gain2=ln2_gain,
+        shift2=ln2_bias,
+        w_router=w_router.T,
         w1=experts_in,
         b1=experts_in_bias,
         w2=experts_out,
@@ -1163,6 +1463,7 @@
     anywhere = pl.BlockSpec(memory_space=pl.ANY)
     in_specs = {name: vmem for name in inputs}
     in_specs.update(lengths=smem, w1=anywhere, w2=anywhere)
+    in_specs.update({name: anywhere for name in inputs if name.startswith("given")})
     small_rows = 8 + experts
     outputs = dict(
         mixed=((rows, width), BF, anywhere),
@@ -1173,12 +1474,20 @@
         d_bias=((local, group, 8, width), F32, anywhere),
     )
     half = width // 2
+    columns = DenseSum.chunk_columns(geo)
+    chunks = 4 * width // columns
     scratch = dict(
+        tokens=((rows, width), BF),
+        cot=((rows, width), BF),
+        w_qkv=((width, 3 * width), BF),
+        w_out=((width, width), BF),
         tile=((local, 8, width), F32),
         tiles=((places, 8, width), F32),
         first=((width, hidden), BF),
         second=((hidden, width), BF),
         bias1=((8, hidden), F32),
+        ids=((8, -(-rows // 128) * 128), F32),
+        ids_t=((-(-rows // 128) * 128, 8), F32),
         held=((2, experts, -(-rows // 128) * 128), F32),
         table=((slots + 128, rows), BF),
         table_t=((rows, slots), BF),
@@ -1209,10 +1518,13 @@
         inbox_tiles=((local, group, 8, width), F32),
         grad_two=((rows, width), F32),
         grad_choice=((rows, 128), F32),
-        got_pair=((half, 4 * width), BF),
-        got_plane=((places, half // places, 4 * width), BF),
-        piece=((planes, half // places, 4 * width // planes), BF),
-        got_z=((planes, half // places, 4 * width // planes), BF),
+        got_pair=((chunks, half, columns), BF),
+        got_plane=((chunks, places, half // places, columns), BF),
+        piece=((chunks, planes, half // places, 128), BF),
+        got_z=((chunks, planes, half // places, 128), BF),
+        wide_z=((planes, half, 128), BF),
+        wide_sum=((half, 128), BF),
+        wide_plane=((places, half // places, 128), BF),
         whole=((width, 4 * width), BF),
         small=((small_rows, width), F32),
         s_pair=((small_rows, width), F32),
@@ -1223,14 +1535,16 @@
         weights_sem=Weights.sems(geo),
         cot_sem=swap_sems(geo),
         x_sem=swap_sems(geo),
-        grad_sem=swap_sems(geo),
-        ret_sem=swap_sems(geo),
+        head_grad_sem=swap_sems(geo),
+        rest_grad_sem=swap_sems(geo),
+        head_ret_sem=swap_sems(geo),
+        rest_ret_sem=swap_sems(geo),
         expert_sem=ExpertGrads.sems(geo),
-        dense_sem=DenseSum.semaphores(geo)[1],
+        dense_sem=DenseSum.semaphores(geo, chunks)[1],
     )
     sem_names = [name + str(i) for name, found in sem_sets.items() for i in range(len(found))]
     sem_shapes = [s for found in sem_sets.values() for s in found]
-    names = [*inputs, *outputs, *scratch, *sem_names, "out_sem"]
+    names = [*inputs, *outputs, *scratch, *sem_names, "out_sem", "in_sem"]
     sizes = (rows, per_micro, seq, capacity, block, width, hidden)
     results = pl.pallas_call(
         functools.partial(block_kernel, geo, sizes, names),
@@ -1239,33 +1553,56 @@
         out_specs=[spec for _, _, spec in outputs.values()],
         scratch_shapes=[pltpu.VMEM(shape, dtype) for shape, dtype in scratch.values()]
         + sem_shapes
-        + [pltpu.SemaphoreType.DMA((5,))],
+        + [pltpu.SemaphoreType.DMA((5,)), pltpu.SemaphoreType.DMA((4,))],
         compiler_params=pltpu.CompilerParams(
             collective_id=0, has_side_effects=True, vmem_limit_bytes=VMEM_LIMIT
         ),
     )(*inputs.values())
     out = dict(zip(outputs, results, strict=True))
-    big, small = out["big_out"], out["small_out"]
-    layers = jnp.sum(out["d_layers"].astype(F32), axis=2)
-    d_bias = jnp.sum(out["d_bias"], axis=1)
-    return (
-        out["mixed"].reshape(tokens.shape),
-        out["grad_tokens"].reshape(tokens.shape),
-        small[0],
-        small[1],
-        big[:, : 3 * width].astype(F32),
-        small[2],
-        small[3],
-        big[:, 3 * width :].astype(F32),
-        small[4],
-        small[5],
-        small[6],
-        small[8:].T,
-        layers[0],
-        d_bias[:, 0, :part],
-        jnp.swapaxes(layers[1], 1, 2),
-        d_bias[:, 1, :],
+    shapes = dict(
+        mixed=((rows, width), BF, anywhere),
+        grad_tokens=((rows, width), F32, anywhere),
+        gain1=((width,), F32, vmem),
+        shift1=((width,), F32, vmem),
+        w_qkv=((width, 3 * width), F32, anywhere),
+        bias_q=((width,), F32, vmem),
+        bias_v=((width,), F32, vmem),
+        w_out=((width, width), F32, anywhere),
+        bias_out=((width,), F32, vmem),
+        gain2=((width,), F32, vmem),
+        shift2=((width,), F32, vmem),
+        router=((experts, width), F32, vmem),
+        w1=((local, width, part), F32, anywhere),
+        b1=((local, part), F32, vmem),
+        w2=((local, part, width), F32, anywhere),
+        b2=((local, width), F32, vmem),
     )
+    room = dict(
+        v_big=((width, 4 * width), BF),
+        v_layers=((2, local, group, width, part), BF),
+        v_tokens=((rows, width), F32),
+        v_mixed=((rows, width), BF),
+        o_big=((width, 4 * width), F32),
+        o_first=((local, width, part), F32),
+        o_second=((local, part, width), F32),
+    )
+    given = ["g_" + name for name in outputs]
+    made = pl.pallas_call(
+        functools.partial(finish_kernel, [*given, *shapes, *room, "sem"]),
+        out_shape=[jax.ShapeDtypeStruct(shape, dtype) for shape, dtype, _ in shapes.values()],
+        in_specs=[vmem if name == "d_bias" else spec for name, (_, _, spec) in outputs.items()],
+        out_specs=[spec for _, _, spec in shapes.values()],
+        scratch_shapes=[pltpu.VMEM(shape, dtype) for shape, dtype in room.values()]
+        + [pltpu.SemaphoreType.DMA((6 + 2 * local,))],
+        compiler_params=pltpu.CompilerParams(vmem_limit_bytes=VMEM_LIMIT),
+    )(*results)
+    made = dict(zip(shapes, made, strict=True))
+    made.update(
+        mixed=made["mixed"].reshape(tokens.shape),
+        grad_tokens=made["grad_tokens"].reshape(tokens.shape),
+        router=made["router"].T,
+    )
+    return tuple(made.values())
 
 
 def solution(mesh):

time: 220 us -> 173 us (0.79)
  local copies, waits for them, and re-layouts: 21.1 us -> 0 us
  Pallas kernels: 189 us -> 172 us
  other arithmetic: 7.95 us -> 0 us
    pallas_call x1, Pallas kernels: 189 us -> 165 us  [on_device(): pl.pallas_call(functools.partial(block_kernel, geo, sizes, names), out_sh...]
    broadcast_in_dim x7 -> x0, local copies, waits for them, and re-layouts: 8.81 us -> none  [on_device(): row = lambda v: v[None, :]]
    convert_element_type x3 -> x0, other arithmetic: 7.95 us -> none  [the longest x1 3.54 us: on_device(): big[:, :3 * width].astype(F32)]
    pallas_call x0 -> x1, Pallas kernels: none -> 7.16 us  [on_device(): pl.pallas_call(functools.partial(finish_kernel, [*given, *shapes, *room,...]
    unnamed x14 -> x0, local copies, waits for them, and re-layouts: 6.57 us -> none
    transpose x3 -> x0, local copies, waits for them, and re-layouts: 3.33 us -> none  [the longest x1 1.97 us: on_device(): jnp.swapaxes(layers[1], 1, 2)]
    slice x2 -> x0, local copies, waits for them, and re-layouts: 2.42 us -> none  [the longest x1 1.58 us: on_device(): small[6]]
where the time goes in v2:
time: 173 us
  Pallas kernels  172 us (99%)
    pallas_call x1, Pallas kernels, on_device(): pl.pallas_call(functools.partial(block_kernel, geo, sizes, names), out_sh...  165 us
    pallas_call x1, Pallas kernels, on_device(): pl.pallas_call(functools.partial(finish_kernel, [*given, *shapes, *room,...  7.16 us

profile of v2, /device:TPU:0, one launch (start us, length us, event | category | flops | bytes accessed | tf_op | source)
XLA Modules:
  0.0 172.7 jit_solution(12423247091087031045)
XLA Ops:
  0.7 164.7 %shard_map.297 = (bf16[576,512]{1,0:T(8,128)(2,1)}, f32[576,512]{1,0:T(8,128)}, bf16[512,2048]{1,0:T(8,128)(2,1)}, f32[24,512]{1,0:T(8,128)}, bf16[2,2,1,512,512...) custom-call(bf16[576,512]{1,0:T(8,128)(2,1)} %bitcast.7, bf16[576,512]{1,0:T(8,128)(2,1)} %bitcast.8, s32[2,2,288]{2,1,0:T(2,128)} %bitcast.10, ...), custom_call_target="tpu_custom_call" | custom-call | tf_op jit(solution)/shard_map/pallas_call | solution.py:1549
  165.4 7.2 %shard_map.298 = (bf16[576,512]{1,0:T(8,128)(2,1)}, f32[576,512]{1,0:T(8,128)}, f32[512]{0:T(512)}, f32[512]{0:T(512)}, f32[512,1536]{1,0:T(8,128)}, /*index=5*/...) custom-call(bf16[576,512]{1,0:T(8,128)(2,1)} %get-tuple-element.38.r, ...), custom_call_target="tpu_custom_call" | custom-call | tf_op jit(solution)/shard_map/pallas_call | solution.py:1590

commit v3 on v2

--- a/solution.py
+++ b/solution.py
@@ -81,11 +81,11 @@
 
 
 def pair_probs(stacked, keys, length):
-    scores = dot_nt(stacked, keys) * HEAD_DIM ** (-0.5)
-    visible = lax.broadcasted_iota(jnp.int32, scores.shape, 1) < length
+    scores = dot_nt(keys, stacked) * HEAD_DIM ** (-0.5)
+    visible = lax.broadcasted_iota(jnp.int32, scores.shape, 0) < length
     scores = jnp.where(visible, scores, -1e30)
-    raised = jnp.exp(scores - jnp.max(scores, axis=-1, keepdims=True))
-    return raised / jnp.sum(raised, axis=-1, keepdims=True)
+    raised = jnp.exp(scores - jnp.max(scores, axis=0, keepdims=True))
+    return raised * (1.0 / jnp.sum(raised, axis=0, keepdims=True))
 
 
 def attend_image(queries, keys, values, length):
@@ -95,7 +95,7 @@
     for g in range(queries.shape[1] // 128):
         cols = slice(g * 128, (g + 1) * 128)
         probs = pair_probs(head_pair(queries[:, cols], low), keys[:, cols], length).astype(BF)
-        out = dot(probs, values[:, cols])
+        out = dot_tn(probs, values[:, cols])
         parts.append(jnp.where(low, out[:seq], out[seq:]).astype(BF))
     return jnp.concatenate(parts, axis=1)
 
@@ -110,13 +110,13 @@
         stacked = head_pair(queries[:, cols], low)
         stacked_grad = head_pair(grad[:, cols], low)
         probs = pair_probs(stacked, keys[:, cols], length)
-        grad_probs = dot_nt(stacked_grad, values[:, cols])
-        parts[2].append(dot_tn(probs.astype(BF), stacked_grad).astype(BF))
-        centre = jnp.sum(probs * grad_probs, axis=-1, keepdims=True)
+        grad_probs = dot_nt(values[:, cols], stacked_grad)
+        parts[2].append(dot(probs.astype(BF), stacked_grad).astype(BF))
+        centre = jnp.sum(probs * grad_probs, axis=0, keepdims=True)
         grad_scores = (probs * (grad_probs - centre)).astype(BF)
-        grad_q = dot(grad_scores, keys[:, cols])
+        grad_q = dot_tn(grad_scores, keys[:, cols])
         parts[0].append((jnp.where(low, grad_q[:seq], grad_q[seq:]) * scale).astype(BF))
-        parts[1].append((dot_tn(grad_scores, stacked) * scale).astype(BF))
+        parts[1].append((dot(grad_scores, stacked) * scale).astype(BF))
     return [jnp.concatenate(part, axis=1) for part in parts]
 
 
@@ -139,16 +139,18 @@
 
 
 class Swap:
-    def __init__(self, geo, block, src, dst, sems, first=0, count=None, base=0):
+    def __init__(self, geo, block, src, dst, sems, first=0, count=None, base=0, stride=None):
         self.geo, self.block, self.src, self.dst = geo, block, src, dst
         self.first, self.count, self.base = first, count or block, base
+        self.stride = stride or block
         self.send_sem, self.recv_sem, self.local_sem = sems
+        self.apart = self.recv_sem.shape[0] > 1
 
     def given(self, p):
         return self.src.at[pl.ds(pl.multiple_of(p * self.block + self.first, 16), self.count)]
 
     def kept(self, p):
-        return self.dst.at[pl.ds(pl.multiple_of(self.base + p * self.count, 16), self.count)]
+        return self.dst.at[pl.ds(pl.multiple_of(self.base + p * self.stride, 16), self.count)]
 
     def local(self):
         mine = self.geo.mine()
@@ -163,42 +165,40 @@
 
         @pl.when(p != mine)
         def _():
-            remote(
-                self.given(p),
-                self.kept(mine),
-                self.send_sem.at[p],
-                self.recv_sem.at[mine],
-                self.geo.partner(p),
-            ).start()
-
-    def copy(self, p):
-        return remote(
-            self.given(p),
-            self.kept(p),
-            self.send_sem.at[p],
-            self.recv_sem.at[p],
-            self.geo.partner(p),
-        )
-
-    def wait_got(self, p):
-        mine = self.geo.mine()
-
-        @pl.when(p == mine)
+            sem = self.recv_sem.at[self.geo.here()[0] if self.apart else 0]
+            remote(self.given(p), self.kept(mine), self.send_sem.at[0], sem, self.geo.partner(p)).start()
+
+    def send_all(self):
+        mine, partners = self.geo.mine(), self.geo.partners
+        each(partners, lambda i: self.send(lax.rem(mine + 1 + i, partners)))
+
+    def blocks(self, count, sem):
+        spot = self.dst.at[pl.ds(0, count * self.count)]
+        return remote(spot, spot, self.send_sem.at[0], self.recv_sem.at[sem], self.geo.partner(0))
+
+    def wait_plane(self, plane):
+        z, quad = self.geo.here()[0], self.geo.plane_experts
+
+        @pl.when(plane == z)
         def _():
             self.local().wait()
-
-        @pl.when(p != mine)
+            self.blocks(quad - 1, plane).wait_recv()
+
+        @pl.when(plane != z)
         def _():
-            self.copy(p).wait_recv()
+            self.blocks(quad, plane).wait_recv()
+
+    def wait_all(self):
+        self.local().wait()
+        self.blocks(self.geo.partners - 1, 0).wait_recv()
 
     def wait_sent(self):
-        mine = self.geo.mine()
-        each(self.geo.partners - 1, lambda i: self.copy(lax.rem(mine + 1 + i, self.geo.partners)).wait_send())
-
-
-def swap_sems(geo):
+        self.blocks(self.geo.partners - 1, 0).wait_send()
+
+
+def swap_sems(groups):
     dma = pltpu.SemaphoreType.DMA
-    return [dma((geo.partners,)), dma((geo.partners,)), dma]
+    return [dma((1,)), dma((groups,)), dma]
 
 
 class Weights:
@@ -515,19 +515,10 @@
     @staticmethod
     def semaphores(geo, chunks):
         dma = pltpu.SemaphoreType.DMA
-        places, planes, both = (chunks, geo.places), (chunks, geo.planes), (chunks, geo.places)
         shapes = dict(
-            pair=(chunks,),
-            plane=places,
-            z=planes,
-            zg=planes,
-            pg=both,
-            cg=both,
-            sp=(1,),
-            sn=(geo.places,),
-            sz=(geo.planes,),
+            pair=chunks, plane=chunks, z=chunks, zg=chunks, pg=chunks, cg=chunks, sp=1, sn=1, sz=1
         )
-        return list(shapes), [dma(s) for s in shapes.values() for _ in range(2)]
+        return list(shapes), [dma((s,)) for s in shapes.values() for _ in range(2)]
 
     def sem(self, name):
         names, _ = self.semaphores(self.geo, 1)
@@ -540,6 +531,44 @@
 
     def others(self, here, count):
         return [lax.rem(here + i, count) for i in range(1, count)]
+
+    def bytes_of(self, name, c, spot):
+        send, recv = self.sem(name)
+        return remote(spot, spot, send.at[c], recv.at[c], self.where()[3])
+
+    def all_plane(self, c):
+        return self.bytes_of("plane", c, self.got_plane.at[c, pl.ds(0, self.geo.places - 1)])
+
+    def all_z(self, c):
+        return self.bytes_of("z", c, self.got_z.at[c, pl.ds(0, self.geo.planes - 1)])
+
+    def all_zg(self, c):
+        spot = self.whole.at[pl.ds(0, self.rows), pl.ds(0, (self.geo.planes - 1) * self.part)]
+        return self.bytes_of("zg", c, spot)
+
+    def all_pg(self, c):
+        spot = self.whole.at[pl.ds(0, (self.geo.places - 1) * self.rows), pl.ds(0, self.columns)]
+        return self.bytes_of("pg", c, spot)
+
+    def all_sn(self):
+        return self.bytes_of("sn", 0, self.s_plane.at[pl.ds(0, self.geo.places - 1)])
+
+    def all_sz(self):
+        return self.bytes_of("sz", 0, self.s_z.at[pl.ds(0, self.geo.planes - 1)])
+
+    def all_wide_plane(self, c):
+        return self.bytes_of("plane", c, self.wide_plane.at[pl.ds(0, self.geo.places - 1)])
+
+    def all_wide_z(self, c):
+        return self.bytes_of("z", c, self.wide_z.at[pl.ds(0, self.geo.planes - 1)])
+
+    def all_wide_pg(self, c):
+        spot = self.whole.at[pl.ds(0, (self.geo.places - 1) * self.rows), pl.ds(0, self.part)]
+        return self.bytes_of("pg", c, spot)
+
+    def all_wide_zg(self, c):
+        spot = self.whole.at[pl.ds(0, self.half), pl.ds(0, (self.geo.planes - 1) * self.part)]
+        return self.bytes_of("zg", c, spot)
 
     def cols(self, c):
         return pl.ds(c * self.columns, self.columns)
@@ -559,7 +588,7 @@
         z, k, n, _ = self.where()
         send, recv = self.sem("plane")
         src = self.mine.at[self.place_rows(k, q), self.cols(c)]
-        return remote(src, self.got_plane.at[c, n], send.at[c, q], recv.at[c, n], (z * 2 + k, q))
+        return remote(src, self.got_plane.at[c, n], send.at[c], recv.at[c], (z * 2 + k, q))
 
     def plane_start(self, c):
         z, k, n, _ = self.where()
@@ -575,15 +604,12 @@
         z, k, n, _ = self.where()
         send, recv = self.sem("z")
         return remote(
-            self.piece.at[c, q], self.got_z.at[c, z], send.at[c, q], recv.at[c, z], (q * 2 + k, n)
+            self.piece.at[c, q], self.got_z.at[c, z], send.at[c], recv.at[c], (q * 2 + k, n)
         )
 
     def z_start(self, c):
         z, k, n, sibling = self.where()
-        send, recv = self.sem("plane")
-        for q in self.others(n, self.geo.places):
-            spot = self.got_plane.at[c, q]
-            remote(spot, spot, send.at[c, q], recv.at[c, q], sibling).wait_recv()
+        self.all_plane(c).wait_recv()
         total = self.got_plane[c, 0].astype(F32)
         for i in range(1, self.geo.places):
             total = total + self.got_plane[c, i].astype(F32)
@@ -602,14 +628,11 @@
         z, k, n, _ = self.where()
         send, recv = self.sem("zg")
         spot = self.spot(c, z)
-        return remote(spot, spot, send.at[c, q], recv.at[c, z], (q * 2 + k, n))
+        return remote(spot, spot, send.at[c], recv.at[c], (q * 2 + k, n))
 
     def gather_z(self, c):
         z, k, n, sibling = self.where()
-        send, recv = self.sem("z")
-        for q in self.others(z, self.geo.planes):
-            spot = self.got_z.at[c, q]
-            remote(spot, spot, send.at[c, q], recv.at[c, q], sibling).wait_recv()
+        self.all_z(c).wait_recv()
         total = self.got_z[c, 0].astype(F32)
         for i in range(1, self.geo.planes):
             total = total + self.got_z[c, i].astype(F32)
@@ -625,38 +648,26 @@
         z, k, n, _ = self.where()
         send, recv = self.sem("pg")
         spot = self.row_spot(c, k, n)
-        return remote(spot, spot, send.at[c, q], recv.at[c, n], (z * 2 + k, q))
-
-    def cg_copy(self, c, q):
-        z, k, n, sibling = self.where()
+        return remote(spot, spot, send.at[c], recv.at[c], (z * 2 + k, q))
+
+    def cg_copy(self, c, k):
         send, recv = self.sem("cg")
-        spot = self.row_spot(c, k, q)
-        return remote(spot, spot, send.at[c, q], recv.at[c, q], sibling)
+        half = pl.ds(pl.multiple_of(k * self.half, 16), self.half)
+        spot = self.whole.at[half, self.cols(c)]
+        return remote(spot, spot, send.at[c], recv.at[c], self.where()[3])
 
     def gather_plane(self, c):
         z, k, n, sibling = self.where()
-        send, recv = self.sem("zg")
-        for q in self.others(z, self.geo.planes):
-            spot = self.spot(c, q)
-            remote(spot, spot, send.at[c, q], recv.at[c, q], sibling).wait_recv()
+        self.all_zg(c).wait_recv()
         for q in self.others(n, self.geo.places):
             self.pg_copy(c, q).start()
-        self.cg_copy(c, n).start()
 
     def gather_pair(self, c):
-        z, k, n, sibling = self.where()
-        send, recv = self.sem("pg")
-        for q in self.others(n, self.geo.places):
-            spot = self.row_spot(c, k, q)
-            remote(spot, spot, send.at[c, q], recv.at[c, q], sibling).wait_recv()
-            self.cg_copy(c, q).start()
+        self.all_pg(c).wait_recv()
+        self.cg_copy(c, self.geo.here()[1]).start()
 
     def gather_end(self, c):
-        z, k, n, sibling = self.where()
-        send, recv = self.sem("cg")
-        for q in range(self.geo.places):
-            spot = self.row_spot(c, 1 - k, q)
-            remote(spot, spot, send.at[c, q], recv.at[c, q], sibling).wait_recv()
+        self.cg_copy(c, 1 - self.geo.here()[1]).wait_recv()
 
 
     def half_part(self, p, c):
@@ -668,7 +679,7 @@
         z, k, n, _ = self.where()
         send, recv = self.sem("z")
         src = self.mine.at[self.half_part(q, c)]
-        return remote(src, self.wide_z.at[z], send.at[c, q], recv.at[c, z], (q * 2 + k, n))
+        return remote(src, self.wide_z.at[z], send.at[c], recv.at[c], (q * 2 + k, n))
 
     def wide_z_start(self, c):
         z, k, n, _ = self.where()
@@ -683,15 +694,13 @@
         z, k, n, _ = self.where()
         send, recv = self.sem("plane")
         src = self.wide_sum.at[pl.ds(pl.multiple_of(q * self.rows, 16), self.rows)]
-        return remote(src, self.wide_plane.at[n], send.at[c, q], recv.at[c, n], (z * 2 + k, q))
+        return remote(src, self.wide_plane.at[n], send.at[c], recv.at[c], (z * 2 + k, q))
 
     def wide_plane_start(self, c):
         z, k, n, sibling = self.where()
-        send, recv = self.sem("z")
         total = self.mine[self.half_part(z, c)].astype(F32)
+        self.all_wide_z(c).wait_recv()
         for q in self.others(z, self.geo.planes):
-            spot = self.wide_z.at[q]
-            remote(spot, spot, send.at[c, q], recv.at[c, q], sibling).wait_recv()
             total = total + self.wide_z[q].astype(F32)
         self.wide_sum[...] = total.astype(BF)
         for q in self.others(n, self.geo.places):
@@ -699,12 +708,10 @@
 
     def wide_gather_plane(self, c):
         z, k, n, sibling = self.where()
-        send, recv = self.sem("plane")
         here = pl.ds(pl.multiple_of(n * self.rows, 16), self.rows)
         total = self.wide_sum[here].astype(F32)
+        self.all_wide_plane(c).wait_recv()
         for q in self.others(n, self.geo.places):
-            spot = self.wide_plane.at[q]
-            remote(spot, spot, send.at[c, q], recv.at[c, q], sibling).wait_recv()
             total = total + self.wide_plane[q].astype(F32)
         first = pl.multiple_of(c * self.columns + z * self.part, 128)
         self.whole[self.place_rows(k, n), pl.ds(first, self.part)] = total.astype(BF)
@@ -720,44 +727,23 @@
         z, k, n, _ = self.where()
         send, recv = self.sem("pg")
         spot = self.wide_spot(c, n)
-        return remote(spot, spot, send.at[c, q], recv.at[c, n], (z * 2 + k, q))
+        return remote(spot, spot, send.at[c], recv.at[c], (z * 2 + k, q))
 
     def wide_zg_copy(self, c, q):
         z, k, n, _ = self.where()
         send, recv = self.sem("zg")
         spot = self.whole.at[self.half_part(z, c)]
-        return remote(spot, spot, send.at[c, q], recv.at[c, z], (q * 2 + k, n))
+        return remote(spot, spot, send.at[c], recv.at[c], (q * 2 + k, n))
 
     def wide_gather_z(self, c):
         z, k, n, sibling = self.where()
-        send, recv = self.sem("pg")
-        for q in self.others(n, self.geo.places):
-            spot = self.wide_spot(c, q)
-            remote(spot, spot, send.at[c, q], recv.at[c, q], sibling).wait_recv()
+        self.all_wide_pg(c).wait_recv()
         for q in self.others(z, self.geo.planes):
             self.wide_zg_copy(c, q).start()
 
-    def wide_pair_copy(self, c):
-        z, k, n, sibling = self.where()
-        send, recv = self.sem("cg")
-        half = pl.ds(pl.multiple_of(k * self.half, 16), self.half)
-        spot = self.whole.at[half, self.cols(c)]
-        return remote(spot, spot, send.at[c, 0], recv.at[c, 0], sibling)
-
     def wide_gather_pair(self, c):
-        z, k, n, sibling = self.where()
-        send, recv = self.sem("zg")
-        for q in self.others(z, self.geo.planes):
-            spot = self.whole.at[self.half_part(q, c)]
-            remote(spot, spot, send.at[c, q], recv.at[c, q], sibling).wait_recv()
-        self.wide_pair_copy(c).start()
-
-    def wide_gather_end(self, c):
-        z, k, n, sibling = self.where()
-        send, recv = self.sem("cg")
-        half = pl.ds(pl.multiple_of((1 - k) * self.half, 16), self.half)
-        spot = self.whole.at[half, self.cols(c)]
-        remote(spot, spot, send.at[c, 0], recv.at[c, 0], sibling).wait_recv()
+        self.all_wide_zg(c).wait_recv()
+        self.cg_copy(c, self.geo.here()[1]).start()
 
     def stages(self, c):
         if c == self.wide_chunk:
@@ -767,7 +753,7 @@
                 self.wide_gather_plane,
                 self.wide_gather_z,
                 self.wide_gather_pair,
-                self.wide_gather_end,
+                self.gather_end,
             )
         return (
             self.plane_start,
@@ -785,12 +771,12 @@
     def sn_copy(self, q):
         z, k, n, _ = self.where()
         send, recv = self.sem("sn")
-        return remote(self.s_plane.at[n], self.s_plane.at[n], send.at[q], recv.at[n], (z * 2 + k, q))
+        return remote(self.s_plane.at[n], self.s_plane.at[n], send.at[0], recv.at[0], (z * 2 + k, q))
 
     def sz_copy(self, q):
         z, k, n, _ = self.where()
         send, recv = self.sem("sz")
-        return remote(self.s_z.at[z], self.s_z.at[z], send.at[q], recv.at[z], (q * 2 + k, n))
+        return remote(self.s_z.at[z], self.s_z.at[z], send.at[0], recv.at[0], (q * 2 + k, n))
 
     def small_plane(self):
         z, k, n, _ = self.where()
@@ -802,11 +788,7 @@
     def small_z(self):
         z, k, n, sibling = self.where()
         geo = self.geo
-        send, recv = self.sem("sn")
-        for i in range(1, geo.places):
-            q = lax.rem(n + i, geo.places)
-            spot = self.s_plane.at[q]
-            remote(spot, spot, send.at[q], recv.at[q], sibling).wait_recv()
+        self.all_sn().wait_recv()
         total = self.s_plane[0]
         for i in range(1, geo.places):
             total = total + self.s_plane[i]
@@ -817,40 +799,22 @@
     def small_finish(self, out):
         z, k, n, sibling = self.where()
         geo = self.geo
-        send, recv = self.sem("sz")
-        for i in range(1, geo.planes):
-            q = lax.rem(z + i, geo.planes)
-            spot = self.s_z.at[q]
-            remote(spot, spot, send.at[q], recv.at[q], sibling).wait_recv()
+        self.all_sz().wait_recv()
         total = self.s_z[0]
         for i in range(1, geo.planes):
             total = total + self.s_z[i]
         out[...] = total
 
     def wait_sent(self, chunks):
-        z, k, n, _ = self.where()
-        for q in self.others(n, self.geo.places):
-            self.sn_copy(q).wait_send()
-        for q in self.others(z, self.geo.planes):
-            self.sz_copy(q).wait_send()
+        self.all_sn().wait_send()
+        self.all_sz().wait_send()
         for c in range(chunks):
-            if c == self.wide_chunk:
-                for q in self.others(n, self.geo.places):
-                    self.wide_plane_copy(c, q).wait_send()
-                    self.wide_pg_copy(c, q).wait_send()
-                for q in self.others(z, self.geo.planes):
-                    self.wide_z_copy(c, q).wait_send()
-                    self.wide_zg_copy(c, q).wait_send()
-                self.wide_pair_copy(c).wait_send()
-                continue
-            for q in self.others(n, self.geo.places):
-                self.plane_copy(c, q).wait_send()
-                self.pg_copy(c, q).wait_send()
-            for q in self.others(z, self.geo.planes):
-                self.z_copy(c, q).wait_send()
-                self.zg_copy(c, q).wait_send()
-            for q in range(self.geo.places):
-                self.cg_copy(c, q).wait_send()
+            wide = c == self.wide_chunk
+            (self.all_wide_plane if wide else self.all_plane)(c).wait_send()
+            (self.all_wide_z if wide else self.all_z)(c).wait_send()
+            (self.all_wide_pg if wide else self.all_pg)(c).wait_send()
+            (self.all_wide_zg if wide else self.all_zg)(c).wait_send()
+            self.cg_copy(c, 0).wait_send()
 
 
 def greet_start(devices):
@@ -924,31 +888,31 @@
         return [ref for key, ref in zip(names, refs, strict=True) if key.startswith(name)]
 
     greet_start(all_devices(geo))
-    arrive = [
-        pltpu.make_async_copy(src, dst, r.in_sem.at[i])
-        for i, (src, dst) in enumerate(
-            (
-                (r.given_cot, r.cot),
-                (r.given_tokens, r.tokens),
-                (r.given_w_qkv, r.w_qkv),
-                (r.given_w_out, r.w_out),
-            )
-        )
-    ]
-    for copy in arrive:
+    own = [name for name in names if name.startswith("given_")]
+    arrive = {
+        name[6:]: pltpu.make_async_copy(getattr(r, name), getattr(r, name[6:]), r.in_sem.at[i])
+        for i, name in enumerate(own)
+    }
+    for copy in arrive.values():
         copy.start()
+
+    def need(*wanted):
+        for name in wanted:
+            arrive[name].wait()
+
+    need("choices")
     weights = Weights(
         geo, (r.w1, r.w2), (r.first, r.second), r.tile, r.tiles, sems("weights_sem")
     )
     cot_swap = Swap(geo, block, r.send_a, r.cot_got, sems("cot_sem"))
     x_swap = Swap(geo, block, r.send_b, r.x_got, sems("x_sem"))
     grad_swap, late_grad_swap = (
-        Swap(geo, block, r.send_a, r.grad_got, sems("head_grad_sem"), 0, head, 0),
-        Swap(geo, block, r.send_a, r.grad_got, sems("rest_grad_sem"), head, rest, heads),
+        Swap(geo, block, r.send_a, r.grad_got, sems("head_grad_sem"), 0, head, 0, head),
+        Swap(geo, block, r.send_a, r.grad_got, sems("rest_grad_sem"), head, rest, heads, rest),
     )
     ret_swap, late_ret_swap = (
-        Swap(geo, block, r.send_b, r.ret_got, sems("head_ret_sem"), 0, head, 0),
-        Swap(geo, block, r.send_b, r.ret_got, sems("rest_ret_sem"), head, rest, heads),
+        Swap(geo, block, r.send_b, r.ret_got, sems("head_ret_sem"), 0, head, 0, head),
+        Swap(geo, block, r.send_b, r.ret_got, sems("rest_ret_sem"), head, rest, heads, rest),
     )
 
     r.ids[...] = jnp.zeros(r.ids.shape, F32)
@@ -986,7 +950,7 @@
 
         @pl.when(i == 0)
         def _():
-            arrive[0].wait()
+            need("cot")
             pl.semaphore_wait(pltpu.get_barrier_semaphore(), len(all_devices(geo)))
 
         blocks = dot(r.table[span(plane, chunk), :], r.cot[...])
@@ -996,6 +960,7 @@
 
     each(geo.planes, send_cot)
     r.table[pl.ds(slots, 128), :] = jnp.zeros((128, rows), BF)
+    need("b1", "b2")
     for i in range(geo.local_experts):
         r.tile[i] = jnp.zeros((8, width), F32)
         r.tile[i, 0:1, 0:part] = r.b1[i : i + 1, :].astype(F32)
@@ -1007,9 +972,9 @@
         normed = unit * vector(r.gain1) + vector(r.shift1)
         r.normed[span(i, seq), :] = normed.astype(BF)
 
-    arrive[1].wait()
+    need("tokens", "gain1", "shift1")
     each(images, norm_in)
-    arrive[2].wait()
+    need("w_qkv", "bias_q", "bias_v")
     for c in range(3 * width // tile):
         cols = slice(c * tile, (c + 1) * tile)
         out = dot(r.normed[...], r.w_qkv[:, cols])
@@ -1048,7 +1013,7 @@
         r.probs[here, 0:experts] = probs
 
     r.probs[...] = jnp.zeros(r.probs.shape, F32)
-    arrive[3].wait()
+    need("w_out", "bias_out", "gain2", "shift2", "w_router")
     each(images, branch)
     probs_t = jnp.transpose(r.probs[...])[0:experts, :]
     high, low = split_two(probs_t)
@@ -1088,13 +1053,21 @@
     r.sum_pre[...] = jnp.zeros(r.sum_pre.shape, F32)
     r.sum_ret[...] = jnp.zeros(r.sum_ret.shape, F32)
 
+    def send_late(first, last):
+        for i in range(first, last):
+            for j in range(quad):
+                late_grad_swap.send(lax.rem(z + i, geo.planes) * quad + j)
+
     def expert_chunk(i):
         plane = lax.rem(z + i, geo.planes)
         here = span(plane, chunk)
-        for j in range(quad):
-            cot_swap.wait_got(plane * quad + j)
-        for j in range(quad):
-            x_swap.wait_got(plane * quad + j)
+        cot_swap.wait_plane(plane)
+        x_swap.wait_plane(plane)
+
+        @pl.when(i == geo.planes - 1)
+        def _():
+            send_late(0, geo.planes // 2)
+
         for j in range(quad):
             at = (plane * quad + j) * block
             group = r.x_got[pl.ds(pl.multiple_of(at + gate_group, 16), 16), 0:128].astype(F32)
@@ -1107,10 +1080,11 @@
             cols = slice(c * tile, (c + 1) * tile)
             pre = dot(r.x_got[here, :], r.first[:, cols]) + r.bias1[0:1, cols]
             square = pre * pre
-            bend = jnp.tanh(root * pre * (1.0 + 0.044715 * square))
-            half = 0.5 * (1.0 + bend)
-            r.hidden[here, cols] = (pre * half).astype(BF)
-            slope = half + 0.5 * pre * (1.0 - bend * bend) * (root + 3 * 0.044715 * root * square)
+            bend = jnp.tanh(pre * (root + 0.044715 * root * square))
+            half = 0.5 + 0.5 * bend
+            hidden_rows = pre * half
+            r.hidden[here, cols] = hidden_rows.astype(BF)
+            slope = half + hidden_rows * (1.0 - bend) * (root + 3 * 0.044715 * root * square)
             back = dot_nt(r.grad_ret[here, :], r.second[cols, :])
             grad_pre = (back * slope).astype(BF)
             r.grad_pre[here, cols] = grad_pre
@@ -1133,8 +1107,9 @@
             grad_swap.send(e)
 
     each(geo.planes, expert_chunk)
-    for swap in (late_grad_swap, ret_swap, late_ret_swap):
-        each(experts, lambda i: swap.send(lax.rem(geo.mine() + 1 + i, experts)))
+    send_late(geo.planes // 2, geo.planes)
+    for swap in (ret_swap, late_ret_swap):
+        swap.send_all()
 
     grads = ExpertGrads(
         geo,
@@ -1185,7 +1160,6 @@
     )
 
     def slot_grads(e):
-        grad_swap.wait_got(e)
         at = pl.ds(pl.multiple_of(e * head + gate_group, 16), 16)
         group = r.grad_got[at, 0:128].astype(F32)
         column = lane_row(group[gate_line : gate_line + 1] + group[gate_line + 1 : gate_line + 2], block)
@@ -1275,10 +1249,10 @@
             grad, unit, scale, vector(r.gain1)
         )
 
-    def mix(i):
+    def mix(there, i):
         here = span(i, seq)
-        total = dot(r.table_t[here, :], r.ret_got[...])
-        chosen = dot(r.table0_t[here, :], r.ret_got[...])
+        total = dot(r.table_t[here, there], r.ret_got[there, :])
+        chosen = dot(r.table0_t[here, there], r.ret_got[there, :])
         probs = r.probs[here, :]
         lane = lax.broadcasted_iota(jnp.int32, probs.shape, 1).astype(F32)
         gates = [
@@ -1293,10 +1267,12 @@
         each(count, lambda i: step(m * count + i))
 
     micros = rows // per_micro
+    last = (micros - 1) * images // micros
+    grad_swap.wait_all()
     each(experts, slot_grads)
     for m in range(micros):
         if m == 1:
-            each(experts, late_grad_swap.wait_got)
+            late_grad_swap.wait_all()
         combine(m)
         some(norm_two_back, m)
         if m == micros - 1 and early:
@@ -1305,8 +1281,11 @@
             dense.pair(chunks - 1).start()
         attend_grad(m)
         if m == micros - 1 and early:
+            attend_back(last)
             stages[0](chunks - 1)
-        some(attend_back, m)
+            each(images - last - 1, lambda i: attend_back(last + 1 + i))
+        else:
+            some(attend_back, m)
         if m < micros - 1:
             some(norm_one_back, m)
     router = dot_tn(r.logits_high[...], r.expert_in[...]) + dot_tn(r.logits_low[...], r.expert_in[...])
@@ -1327,11 +1306,27 @@
         layers_copy.start()
         bias_copy.start()
 
-    beside = [functools.partial(norm_one_back, i) for i in range((micros - 1) * images // micros, images)]
-    beside += [tokens_done, dense.small_plane, dense.small_z]
-    beside += [lambda: each(experts, ret_swap.wait_got), lambda: each(experts, late_ret_swap.wait_got)]
-    beside += [functools.partial(mix, i) for i in range(images)]
-    beside += [mixed_copy.start, lambda: dense.small_finish(r.small_out), owner_done]
+    def early_mix():
+        ret_swap.wait_all()
+        each(last, functools.partial(mix, slice(0, heads)))
+
+    def late_mix():
+        late_ret_swap.wait_all()
+        each(images - last, lambda i: mix(slice(0, slots), last + i))
+        mixed_copy.start()
+
+    beside = [[] for _ in stages]
+    beside[0] = [lambda: some(norm_one_back, micros - 1), tokens_done]
+    beside[1] = [dense.small_plane]
+    beside[2] = [dense.small_z, early_mix]
+    beside[3] = [owner_done]
+    small_copy = pltpu.make_async_copy(r.small, r.small_out, r.out_sem.at[5])
+
+    def small_done():
+        dense.small_finish(r.small)
+        small_copy.start()
+
+    beside[4] = [small_done, late_mix]
     for c in range(late):
         for first in range(c * columns, (c + 1) * columns, tile):
             dense_grad(first)
@@ -1341,11 +1336,8 @@
             dense.stages(c)[stage](c)
         if early and done + stage < len(stages):
             stages[done + stage](chunks - 1)
-        for step in beside[:4]:
+        for step in beside[stage]:
             step()
-        beside = beside[4:]
-    for step in beside:
-        step()
     big_copy = pltpu.make_async_copy(r.whole, r.big_out, r.out_sem.at[4])
     big_copy.start()
     for swap in (grad_swap, late_grad_swap, ret_swap, late_ret_swap):
@@ -1353,7 +1345,7 @@
     weights.wait_sent()
     grads.wait_sent()
     dense.wait_sent(chunks)
-    for copy in (mixed_copy, tokens_copy, layers_copy, bias_copy, big_copy):
+    for copy in (mixed_copy, tokens_copy, layers_copy, bias_copy, small_copy, big_copy):
         copy.wait()
 
 
@@ -1361,49 +1353,58 @@
     r = SimpleNamespace(**dict(zip(names, refs, strict=True)))
     width, part = r.w_out.shape[0], r.w1.shape[2]
     local, group = r.g_d_layers.shape[1:3]
-    come_big = pltpu.make_async_copy(r.g_big_out, r.v_big, r.sem.at[0])
-    come_layers = pltpu.make_async_copy(r.g_d_layers, r.v_layers, r.sem.at[1])
-    come_tokens = pltpu.make_async_copy(r.g_grad_tokens, r.v_tokens, r.sem.at[2])
-    come_mixed = pltpu.make_async_copy(r.g_mixed, r.v_mixed, r.sem.at[3])
+    sems = iter(range(len(names)))
+
+    def move(src, dst):
+        copy = pltpu.make_async_copy(src, dst, r.sem.at[next(sems)])
+        copy.start()
+        return copy
+
+    come_layers = [
+        [move(r.g_d_layers.at[layer, i], r.v_layers.at[layer, i]) for layer in range(2)] for i in range(local)
+    ]
+    come_big = [
+        move(r.g_big_out.at[:, c * width : (c + 1) * width], r.v_big.at[:, c * width : (c + 1) * width])
+        for c in range(4)
+    ]
+    come_small, come_bias = move(r.g_small_out, r.v_small), move(r.g_d_bias, r.v_bias)
+    come_tokens, come_mixed = move(r.g_grad_tokens, r.v_tokens), move(r.g_mixed, r.v_mixed)
     copies = []
-    for copy in (come_big, come_layers, come_tokens, come_mixed):
-        copy.start()
-    vectors = dict(gain1=0, shift1=1, bias_q=2, bias_v=3, bias_out=4, gain2=5, shift2=6)
-    for name, line in vectors.items():
-        getattr(r, name)[...] = r.g_small_out[line]
-    r.router[...] = r.g_small_out[8:, :]
-    tiles = r.g_d_bias[:, 0]
-    for g in range(1, group):
-        tiles = tiles + r.g_d_bias[:, g]
-    r.b1[...] = tiles[:, 0, 0:part]
-    r.b2[...] = tiles[:, 1, :]
-
-    def leave(src, dst, sem):
-        copy = pltpu.make_async_copy(src, dst, sem)
-        copy.start()
-        copies.append(copy)
-
-    come_big.wait()
-    for i, (out, first) in enumerate(((r.w_qkv, 0), (r.w_out, 3 * width))):
-        cols = slice(first, first + out.shape[1])
-        r.o_big[:, cols] = r.v_big[:, cols].astype(F32)
-        leave(r.o_big.at[:, cols], out, r.sem.at[4 + i])
-    come_tokens.wait()
-    leave(r.v_tokens, r.grad_tokens, r.sem.at[2])
-    come_mixed.wait()
-    leave(r.v_mixed, r.mixed, r.sem.at[3])
-    come_layers.wait()
     for i in range(local):
         for layer in range(2):
+            come_layers[i][layer].wait()
             total = r.v_layers[layer, i, 0].astype(F32)
             for g in range(1, group):
                 total = total + r.v_layers[layer, i, g].astype(F32)
             if layer == 0:
                 r.o_first[i] = total
-                leave(r.o_first.at[i], r.w1.at[i], r.sem.at[6 + 2 * i])
+                copies.append(move(r.o_first.at[i], r.w1.at[i]))
             else:
                 r.o_second[i] = jnp.transpose(total)
-                leave(r.o_second.at[i], r.w2.at[i], r.sem.at[7 + 2 * i])
+                copies.append(move(r.o_second.at[i], r.w2.at[i]))
+    for c in range(4):
+        come_big[c].wait()
+        cols = slice(c * width, (c + 1) * width)
+        r.o_big[:, cols] = r.v_big[:, cols].astype(F32)
+        copies.append(move(r.o_big.at[:, cols], r.w_qkv.at[:, cols] if c < 3 else r.w_out))
+    come_small.wait()
+    lines = ("gain1", "shift1", "bias_q", "bias_v", "bias_out", "gain2", "shift2")
+    for line, name in enumerate(lines):
+        row = getattr(r, "v_" + name)
+        row[...] = r.v_small[line]
+        copies.append(move(row, getattr(r, name)))
+    copies.append(move(r.v_small.at[8:], r.router))
+    come_bias.wait()
+    tiles = r.v_bias[:, 0]
+    for g in range(1, group):
+        tiles = tiles + r.v_bias[:, g]
+    r.v_b1[...] = tiles[:, 0, 0:part]
+    r.v_b2[...] = tiles[:, 1, :]
+    copies += [move(r.v_b1, r.b1), move(r.v_b2, r.b2)]
+    come_tokens.wait()
+    copies.append(move(r.v_tokens, r.grad_tokens))
+    come_mixed.wait()
+    copies.append(move(r.v_mixed, r.mixed))
     for copy in copies:
         copy.wait()
 
@@ -1440,24 +1441,24 @@
     hidden = part * geo.places
     places, planes, local, group = geo.places, geo.planes, geo.local_experts, geo.group
     inputs = dict(
+        given_choices=jnp.swapaxes(expert_index, 1, 2),
+        given_cot=grad_out.reshape(rows, width),
         given_tokens=tokens.reshape(rows, width),
-        given_cot=grad_out.reshape(rows, width),
-        choices=jnp.swapaxes(expert_index, 1, 2),
         lengths=image_lengths,
-        gain1=ln1_gain,
-        shift1=ln1_bias,
+        given_gain1=ln1_gain,
+        given_shift1=ln1_bias,
         given_w_qkv=w_qkv,
-        bias_q=bias_query,
-        bias_v=bias_value,
+        given_bias_q=bias_query,
+        given_bias_v=bias_value,
         given_w_out=w_out,
-        bias_out=bias_out,
-        gain2=ln2_gain,
-        shift2=ln2_bias,
-        w_router=w_router.T,
+        given_bias_out=bias_out,
+        given_gain2=ln2_gain,
+        given_shift2=ln2_bias,
+        given_w_router=w_router.T,
         w1=experts_in,
-        b1=experts_in_bias,
+        given_b1=experts_in_bias,
         w2=experts_out,
-        b2=experts_out_bias,
+        given_b2=experts_out_bias,
     )
     vmem, smem = pl.BlockSpec(memory_space=pltpu.VMEM), pl.BlockSpec(memory_space=pltpu.SMEM)
     anywhere = pl.BlockSpec(memory_space=pl.ANY)
@@ -1469,18 +1470,15 @@
         mixed=((rows, width), BF, anywhere),
         grad_tokens=((rows, width), F32, anywhere),
         big_out=((width, 4 * width), BF, anywhere),
-        small_out=((small_rows, width), F32, vmem),
+        small_out=((small_rows, width), F32, anywhere),
         d_layers=((2, local, group, width, part), BF, anywhere),
         d_bias=((local, group, 8, width), F32, anywhere),
     )
     half = width // 2
     columns = DenseSum.chunk_columns(geo)
     chunks = 4 * width // columns
-    scratch = dict(
-        tokens=((rows, width), BF),
-        cot=((rows, width), BF),
-        w_qkv=((width, 3 * width), BF),
-        w_out=((width, width), BF),
+    scratch = {name[6:]: (a.shape, a.dtype) for name, a in inputs.items() if name.startswith("given")}
+    scratch.update(
         tile=((local, 8, width), F32),
         tiles=((places, 8, width), F32),
         first=((width, hidden), BF),
@@ -1533,12 +1531,12 @@
     )
     sem_sets = dict(
         weights_sem=Weights.sems(geo),
-        cot_sem=swap_sems(geo),
-        x_sem=swap_sems(geo),
-        head_grad_sem=swap_sems(geo),
-        rest_grad_sem=swap_sems(geo),
-        head_ret_sem=swap_sems(geo),
-        rest_ret_sem=swap_sems(geo),
+        cot_sem=swap_sems(planes),
+        x_sem=swap_sems(planes),
+        head_grad_sem=swap_sems(1),
+        rest_grad_sem=swap_sems(1),
+        head_ret_sem=swap_sems(1),
+        rest_ret_sem=swap_sems(1),
         expert_sem=ExpertGrads.sems(geo),
         dense_sem=DenseSum.semaphores(geo, chunks)[1],
     )
@@ -1553,47 +1551,50 @@
         out_specs=[spec for _, _, spec in outputs.values()],
         scratch_shapes=[pltpu.VMEM(shape, dtype) for shape, dtype in scratch.values()]
         + sem_shapes
-        + [pltpu.SemaphoreType.DMA((5,)), pltpu.SemaphoreType.DMA((4,))],
+        + [pltpu.SemaphoreType.DMA((6,)), pltpu.SemaphoreType.DMA((len(inputs),))],
         compiler_params=pltpu.CompilerParams(
             collective_id=0, has_side_effects=True, vmem_limit_bytes=VMEM_LIMIT
         ),
     )(*inputs.values())
     out = dict(zip(outputs, results, strict=True))
     shapes = dict(
-        mixed=((rows, width), BF, anywhere),
-        grad_tokens=((rows, width), F32, anywhere),
-        gain1=((width,), F32, vmem),
-        shift1=((width,), F32, vmem),
-        w_qkv=((width, 3 * width), F32, anywhere),
-        bias_q=((width,), F32, vmem),
-        bias_v=((width,), F32, vmem),
-        w_out=((width, width), F32, anywhere),
-        bias_out=((width,), F32, vmem),
-        gain2=((width,), F32, vmem),
-        shift2=((width,), F32, vmem),
-        router=((experts, width), F32, vmem),
-        w1=((local, width, part), F32, anywhere),
-        b1=((local, part), F32, vmem),
-        w2=((local, part, width), F32, anywhere),
-        b2=((local, width), F32, vmem),
+        mixed=((rows, width), BF),
+        grad_tokens=((rows, width), F32),
+        gain1=((width,), F32),
+        shift1=((width,), F32),
+        w_qkv=((width, 3 * width), F32),
+        bias_q=((width,), F32),
+        bias_v=((width,), F32),
+        w_out=((width, width), F32),
+        bias_out=((width,), F32),
+        gain2=((width,), F32),
+        shift2=((width,), F32),
+        router=((experts, width), F32),
+        w1=((local, width, part), F32),
+        b1=((local, part), F32),
+        w2=((local, part, width), F32),
+        b2=((local, width), F32),
     )
     room = dict(
         v_big=((width, 4 * width), BF),
         v_layers=((2, local, group, width, part), BF),
         v_tokens=((rows, width), F32),
         v_mixed=((rows, width), BF),
+        v_small=((small_rows, width), F32),
+        v_bias=((local, group, 8, width), F32),
         o_big=((width, 4 * width), F32),
         o_first=((local, width, part), F32),
         o_second=((local, part, width), F32),
     )
+    room.update({"v_" + name: spec for name, spec in shapes.items() if len(spec[0]) == 1 or name in ("b1", "b2")})
     given = ["g_" + name for name in outputs]
     made = pl.pallas_call(
         functools.partial(finish_kernel, [*given, *shapes, *room, "sem"]),
-        out_shape=[jax.ShapeDtypeStruct(shape, dtype) for shape, dtype, _ in shapes.values()],
-        in_specs=[vmem if name == "d_bias" else spec for name, (_, _, spec) in outputs.items()],
-        out_specs=[spec for _, _, spec in shapes.values()],
+        out_shape=[jax.ShapeDtypeStruct(shape, dtype) for shape, dtype in shapes.values()],
+        in_specs=[anywhere] * len(outputs),
+        out_specs=[anywhere] * len(shapes),
         scratch_shapes=[pltpu.VMEM(shape, dtype) for shape, dtype in room.values()]
-        + [pltpu.SemaphoreType.DMA((6 + 2 * local,))],
+        + [pltpu.SemaphoreType.DMA((24 + 4 * local,))],
         compiler_params=pltpu.CompilerParams(vmem_limit_bytes=VMEM_LIMIT),
     )(*results)
     made = dict(zip(shapes, made, strict=True))

time: 173 us -> 164 us (0.948)
  Pallas kernels: 172 us -> 163 us
    pallas_call x1, Pallas kernels: 165 us -> 157 us  [on_device(): pl.pallas_call(functools.partial(block_kernel, geo, sizes, names), out_sh...]
where the time goes in v3:
time: 164 us
  Pallas kernels  163 us (99%)
    pallas_call x1, Pallas kernels, on_device(): pl.pallas_call(functools.partial(block_kernel, geo, sizes, names), out_sh...  157 us
    pallas_call x1, Pallas kernels, on_device(): pl.pallas_call(functools.partial(finish_kernel, [*given, *shapes, *room,...  5.54 us

profile of v3, /device:TPU:0, one launch (start us, length us, event | category | flops | bytes accessed | tf_op | source)
XLA Modules:
  0.0 163.6 jit_solution(4804393662396427381)
XLA Ops:
  0.7 157.2 %shard_map.297 = (bf16[576,512]{1,0:T(8,128)(2,1)}, f32[576,512]{1,0:T(8,128)}, bf16[512,2048]{1,0:T(8,128)(2,1)}, f32[24,512]{1,0:T(8,128)}, bf16[2,2,1,512,512...) custom-call(s32[2,2,288]{2,1,0:T(2,128)} %bitcast.10, bf16[576,512]{1,0:T(8,128)(2,1)} %bitcast.7, bf16[576,512]{1,0:T(8,128)(2,1)} %bitcast.8, ...), custom_call_target="tpu_custom_call" | custom-call | tf_op jit(solution)/shard_map/pallas_call | solution.py:1547
  157.9 5.5 %shard_map.298 = (bf16[576,512]{1,0:T(8,128)(2,1)}, f32[576,512]{1,0:T(8,128)}, f32[512]{0:T(512)}, f32[512]{0:T(512)}, f32[512,1536]{1,0:T(8,128)}, /*index=5*/...) custom-call(bf16[576,512]{1,0:T(8,128)(2,1)} %get-tuple-element.38.r, ...), custom_call_target="tpu_custom_call" | custom-call | tf_op jit(solution)/shard_map/pallas_call | solution.py:1591

commit v4 on v3

--- a/solution.py
+++ b/solution.py
@@ -1050,8 +1050,6 @@
     x_swap.wait_sent()
 
     root = 0.7978845608028654
-    r.sum_pre[...] = jnp.zeros(r.sum_pre.shape, F32)
-    r.sum_ret[...] = jnp.zeros(r.sum_ret.shape, F32)
 
     def send_late(first, last):
         for i in range(first, last):
@@ -1074,8 +1072,6 @@
             gate = lane_row(group[gate_line : gate_line + 1] + group[gate_line + 1 : gate_line + 2], block)
             there = span(plane * quad + j, block)
             r.grad_ret[there, :] = (gate * r.cot_got[there, :].astype(F32)).astype(BF)
-        total_ret = jnp.sum(r.grad_ret[here, :].astype(F32), axis=0, keepdims=True)
-        r.sum_ret[0:1, :] = r.sum_ret[0:1, :] + total_ret
         for c in range(hidden // tile):
             cols = slice(c * tile, (c + 1) * tile)
             pre = dot(r.x_got[here, :], r.first[:, cols]) + r.bias1[0:1, cols]
@@ -1086,10 +1082,7 @@
             r.hidden[here, cols] = hidden_rows.astype(BF)
             slope = half + hidden_rows * (1.0 - bend) * (root + 3 * 0.044715 * root * square)
             back = dot_nt(r.grad_ret[here, :], r.second[cols, :])
-            grad_pre = (back * slope).astype(BF)
-            r.grad_pre[here, cols] = grad_pre
-            total = jnp.sum(grad_pre.astype(F32), axis=0, keepdims=True)
-            r.sum_pre[0:1, cols] = r.sum_pre[0:1, cols] + total
+            r.grad_pre[here, cols] = (back * slope).astype(BF)
         returned = dot(r.hidden[here, :], r.second[...]) + r.tiles[0, 1:2, :]
         r.send_b[here, :] = returned.astype(BF)
         grad_in = dot_nt(r.grad_pre[here, :], r.first[...])
@@ -1132,6 +1125,9 @@
     weight_grads(1 - k)
     grads.pair(0).start()
     grads.pair(1).start()
+    ones = jnp.ones((16, slots), BF)
+    r.sum_pre[...] = dot(ones, r.grad_pre[...])[0:8]
+    r.sum_ret[...] = dot(ones, r.grad_ret[...])[0:8]
     r.d_tiles[...] = jnp.zeros(r.d_tiles.shape, F32)
     for s in range(geo.places):
         r.d_tiles[s, 0:1, 0:part] = r.sum_pre[0:1, s * part : (s + 1) * part]

time: 164 us -> 163 us (level)
  no operation moved by 1% of the time
where the time goes in v4:
time: 163 us
  Pallas kernels  162 us (99%)
    pallas_call x1, Pallas kernels, on_device(): pl.pallas_call(functools.partial(block_kernel, geo, sizes, names), out_sh...  157 us
    pallas_call x1, Pallas kernels, on_device(): pl.pallas_call(functools.partial(finish_kernel, [*given, *shapes, *room,...  5.54 us

profile of v4, /device:TPU:0, one launch (start us, length us, event | category | flops | bytes accessed | tf_op | source)
XLA Modules:
  0.0 163.2 jit_solution(13244527479852862087)
XLA Ops:
  0.7 156.8 %shard_map.297 = (bf16[576,512]{1,0:T(8,128)(2,1)}, f32[576,512]{1,0:T(8,128)}, bf16[512,2048]{1,0:T(8,128)(2,1)}, f32[24,512]{1,0:T(8,128)}, bf16[2,2,1,512,512...) custom-call(s32[2,2,288]{2,1,0:T(2,128)} %bitcast.10, bf16[576,512]{1,0:T(8,128)(2,1)} %bitcast.7, bf16[576,512]{1,0:T(8,128)(2,1)} %bitcast.8, ...), custom_call_target="tpu_custom_call" | custom-call | tf_op jit(solution)/shard_map/pallas_call | solution.py:1543
  157.4 5.5 %shard_map.298 = (bf16[576,512]{1,0:T(8,128)(2,1)}, f32[576,512]{1,0:T(8,128)}, f32[512]{0:T(512)}, f32[512]{0:T(512)}, f32[512,1536]{1,0:T(8,128)}, /*index=5*/...) custom-call(bf16[576,512]{1,0:T(8,128)(2,1)} %get-tuple-element.38.r, ...), custom_call_target="tpu_custom_call" | custom-call | tf_op jit(solution)/shard_map/pallas_call | solution.py:1587
